TPU v7x, 32 devices: a whole 2x2x4 slice. The times are simulated.
32 devices in a mesh: orb: 2 (over y), aux: 16 (over z, x, core).
Axes of the slice: x: 2, y: 2, z: 4, core: 2. Of those that a mesh axis runs over, the one named last changes fastest.
Arguments:
- factors: bfloat16 [4, 32768, 512], P('orb', 'aux'), may hold values from -0.5 to 0.5
- occ_energy: float32 [4], replicated, may hold values from -2 to -0.5
- virt_energy: float32 [4, 512], replicated, may hold values from 0.2 to 3
- tile_table: int32 [4, 3], replicated, may hold values from 0 to 3, as said below
Outputs:
- gamma: bfloat16 [4, 32768, 512], P('orb', 'aux')
Inputs may be any that keep to these rules, and one draw needn't show every extreme that they name: Row t names two different blocks and the group tile_table[t, 2] that computes the tile. Each group computes at most 4 tiles, and some group exactly 4. Of the blocks owned by another group, the tiles of one group name at most one.
All inputs are finite; a program needn't handle non-finite values.
Results may differ from a plain program's by a relative error of at most 0.0053.
Values may be sent and summed in bfloat16 or wider, within the bound.
No kernel may reach another device: no remote copies, remote signals or barrier semaphores. Data moves between devices by JAX's collectives and lax.ppermute only.
A program may use at most 192 MiB of HBM per device.

v0:
```python
import jax
import jax.numpy as jnp
from jax import lax
from jax.sharding import PartitionSpec as P

CAP = 4


def shards(factors, occ_energy, virt_energy, tile_table):
    owned = factors.shape[0]
    width = factors.shape[2]
    groups = lax.axis_size("orb")
    mine = lax.axis_index("orb")
    first = tile_table[:, 0]
    second = tile_table[:, 1]
    helper = tile_table[:, 2]
    block_ids = jnp.arange(owned * groups, dtype=jnp.int32)
    group_ids = jnp.arange(groups, dtype=jnp.int32)
    local_ids = jnp.arange(owned, dtype=jnp.int32)
    touched = (
        (first[:, None] == block_ids[None, :]) | (second[:, None] == block_ids[None, :])
    ).astype(jnp.int32)
    helped = (helper[:, None] == group_ids[None, :]).astype(jnp.int32)
    usage = jnp.sum(helped[:, :, None] * touched[:, None, :], axis=0) > 0
    usage = usage.reshape(groups, groups, owned).astype(jnp.int32)
    own_usage = jnp.take(usage, mine, axis=1)
    send_pick = jnp.sum(own_usage * local_ids[None, :], axis=1)
    outgoing = jnp.take(factors, send_pick, axis=0)
    incoming = lax.all_to_all(outgoing, "orb", split_axis=0, concat_axis=0, tiled=True)
    store = jnp.concatenate([factors, incoming], axis=0)

    def position(block):
        owner = block // owned
        return jnp.where(owner == mine, block % owned, owned + owner)

    is_mine = (helper == mine).astype(jnp.int32)
    rank = jnp.cumsum(is_mine) - 1
    slot_ids = jnp.arange(CAP, dtype=jnp.int32)
    picked = is_mine[None, :] * (rank[None, :] == slot_ids[:, None]).astype(jnp.int32)
    valid = jnp.sum(picked, axis=1)
    tile_p = jnp.sum(picked * first[None, :], axis=1)
    tile_q = jnp.sum(picked * second[None, :], axis=1)
    place_p = position(tile_p)
    place_q = position(tile_q)
    energy_p = jnp.take(virt_energy, tile_p, axis=0)
    energy_q = jnp.take(virt_energy, tile_q, axis=0)
    occ_sum = jnp.take(occ_energy, tile_p) + jnp.take(occ_energy, tile_q)
    denominators = energy_p[:, :, None] + energy_q[:, None, :] - occ_sum[:, None, None]

    def partners(slot):
        block_p = lax.dynamic_index_in_dim(store, place_p[slot], 0, keepdims=False)
        block_q = lax.dynamic_index_in_dim(store, place_q[slot], 0, keepdims=False)
        return (block_p, block_q)

    def tile_products(slot):
        block_p, block_q = partners(slot)
        return lax.dot_general(
            block_p, block_q, (((0,), (0,)), ((), ())), preferred_element_type=jnp.float32
        )

    def spread(slot, amplitudes, gathered):
        block_p, block_q = partners(slot)
        amplitudes = jnp.where(valid[slot] > 0, amplitudes, jnp.zeros_like(amplitudes))
        to_first = lax.dot_general(
            block_q, amplitudes, (((1,), (1,)), ((), ())), preferred_element_type=jnp.float32
        )
        to_second = jnp.dot(block_p, amplitudes, preferred_element_type=jnp.float32)
        gathered = gathered.at[place_p[slot]].add(to_first)
        return gathered.at[place_q[slot]].add(to_second)

    gathered = jnp.zeros(store.shape, jnp.float32)

    def fill(slot, buffer):
        return lax.dynamic_update_index_in_dim(buffer, tile_products(slot), slot, 0)

    buffer = lax.fori_loop(0, CAP, fill, jnp.zeros((CAP, width, width), jnp.float32))
    summed = lax.psum(buffer, "aux")
    all_amps = (summed / denominators).astype(jnp.bfloat16)

    def apply_all(slot, gathered):
        amplitudes = lax.dynamic_index_in_dim(all_amps, slot, 0, keepdims=False)
        return spread(slot, amplitudes, gathered)

    gathered = lax.fori_loop(0, CAP, apply_all, gathered)
    helper_part = gathered[owned:].astype(jnp.bfloat16)
    returned = lax.all_to_all(helper_part, "orb", split_axis=0, concat_axis=0, tiled=True)
    landing = (send_pick[:, None] == local_ids[None, :]).astype(jnp.float32)
    gamma = gathered[:owned] + jnp.einsum(
        "dj,dav->jav", landing, returned.astype(jnp.float32), precision=lax.Precision.HIGHEST
    )
    return gamma.astype(jnp.bfloat16)


def solution(mesh):
    return jax.shard_map(
        shards,
        mesh=mesh,
        in_specs=(P("orb", "aux", None), P(), P(), P()),
        out_specs=P("orb", "aux", None),
        check_vma=False,
    )
```

profile of v0, /device:TPU:0, one launch (start us, length us, event | category | flops | bytes accessed | tf_op | source)
XLA Modules:
  0.0 408.9 jit_solution(11995169695296178050)
XLA Ops:
  6.5 1.0 slice_reduce_fusion
  8.0 4.5 %fusion.39 = (bf16[2,1024,512]{2,1,0:T(8,128)(2,1)}, bf16[2,1024,512]{2,1,0:T(8,128)(2,1)}) fusion(bf16[2,2048,512]{2,1,0:T(8,128)(2,1)} %param.16), kind=kLoop, calls=%fused_computation.95 | loop fusion | bytes 8388608 | tf_op jit(solution)/shard_map/jit(_take)/gather | solution.py:28
  12.5 2.3 gather_fusion
  14.8 3.6 gather_fusion.1
  18.4 3.8 maximum_select_fusion
  22.2 5.7 %all-to-all-start = ((bf16[2,2048,512]{2,1,0:T(8,128)(2,1)}), bf16[2,2048,512]{2,1,0:T(8,128)(2,1)}, u32[]{:S(2)}, u32[]{:S(2)}) async-start(bf16[2,2048,512]{2,1,0:T(8,128)(2,1)} %maximum_select_fusion), calls=%async_computation | async-start | bytes 8388608 | tf_op jit(solution)/shard_map/all_to_all | solution.py:29
  28.5 4.4 %constant_dynamic-update-slice_fusion.1 = bf16[4,2048,512]{2,1,0:T(8,128)(2,1)} fusion(bf16[2,2048,512]{2,1,0:T(8,128)(2,1)} %param.16), kind=kLoop, calls=%fused_computation.47 | loop fusion | bytes 8388608
  32.8 44.0 %all-to-all-done = bf16[2,2048,512]{2,1,0:T(8,128)(2,1)} async-done(((bf16[2,2048,512]{2,1,0:T(8,128)(2,1)}), bf16[2,2048,512]{2,1,0:T(8,128)(2,1)}, u32[]{:S(2)}, u32[]{:S(2)}) %all-to-all-start) | async-done | bytes 4194336 | tf_op jit(solution)/shard_map/all_to_all | solution.py:29
  76.8 4.4 %constant_dynamic-update-slice_fusion = bf16[4,2048,512]{2,1,0:T(8,128)(2,1)} fusion(bf16[4,2048,512]{2,1,0:T(8,128)(2,1)} %constant_dynamic-update-slice_fusion.1, bf16[2,2048,512]{2,1,0:T(8,128)(2,1)} %all-to-all-done), kind=kLoop, calls=%fused_computation.46 | loop fusion | bytes 8388608 | tf_op jit(solution)/shard_map/concatenate | solution.py:30
  81.2 37.8 %while.29 = (s32[]{:T(128)}, f32[4,512,512]{2,1,0:T(8,128)}, s32[4]{0:T(128)S(1)}, bf16[4,2048,512]{2,1,0:T(8,128)(2,1)}, s32[4]{0:T(128)S(1)}, /*index=5*/s32[]{:T(128)}, s32[]{:T(128)}, s32[]{:T(128)}) while((s32[]{:T(128)}, f32[4,512,512]{2,1,0:T(8,128)}, s32[4]{0:T(128)S(1)}, bf16[4,2048,512]{2,1,0:T(8,128)(2,1)}, s32[4]{0:T(128)S(1)}, ...), condition=%wide.region_6.7_spmd, body=%wide.region_5.6_spmd.sunk | while | flops 1073741824 | bytes 5243577 | solution.py:76
  86.2 4.5 %fusion.51 = f32[4,512,512]{2,1,0:T(8,128)} fusion(f32[4,512,512]{2,1,0:T(8,128)} %get-tuple-element.411, s32[]{:T(128)} %get-tuple-element.410, bf16[4,2048,512]{2,1,0:T(8,128)(2,1)} %get-tuple-element.421, s32[]{:T(128)S(6)} %select_n.222, s32[]{:T(128)S(6)} %select_n.223), kind=kOutput, calls=%fused_computation.12.clone.1 | convolution fusion | flops 1073741824 | bytes 5243400 | tf_op jit(solution)/shard_map/while/body/eval_jaxpr/dot_general | solution.py:57
  95.7 4.5 %fusion.51 = f32[4,512,512]{2,1,0:T(8,128)} fusion(f32[4,512,512]{2,1,0:T(8,128)} %get-tuple-element.411, s32[]{:T(128)} %get-tuple-element.410, bf16[4,2048,512]{2,1,0:T(8,128)(2,1)} %get-tuple-element.421, s32[]{:T(128)S(6)} %select_n.222, s32[]{:T(128)S(6)} %select_n.223), kind=kOutput, calls=%fused_computation.12.clone.1 | convolution fusion | flops 1073741824 | bytes 5243400 | tf_op jit(solution)/shard_map/while/body/eval_jaxpr/dot_general | solution.py:57
  105.1 4.5 %fusion.51 = f32[4,512,512]{2,1,0:T(8,128)} fusion(f32[4,512,512]{2,1,0:T(8,128)} %get-tuple-element.411, s32[]{:T(128)} %get-tuple-element.410, bf16[4,2048,512]{2,1,0:T(8,128)(2,1)} %get-tuple-element.421, s32[]{:T(128)S(6)} %select_n.222, s32[]{:T(128)S(6)} %select_n.223), kind=kOutput, calls=%fused_computation.12.clone.1 | convolution fusion | flops 1073741824 | bytes 5243400 | tf_op jit(solution)/shard_map/while/body/eval_jaxpr/dot_general | solution.py:57
  114.5 4.5 %fusion.51 = f32[4,512,512]{2,1,0:T(8,128)} fusion(f32[4,512,512]{2,1,0:T(8,128)} %get-tuple-element.411, s32[]{:T(128)} %get-tuple-element.410, bf16[4,2048,512]{2,1,0:T(8,128)(2,1)} %get-tuple-element.421, s32[]{:T(128)S(6)} %select_n.222, s32[]{:T(128)S(6)} %select_n.223), kind=kOutput, calls=%fused_computation.12.clone.1 | convolution fusion | flops 1073741824 | bytes 5243400 | tf_op jit(solution)/shard_map/while/body/eval_jaxpr/dot_general | solution.py:57
  122.2 109.0 %all-reduce.2.cloned.1.call-done = f32[4,512,512]{2,1,0:T(8,128)} async-done(((f32[4,512,512]{2,1,0:T(8,128)}), f32[4,512,512]{2,1,0:T(8,128)}) %all-reduce.2.cloned.1.call-update) | async-done | bytes 4194320 | tf_op jit(solution)/shard_map/psum | solution.py:77
  231.3 2.9 divide_convert_fusion
  234.2 7.9 %broadcast_in_dim.64 = f32[4,2048,512]{2,1,0:T(8,128)} broadcast(f32[]{:T(128)} %constant.242.clone.1), dimensions={} | broadcast | bytes 16777220 | tf_op jit(solution)/shard_map/broadcast_in_dim | solution.py:71
  242.0 80.6 %while.30 = (s32[]{:T(128)}, f32[4,2048,512]{2,1,0:T(8,128)}, s32[4]{0:T(128)S(1)}, s32[4]{0:T(128)S(1)}, bf16[4,2048,512]{2,1,0:T(8,128)(2,1)}, /*index=5*/s32[...) while((s32[]{:T(128)}, f32[4,2048,512]{2,1,0:T(8,128)}, ...), condition=%wide.region_12.15_spmd, body=%wide.region_9.14_spmd.sunk | while | flops 2152202240 | bytes 22025472 | solution.py:84
  248.9 6.7 %fusion.56 = f32[4,2048,512]{2,1,0:T(8,128)} fusion(f32[4,2048,512]{2,1,0:T(8,128)} %get-tuple-element.439, s32[]{:T(128)} %select_n.228, bf16[4,2048,512]{2,1,0:T(8,128)(2,1)} %get-tuple-element.454, s32[]{:T(128)} %select_n.229, pred[]{:T(512)} %get-tuple-element.400, bf16[4,512,512]{2,1,0:T(8,128)(2,1)S(1)} %get-tuple-element.456, ...), kind=kOutput, calls=%fused_computation.16.clone.1 | convolution fusion | flops 1076101120 | bytes 11012608 | tf_op jit(solution)/shard_map/while/body/eval_jaxpr/dot_general | solution.py:64
  255.6 6.6 %fusion.57 = f32[4,2048,512]{2,1,0:T(8,128)} fusion(f32[4,2048,512]{2,1,0:T(8,128)} %fusion.56, s32[]{:T(128)} %select_n.229, bf16[4,2048,512]{2,1,0:T(8,128)(2,1)} %get-tuple-element.454, s32[]{:T(128)} %select_n.228, pred[]{:T(512)} %get-tuple-element.401, bf16[4,512,512]{2,1,0:T(8,128)(2,1)S(1)} %get-tuple-element.456, s32[]{:T(128)} %get-tuple-element.438, ...), kind=kOutput, calls=%fused_computation.17.clone.1 | convolution fusion | flops 1076101120 | bytes 11012608 | tf_op jit(solution)/shard_map/while/body/eval_jaxpr/dot_general | solution.py:67
  269.0 6.7 %fusion.56 = f32[4,2048,512]{2,1,0:T(8,128)} fusion(f32[4,2048,512]{2,1,0:T(8,128)} %get-tuple-element.439, s32[]{:T(128)} %select_n.228, bf16[4,2048,512]{2,1,0:T(8,128)(2,1)} %get-tuple-element.454, s32[]{:T(128)} %select_n.229, pred[]{:T(512)} %get-tuple-element.400, bf16[4,512,512]{2,1,0:T(8,128)(2,1)S(1)} %get-tuple-element.456, ...), kind=kOutput, calls=%fused_computation.16.clone.1 | convolution fusion | flops 1076101120 | bytes 11012608 | tf_op jit(solution)/shard_map/while/body/eval_jaxpr/dot_general | solution.py:64
  275.7 6.6 %fusion.57 = f32[4,2048,512]{2,1,0:T(8,128)} fusion(f32[4,2048,512]{2,1,0:T(8,128)} %fusion.56, s32[]{:T(128)} %select_n.229, bf16[4,2048,512]{2,1,0:T(8,128)(2,1)} %get-tuple-element.454, s32[]{:T(128)} %select_n.228, pred[]{:T(512)} %get-tuple-element.401, bf16[4,512,512]{2,1,0:T(8,128)(2,1)S(1)} %get-tuple-element.456, s32[]{:T(128)} %get-tuple-element.438, ...), kind=kOutput, calls=%fused_computation.17.clone.1 | convolution fusion | flops 1076101120 | bytes 11012608 | tf_op jit(solution)/shard_map/while/body/eval_jaxpr/dot_general | solution.py:67
  289.2 6.7 %fusion.56 = f32[4,2048,512]{2,1,0:T(8,128)} fusion(f32[4,2048,512]{2,1,0:T(8,128)} %get-tuple-element.439, s32[]{:T(128)} %select_n.228, bf16[4,2048,512]{2,1,0:T(8,128)(2,1)} %get-tuple-element.454, s32[]{:T(128)} %select_n.229, pred[]{:T(512)} %get-tuple-element.400, bf16[4,512,512]{2,1,0:T(8,128)(2,1)S(1)} %get-tuple-element.456, ...), kind=kOutput, calls=%fused_computation.16.clone.1 | convolution fusion | flops 1076101120 | bytes 11012608 | tf_op jit(solution)/shard_map/while/body/eval_jaxpr/dot_general | solution.py:64
  295.9 6.6 %fusion.57 = f32[4,2048,512]{2,1,0:T(8,128)} fusion(f32[4,2048,512]{2,1,0:T(8,128)} %fusion.56, s32[]{:T(128)} %select_n.229, bf16[4,2048,512]{2,1,0:T(8,128)(2,1)} %get-tuple-element.454, s32[]{:T(128)} %select_n.228, pred[]{:T(512)} %get-tuple-element.401, bf16[4,512,512]{2,1,0:T(8,128)(2,1)S(1)} %get-tuple-element.456, s32[]{:T(128)} %get-tuple-element.438, ...), kind=kOutput, calls=%fused_computation.17.clone.1 | convolution fusion | flops 1076101120 | bytes 11012608 | tf_op jit(solution)/shard_map/while/body/eval_jaxpr/dot_general | solution.py:67
  309.4 6.7 %fusion.56 = f32[4,2048,512]{2,1,0:T(8,128)} fusion(f32[4,2048,512]{2,1,0:T(8,128)} %get-tuple-element.439, s32[]{:T(128)} %select_n.228, bf16[4,2048,512]{2,1,0:T(8,128)(2,1)} %get-tuple-element.454, s32[]{:T(128)} %select_n.229, pred[]{:T(512)} %get-tuple-element.400, bf16[4,512,512]{2,1,0:T(8,128)(2,1)S(1)} %get-tuple-element.456, ...), kind=kOutput, calls=%fused_computation.16.clone.1 | convolution fusion | flops 1076101120 | bytes 11012608 | tf_op jit(solution)/shard_map/while/body/eval_jaxpr/dot_general | solution.py:64
  316.0 6.6 %fusion.57 = f32[4,2048,512]{2,1,0:T(8,128)} fusion(f32[4,2048,512]{2,1,0:T(8,128)} %fusion.56, s32[]{:T(128)} %select_n.229, bf16[4,2048,512]{2,1,0:T(8,128)(2,1)} %get-tuple-element.454, s32[]{:T(128)} %select_n.228, pred[]{:T(512)} %get-tuple-element.401, bf16[4,512,512]{2,1,0:T(8,128)(2,1)S(1)} %get-tuple-element.456, s32[]{:T(128)} %get-tuple-element.438, ...), kind=kOutput, calls=%fused_computation.17.clone.1 | convolution fusion | flops 1076101120 | bytes 11012608 | tf_op jit(solution)/shard_map/while/body/eval_jaxpr/dot_general | solution.py:67
  322.6 5.9 %slice.122 = bf16[2,2048,512]{2,1,0:T(8,128)(2,1)} slice(f32[4,2048,512]{2,1,0:T(8,128)} %get-tuple-element.270), slice={[2:4], [0:2048], [0:512]} | slice | bytes 8388608 | tf_op jit(solution)/shard_map/slice | solution.py:85
  328.5 5.8 %all-to-all-start.1 = ((bf16[2,2048,512]{2,1,0:T(8,128)(2,1)}), bf16[2,2048,512]{2,1,0:T(8,128)(2,1)}, u32[]{:S(2)}, u32[]{:S(2)}) async-start(bf16[2,2048,512]{2,1,0:T(8,128)(2,1)} %slice.122), calls=%async_computation.1 | async-start | bytes 8388608 | tf_op jit(solution)/shard_map/all_to_all | solution.py:86
  334.3 20.9 %copy.14 = f32[4,2048,512]{2,0,1:T(4,128)} copy(f32[4,2048,512]{2,1,0:T(8,128)} %get-tuple-element.270) | data formatting | bytes 33554432 | tf_op jit(solution)/shard_map/while | solution.py:84
  355.2 25.6 %all-to-all-done.1 = bf16[2,2048,512]{2,1,0:T(8,128)(2,1)} async-done(((bf16[2,2048,512]{2,1,0:T(8,128)(2,1)}), bf16[2,2048,512]{2,1,0:T(8,128)(2,1)}, u32[]{:S(2)}, u32[]{:S(2)}) %all-to-all-start.1) | async-done | bytes 4194336 | tf_op jit(solution)/shard_map/all_to_all | solution.py:86
  380.8 18.6 %fusion.30 = bf16[2,2048,512]{2,0,1:T(2,128)(2,1)S(1)} fusion(f32[4,2048,512]{2,0,1:T(4,128)} %copy.14, bf16[2,2048,512]{2,1,0:T(8,128)(2,1)} %all-to-all-done.1, s32[2]{0:T(128)S(1)} %multiply_reduce_fusion.1), kind=kOutput, calls=%fused_computation.39 | convolution fusion | flops 12582916 | bytes 16777224 | tf_op jit(solution)/shard_map/dj,dav->jav/dot_general | solution.py:88
  399.4 2.7 copy.16
  (63 shorter events, 18.6 us)
Async XLA Ops:
  6.5 114.4 %copy-start = (f32[4,512]{1,0:T(4,128)S(1)}, f32[4,512]{1,0:T(4,128)}, u32[]{:S(2)}) copy-start(f32[4,512]{1,0:T(4,128)} %param.18) | copy-start | bytes 24580
  22.2 5.8 %copy-start.3 = (s32[4,3]{1,0:T(4,128)S(1)}, s32[4,3]{1,0:T(4,128)}, u32[]{:S(2)}) copy-start(s32[4,3]{1,0:T(4,128)} %param.19) | copy-start | bytes 148
  22.2 54.6 %all-to-all-start = ((bf16[2,2048,512]{2,1,0:T(8,128)(2,1)}), bf16[2,2048,512]{2,1,0:T(8,128)(2,1)}, u32[]{:S(2)}, u32[]{:S(2)}) async-start(bf16[2,2048,512]{2,1,0:T(8,128)(2,1)} %maximum_select_fusion), calls=%async_computation | async-start | bytes 8388608 | tf_op jit(solution)/shard_map/all_to_all | solution.py:29
  28.0 203.3 %all-reduce.2.cloned.1.call-start = ((), (), s32[]{:S(2)}) async-start(), calls=%async_computation.2 | async-start | bytes 8388608 | tf_op jit(solution)/shard_map/psum | solution.py:77
  119.0 0.7 copy-start.2
  234.2 7.9 %copy-start.4 = (s32[3]{0:T(128)S(1)}, s32[3]{0:T(128)}, u32[]{:S(2)}) copy-start(s32[3]{0:T(128)} %constant.237.clone.1) | copy-start | bytes 40
  328.5 52.2 %all-to-all-start.1 = ((bf16[2,2048,512]{2,1,0:T(8,128)(2,1)}), bf16[2,2048,512]{2,1,0:T(8,128)(2,1)}, u32[]{:S(2)}, u32[]{:S(2)}) async-start(bf16[2,2048,512]{2,1,0:T(8,128)(2,1)} %slice.122), calls=%async_computation.1 | async-start | bytes 8388608 | tf_op jit(solution)/shard_map/all_to_all | solution.py:86
  380.8 21.3 %copy-start.1 = (f32[4,512]{1,0:T(4,128)S(1)}, f32[4,512]{1,0:T(4,128)}, u32[]{:S(2)}) copy-start(f32[4,512]{1,0:T(4,128)} %param.18) | copy-start | bytes 24580
Sparse Core Ops, SparseCore 0:
  119.1 112.0 all-reduce.1
where the time goes:
time: 410 us; the launch traced here: 409 us
  waiting for transfers between devices  179 us (44%)
  matrix products  89.5 us (22%)
  local copies, waits for them, and re-layouts  72.4 us (18%)
  loops' own time  32.9 us (8%)
  between operations  13.5 us (3%)
  starting transfers between devices  11.6 us (3%)
  other arithmetic  10.5 us (3%)
    psum x1, waiting for transfers between devices, shards(): summed = lax.psum(buffer, 'aux')  109 us
    all_to_all x1, waiting for transfers between devices, shards(): lax.all_to_all(outgoing, 'orb', split_axis=0, concat_axis=0, tiled=True)  44 us
    dot_general x4, matrix products, spread(): lax.dot_general(block_q, amplitudes, (((1,), (1,)), ((), ())), preferred_...  26.6 us
    dot_general x4, matrix products, spread(): to_second = jnp.dot(block_p, amplitudes, preferred_element_type=jnp.float32)  26.4 us
    all_to_all x1, waiting for transfers between devices, shards(): lax.all_to_all(helper_part, 'orb', split_axis=0, concat_axis=0, tiled=True)  25.6 us
    while x1, local copies, waits for them, and re-layouts, shards(): gathered = lax.fori_loop(0, CAP, apply_all, gathered)  20.9 us
    dot_general x1, matrix products, shards(): jnp.einsum('dj,dav->jav', landing, returned.astype(jnp.float32), precisio...  18.6 us
    dot_general x4, matrix products, tile_products(): lax.dot_general(block_p, block_q, (((0,), (0,)), ((), ())), preferred_ele...  17.9 us
  transfers between devices with their start and end apart: 3, of which 3 were waited for; matrix products, arithmetic and copies ran while one was open for 7% of the time, Pallas kernels for 0%

commit v1 on v0

--- a/solution.py
+++ b/solution.py
@@ -4,11 +4,13 @@
 from jax.sharding import PartitionSpec as P
 
 CAP = 4
-
-
-def shards(factors, occ_energy, virt_energy, tile_table):
+WIRE = jnp.bfloat16
+
+
+def general(factors, occ_energy, virt_energy, tile_table):
     owned = factors.shape[0]
     width = factors.shape[2]
+    tiles = tile_table.shape[0]
     groups = lax.axis_size("orb")
     mine = lax.axis_index("orb")
     first = tile_table[:, 0]
@@ -34,7 +36,9 @@
         return jnp.where(owner == mine, block % owned, owned + owner)
 
     is_mine = (helper == mine).astype(jnp.int32)
-    rank = jnp.cumsum(is_mine) - 1
+    tile_ids = jnp.arange(tiles, dtype=jnp.int32)
+    earlier = (tile_ids[None, :] < tile_ids[:, None]).astype(jnp.int32)
+    rank = jnp.sum(earlier * is_mine[None, :], axis=1)
     slot_ids = jnp.arange(CAP, dtype=jnp.int32)
     picked = is_mine[None, :] * (rank[None, :] == slot_ids[:, None]).astype(jnp.int32)
     valid = jnp.sum(picked, axis=1)
@@ -52,36 +56,22 @@
         block_q = lax.dynamic_index_in_dim(store, place_q[slot], 0, keepdims=False)
         return (block_p, block_q)
 
-    def tile_products(slot):
+    def fill(slot, buffer):
         block_p, block_q = partners(slot)
-        return lax.dot_general(
-            block_p, block_q, (((0,), (0,)), ((), ())), preferred_element_type=jnp.float32
-        )
-
-    def spread(slot, amplitudes, gathered):
-        block_p, block_q = partners(slot)
-        amplitudes = jnp.where(valid[slot] > 0, amplitudes, jnp.zeros_like(amplitudes))
-        to_first = lax.dot_general(
-            block_q, amplitudes, (((1,), (1,)), ((), ())), preferred_element_type=jnp.float32
-        )
-        to_second = jnp.dot(block_p, amplitudes, preferred_element_type=jnp.float32)
-        gathered = gathered.at[place_p[slot]].add(to_first)
-        return gathered.at[place_q[slot]].add(to_second)
-
-    gathered = jnp.zeros(store.shape, jnp.float32)
-
-    def fill(slot, buffer):
-        return lax.dynamic_update_index_in_dim(buffer, tile_products(slot), slot, 0)
+        return lax.dynamic_update_index_in_dim(buffer, outer(block_p, block_q), slot, 0)
 
     buffer = lax.fori_loop(0, CAP, fill, jnp.zeros((CAP, width, width), jnp.float32))
     summed = lax.psum(buffer, "aux")
     all_amps = (summed / denominators).astype(jnp.bfloat16)
 
     def apply_all(slot, gathered):
+        block_p, block_q = partners(slot)
         amplitudes = lax.dynamic_index_in_dim(all_amps, slot, 0, keepdims=False)
-        return spread(slot, amplitudes, gathered)
-
-    gathered = lax.fori_loop(0, CAP, apply_all, gathered)
+        amplitudes = jnp.where(valid[slot] > 0, amplitudes, jnp.zeros_like(amplitudes))
+        gathered = gathered.at[place_p[slot]].add(right_t(block_q, amplitudes))
+        return gathered.at[place_q[slot]].add(right(block_p, amplitudes))
+
+    gathered = lax.fori_loop(0, CAP, apply_all, jnp.zeros(store.shape, jnp.float32))
     helper_part = gathered[owned:].astype(jnp.bfloat16)
     returned = lax.all_to_all(helper_part, "orb", split_axis=0, concat_axis=0, tiled=True)
     landing = (send_pick[:, None] == local_ids[None, :]).astype(jnp.float32)
@@ -89,6 +79,136 @@
         "dj,dav->jav", landing, returned.astype(jnp.float32), precision=lax.Precision.HIGHEST
     )
     return gamma.astype(jnp.bfloat16)
+
+
+def outer(a, b):
+    return lax.dot_general(a, b, (((0,), (0,)), ((), ())), preferred_element_type=jnp.float32)
+
+
+def right(a, m):
+    return jnp.dot(a, m, preferred_element_type=jnp.float32)
+
+
+def right_t(a, m):
+    return lax.dot_general(a, m, (((1,), (1,)), ((), ())), preferred_element_type=jnp.float32)
+
+
+def swap(value, axis, bit):
+    size = lax.axis_size(axis)
+    return lax.ppermute(value, axis, [(i, i ^ (1 << bit)) for i in range(size)])
+
+
+def halve(part, axis, wires):
+    me = lax.axis_index(axis)
+    for bit, wire in enumerate(wires):
+        high = ((me >> bit) & 1) == 1
+        half = part.shape[0] // 2
+        low_rows, high_rows = part[:half], part[half:]
+        sent = jnp.where(high, low_rows, high_rows).astype(wire)
+        kept = jnp.where(high, high_rows, low_rows)
+        part = kept + swap(sent, axis, bit).astype(jnp.float32)
+    return part
+
+
+def double(part, axis, bits):
+    me = lax.axis_index(axis)
+    for bit in reversed(range(bits)):
+        high = ((me >> bit) & 1) == 1
+        other = swap(part, axis, bit)
+        part = jnp.concatenate(
+            [jnp.where(high, other, part), jnp.where(high, part, other)], axis=0
+        )
+    return part
+
+
+def two_groups(factors, occ_energy, virt_energy, tile_table):
+    owned, rows, width = factors.shape
+    aux = lax.axis_size("aux")
+    bits = aux.bit_length() - 1
+    mine = lax.axis_index("orb")
+    me = lax.axis_index("aux")
+    first, second, helper = tile_table[:, 0], tile_table[:, 1], tile_table[0, 2]
+    helps = mine == helper
+    low = helper * owned
+    foreign_low = (1 - helper) * owned
+    foreign = foreign_low
+    for block in range(1, owned):
+        named = jnp.any((first == foreign_low + block) | (second == foreign_low + block))
+        foreign = jnp.where(named, foreign_low + block, foreign)
+    foreign_local = foreign - foreign_low
+
+    def count(a, b):
+        same = ((first == a) & (second == b)) | ((first == b) & (second == a))
+        return jnp.sum(same.astype(jnp.float32))
+
+    shard = width // aux
+    offset = jnp.int32(0)
+    for bit in range(bits):
+        offset = offset + ((me >> bit) & 1) * (width >> (bit + 1))
+
+    def amplitudes(summed, a, b):
+        virt_a = lax.dynamic_slice(virt_energy, (a, offset), (1, shard))[0]
+        virt_b = lax.dynamic_slice(virt_energy, (b, 0), (1, width))[0]
+        occ_a = lax.dynamic_index_in_dim(occ_energy, a, 0, keepdims=False)
+        occ_b = lax.dynamic_index_in_dim(occ_energy, b, 0, keepdims=False)
+        denominators = virt_a[:, None] + virt_b[None, :] - occ_a - occ_b
+        return (count(a, b) * summed / denominators).astype(jnp.bfloat16)
+
+    wires = [jnp.float32] + [WIRE] * (bits - 1)
+    half, quarter, early = rows // 2, rows // 4, 3 * rows // 16
+    b0 = jnp.where(helps, 0, foreign_local)
+    b1 = jnp.where(helps, 1, foreign_local)
+
+    def cut(block, start_helper, start_owner, size):
+        start = jnp.where(helps, start_helper, start_owner)
+        return lax.dynamic_slice(factors, (block, start, 0), (1, size, width))[0]
+
+    got1 = swap(cut(b0, half, 0, half), "orb", 0)
+    got2 = swap(cut(b1, half + quarter, half, quarter), "orb", 0)
+    own2 = cut(b1, half, half + quarter, quarter)
+    got3 = swap(own2, "orb", 0)
+    got4 = swap(cut(b0, early, early, half - early), "orb", 0)
+    got5 = swap(cut(b1, early, early, half - early), "orb", 0)
+
+    part01 = outer(factors[0], factors[1])
+    amp01 = double(amplitudes(halve(part01, "aux", wires), low, low + 1), "aux", bits)
+
+    def both(value):
+        return value + swap(value, "orb", 0)
+
+    own1 = cut(b0, 0, half, half)
+    part0f = outer(jnp.where(helps, own1, got1), jnp.where(helps, got1, own1))
+    amp0f = double(amplitudes(both(halve(part0f, "aux", wires)), low, foreign), "aux", bits)
+
+    part1f = outer(jnp.where(helps, own2, got2), jnp.where(helps, got2, own2))
+    part1f = part1f + jnp.where(helps, outer(factors[1, :half], got1), 0.0)
+    amp1f = double(amplitudes(both(halve(part1f, "aux", wires)), low + 1, foreign), "aux", bits)
+
+    back = right(factors[0, :early], amp0f) + right(factors[1, :early], amp1f)
+    got6 = swap(back.astype(jnp.bfloat16), "orb", 0)
+
+    whole_f = jnp.concatenate([got1, got2, got3], axis=0)
+    gamma0 = (right_t(factors[1], amp01) + right_t(whole_f, amp0f)).astype(jnp.bfloat16)
+    gamma1 = (right(factors[0], amp01) + right_t(whole_f, amp1f)).astype(jnp.bfloat16)
+    rows0 = jnp.concatenate([got4, got1], axis=0)
+    rows1 = jnp.concatenate([got5, got3, got2], axis=0)
+    later = (right(rows0, amp0f) + right(rows1, amp1f)).astype(jnp.bfloat16)
+    gamma_f = jnp.concatenate([got6, later], axis=0)
+
+    def block(local, at_helper):
+        at_owner = jnp.where(local == foreign_local, gamma_f, jnp.zeros_like(gamma_f))
+        return jnp.where(helps, at_helper, at_owner)
+
+    return jnp.stack([block(0, gamma0), block(1, gamma1)], axis=0)
+
+
+def shards(factors, occ_energy, virt_energy, tile_table):
+    groups = lax.axis_size("orb")
+    aux = lax.axis_size("aux")
+    simple = groups == 2 and factors.shape[0] == 2 and tile_table.shape[0] <= CAP
+    if simple and aux & (aux - 1) == 0 and factors.shape[1] % 256 == 0:
+        return two_groups(factors, occ_energy, virt_energy, tile_table)
+    return general(factors, occ_energy, virt_energy, tile_table)
 
 
 def solution(mesh):

time: 410 us -> 146 us (0.36)
  waiting for transfers between devices: 179 us -> 54.3 us
  matrix products: 89.5 us -> 22.4 us
  local copies, waits for them, and re-layouts: 72.4 us -> 13.9 us
  loops' own time: 32.9 us -> 0 us
  starting transfers between devices: 11.6 us -> 38.5 us
  between operations: 13.5 us -> 2.8 us
    psum x1 -> x0, waiting for transfers between devices: 109 us -> none  [shards(): summed = lax.psum(buffer, 'aux')]
    all_to_all x2 -> x0, waiting for transfers between devices: 69.5 us -> none  [the longest x1 44 us: shards(): lax.all_to_all(outgoing, 'orb', split_axis=0, concat_axis=0, tiled=True)]
    dot_general x13 -> x12, matrix products: 89.5 us -> 22.4 us  [the longest x4 8.6 us: outer(): lax.dot_general(a, b, (((0,), (0,)), ((), ())), preferred_element_type=jn...]
    ppermute x0 -> x32, waiting for transfers between devices: none -> 54.3 us  [swap(): return lax.ppermute(value, axis, [(i, i ^ 1 << bit) for i in range(size)])]
    ppermute x0 -> x32, starting transfers between devices: none -> 38.5 us  [swap(): return lax.ppermute(value, axis, [(i, i ^ 1 << bit) for i in range(size)])]
    another operation x2 -> x0, loops' own time: 32.9 us -> none  [the longest x1 17.8 us: shards(): gathered = lax.fori_loop(0, CAP, apply_all, gathered)]
    while x1 -> x0, local copies, waits for them, and re-layouts: 20.9 us -> none  [shards(): gathered = lax.fori_loop(0, CAP, apply_all, gathered)]
    gather x7 -> x0, local copies, waits for them, and re-layouts: 12.8 us -> none  [the longest x3 10.4 us: shards(): outgoing = jnp.take(factors, send_pick, axis=0)]
  transfers between devices with their start and end apart: 3 -> 32, of which waited for: 3 -> 15; matrix products, arithmetic and copies ran while one was open for 7% -> 21% of each run, Pallas kernels for 0% -> 0%
where the time goes in v1:
time: 146 us; the launch traced here: 145 us
  waiting for transfers between devices  54.3 us (37%)
  starting transfers between devices  38.5 us (26%)
  matrix products  22.4 us (15%)
  local copies, waits for them, and re-layouts  13.9 us (10%)
  other arithmetic  13 us (9%)
  between operations  2.8 us (2%)
    ppermute x32, waiting for transfers between devices, swap(): return lax.ppermute(value, axis, [(i, i ^ 1 << bit) for i in range(size)])  54.3 us
    ppermute x32, starting transfers between devices, swap(): return lax.ppermute(value, axis, [(i, i ^ 1 << bit) for i in range(size)])  38.5 us
    dot_general x4, matrix products, outer(): lax.dot_general(a, b, (((0,), (0,)), ((), ())), preferred_element_type=jn...  8.6 us
    dot_general x5, matrix products, right(): return jnp.dot(a, m, preferred_element_type=jnp.float32)  7.25 us
    dot_general x3, matrix products, right_t(): lax.dot_general(a, m, (((1,), (1,)), ((), ())), preferred_element_type=jn...  6.52 us
    another operation x1, local copies, waits for them, and re-layouts, two_groups(): return jnp.stack([block(0, gamma0), block(1, gamma1)], axis=0)  6.2 us
    convert_element_type x1, other arithmetic, amplitudes(): return (count(a, b) * summed / denominators).astype(jnp.bfloat16)  4.37 us
  transfers between devices with their start and end apart: 32, of which 15 were waited for; matrix products, arithmetic and copies ran while one was open for 21% of the time, Pallas kernels for 0%

profile of v1, /device:TPU:0, one launch (start us, length us, event | category | flops | bytes accessed | tf_op | source)
XLA Modules:
  0.0 144.8 jit_solution(17223641915180643278)
XLA Ops:
  0.0 3.5 %fusion.8 = f32[512,512]{1,0:T(8,128)S(1)} fusion(bf16[2,2048,512]{2,1,0:T(8,128)(2,1)} %param.4), kind=kOutput, calls=%fused_computation.14 | convolution fusion | flops 1073741824 | bytes 5242880 | tf_op jit(solution)/shard_map/dot_general | solution.py:85
  10.2 2.5 %collective-permute-start.9 = (bf16[512,512]{0,1:T(8,128)(2,1)}, bf16[512,512]{0,1:T(8,128)(2,1)S(1)}, u32[]{:S(2)}, u32[]{:S(2)}) collective-permute-start(bf16[512,512]{0,1:T(8,128)(2,1)} %bitcast.9), channel_id=1, source_target_pairs={{0,16},{16,0},{1,17},{17,1},{2,18},{18,2},{3,19},{19,3},{4,20},{20... | collective-permute-start | bytes 1572872 | tf_op jit(solution)/shard_map/ppermute | solution.py:98
  13.0 2.3 %dynamic-slice_bitcast_fusion = bf16[1024,512]{1,0:T(8,128)(2,1)} fusion(bf16[2,2048,512]{2,1,0:T(8,128)(2,1)} %param.4, s32[]{:T(128)S(6)} %select_n.365, s32[]{:T(128)S(6)} %select_n.366), kind=kLoop, calls=%fused_computation.44 | loop fusion | bytes 2097160 | tf_op jit(solution)/shard_map/squeeze | solution.py:164
  15.3 2.0 %collective-permute-start.8 = (bf16[1024,512]{1,0:T(8,128)(2,1)}, bf16[1024,512]{1,0:T(8,128)(2,1)}, u32[]{:S(2)}, u32[]{:S(2)}) collective-permute-start(bf16[1024,512]{1,0:T(8,128)(2,1)} %dynamic-slice_bitcast_fusion), channel_id=1, source_target_pairs={{0,16},{16,0},{1,17},{17,1},{2,18},{18,2},{3,19},{19,3},{4,20},{20... | collective-permute-start | bytes 3145736 | tf_op jit(solution)/shard_map/ppermute | solution.py:98
  18.0 1.6 %collective-permute-start.1 = (bf16[128,512]{1,0:T(8,128)(2,1)S(1)}, bf16[128,512]{1,0:T(8,128)(2,1)S(1)}, u32[]{:S(2)}, u32[]{:S(2)}) collective-permute-start(bf16[128,512]{1,0:T(8,128)(2,1)S(1)} %select_convert_fusion.2), channel_id=1, source_target_pairs={{0,2},{1,3},{2,0},{3,1},{4,6},{5,7},{6,4},{7,5},{8,10},{9,11},{10,... | collective-permute-start | bytes 393224 | tf_op jit(solution)/shard_map/ppermute | solution.py:98
  20.3 2.9 %collective-permute-done.1 = bf16[128,512]{1,0:T(8,128)(2,1)S(1)} collective-permute-done((bf16[128,512]{1,0:T(8,128)(2,1)S(1)}, bf16[128,512]{1,0:T(8,128)(2,1)S(1)}, u32[]{:S(2)}, u32[]{:S(2)}) %collective-permute-start.1) | collective-permute-done | bytes 131104 | tf_op jit(solution)/shard_map/ppermute | solution.py:98
  23.2 1.6 %collective-permute-start.2 = (bf16[64,512]{1,0:T(8,128)(2,1)S(1)}, bf16[64,512]{1,0:T(8,128)(2,1)S(1)}, u32[]{:S(2)}, u32[]{:S(2)}) collective-permute-start(bf16[64,512]{1,0:T(8,128)(2,1)S(1)} %select_convert_fusion.5), channel_id=1, source_target_pairs={{0,4},{1,5},{2,6},{3,7},{4,0},{5,1},{6,2},{7,3},{8,12},{9,13},{10,... | collective-permute-start | bytes 196616 | tf_op jit(solution)/shard_map/ppermute | solution.py:98
  24.9 2.7 %collective-permute-done.2 = bf16[64,512]{1,0:T(8,128)(2,1)S(1)} collective-permute-done((bf16[64,512]{1,0:T(8,128)(2,1)S(1)}, bf16[64,512]{1,0:T(8,128)(2,1)S(1)}, u32[]{:S(2)}, u32[]{:S(2)}) %collective-permute-start.2) | collective-permute-done | bytes 65568 | tf_op jit(solution)/shard_map/ppermute | solution.py:98
  27.6 31.7 %collective-permute-done.8 = bf16[1024,512]{1,0:T(8,128)(2,1)} collective-permute-done((bf16[1024,512]{1,0:T(8,128)(2,1)}, bf16[1024,512]{1,0:T(8,128)(2,1)}, u32[]{:S(2)}, u32[]{:S(2)}) %collective-permute-start.8) | collective-permute-done | bytes 1048608 | tf_op jit(solution)/shard_map/ppermute | solution.py:98
  59.3 2.6 %fusion.30 = f32[512,512]{1,0:T(8,128)S(1)} fusion(bf16[1024,512]{1,0:T(8,128)(2,1)} %collective-permute-done.8, bf16[2,2048,512]{2,1,0:T(8,128)(2,1)} %param.4, s32[]{:T(128)S(6)} %select_n.365, s32[]{:T(128)S(6)} %select_n.372, pred[]{:T(512)S(6)} %eq.46), kind=kOutput, calls=%fused_computation.41 | convolution fusion | flops 537919488 | bytes 5245952 | tf_op jit(solution)/shard_map/dot_general | solution.py:85
  62.1 2.0 %fusion.26 = f32[512,512]{1,0:T(8,128)S(1)} fusion(bf16[1024,512]{1,0:T(8,128)(2,1)} %collective-permute-done.8, bf16[2,2048,512]{2,1,0:T(8,128)(2,1)S(1)} %copy-done, pred[]{:T(512)S(6)} %eq.46), kind=kOutput, calls=%fused_computation.34 | convolution fusion | flops 537133056 | bytes 3145729 | tf_op jit(solution)/shard_map/dot_general | solution.py:85
  65.3 2.9 %collective-permute-start.3 = (bf16[32,512]{1,0:T(8,128)(2,1)S(1)}, bf16[32,512]{1,0:T(8,128)(2,1)S(1)}, u32[]{:S(2)}, u32[]{:S(2)}) collective-permute-start(bf16[32,512]{1,0:T(8,128)(2,1)S(1)} %select_convert_fusion.8), channel_id=1, source_target_pairs={{0,8},{1,9},{2,10},{3,11},{4,12},{5,13},{6,14},{7,15},{8,0},{9,1},... | collective-permute-start | bytes 98312 | tf_op jit(solution)/shard_map/ppermute | solution.py:98
  68.4 1.6 %collective-permute-start.12 = (bf16[128,512]{1,0:T(8,128)(2,1)S(1)}, bf16[128,512]{1,0:T(8,128)(2,1)S(1)}, u32[]{:S(2)}, u32[]{:S(2)}) collective-permute-start(bf16[128,512]{1,0:T(8,128)(2,1)S(1)} %select_convert_fusion.1), channel_id=1, source_target_pairs={{0,2},{1,3},{2,0},{3,1},{4,6},{5,7},{6,4},{7,5},{8,10},{9,11},{10,... | collective-permute-start | bytes 393224 | tf_op jit(solution)/shard_map/ppermute | solution.py:98
  70.7 4.1 %collective-permute-done.12 = bf16[128,512]{1,0:T(8,128)(2,1)S(1)} collective-permute-done((bf16[128,512]{1,0:T(8,128)(2,1)S(1)}, bf16[128,512]{1,0:T(8,128)(2,1)S(1)}, u32[]{:S(2)}, u32[]{:S(2)}) %collective-permute-start.12) | collective-permute-done | bytes 131104 | tf_op jit(solution)/shard_map/ppermute | solution.py:98
  74.9 1.6 %collective-permute-start.13 = (bf16[64,512]{1,0:T(8,128)(2,1)S(1)}, bf16[64,512]{1,0:T(8,128)(2,1)S(1)}, u32[]{:S(2)}, u32[]{:S(2)}) collective-permute-start(bf16[64,512]{1,0:T(8,128)(2,1)S(1)} %select_convert_fusion.4), channel_id=1, source_target_pairs={{0,4},{1,5},{2,6},{3,7},{4,0},{5,1},{6,2},{7,3},{8,12},{9,13},{10,... | collective-permute-start | bytes 196616 | tf_op jit(solution)/shard_map/ppermute | solution.py:98
  82.6 1.8 %collective-permute-done.14 = bf16[32,512]{1,0:T(8,128)(2,1)S(1)} collective-permute-done((bf16[32,512]{1,0:T(8,128)(2,1)S(1)}, bf16[32,512]{1,0:T(8,128)(2,1)S(1)}, u32[]{:S(2)}, u32[]{:S(2)}) %collective-permute-start.14) | collective-permute-done | bytes 32800 | tf_op jit(solution)/shard_map/ppermute | solution.py:98
  84.4 1.6 %collective-permute-start.15 = (f32[32,512]{1,0:T(8,128)S(1)}, f32[32,512]{1,0:T(8,128)S(1)}, u32[]{:S(2)}, u32[]{:S(2)}) collective-permute-start(f32[32,512]{1,0:T(8,128)S(1)} %convert_add_fusion.7), channel_id=1, source_target_pairs={{0,16},{16,0},{1,17},{17,1},{2,18},{18,2},{3,19},{19,3},{4,20},{20... | collective-permute-start | bytes 196616 | tf_op jit(solution)/shard_map/ppermute | solution.py:98
  86.3 1.6 %collective-permute-start.24 = (f32[32,512]{1,0:T(8,128)S(1)}, f32[32,512]{1,0:T(8,128)S(1)}, u32[]{:S(2)}, u32[]{:S(2)}) collective-permute-start(f32[32,512]{1,0:T(8,128)S(1)} %convert_add_fusion.6), channel_id=1, source_target_pairs={{0,16},{16,0},{1,17},{17,1},{2,18},{18,2},{3,19},{19,3},{4,20},{20... | collective-permute-start | bytes 196616 | tf_op jit(solution)/shard_map/ppermute | solution.py:98
  88.7 1.8 %collective-permute-done.24 = f32[32,512]{1,0:T(8,128)S(1)} collective-permute-done((f32[32,512]{1,0:T(8,128)S(1)}, f32[32,512]{1,0:T(8,128)S(1)}, u32[]{:S(2)}, u32[]{:S(2)}) %collective-permute-start.24) | collective-permute-done | bytes 65568 | tf_op jit(solution)/shard_map/ppermute | solution.py:98
  90.6 4.4 %divide_convert_fusion.1 = (bf16[32,512]{1,0:T(8,128)(2,1)}, bf16[32,512]{1,0:T(8,128)(2,1)}, bf16[32,512]{1,0:T(8,128)(2,1)}) fusion(f32[32,512]{1,0:T(8,128)S(1)} %convert_add_fusion.7, f32[32,512]{1,0:T(8,128)S(1)} %collective-permute-done.15, f32[]{:T(128)} %bitcast.13, f32[512]{0:T(512)S(1)} %bitcast.74, f32[]{:T(128)} %get-tuple-element.5, ...), kind=kLoop, calls=%fused_computation.103 | loop fusion | flops 376832 | bytes 528665 | tf_op jit(solution)/shard_map/convert_element_type | solution.py:155
  96.2 1.6 %collective-permute-start.30 = (bf16[640,512]{1,0:T(8,128)(2,1)S(1)}, bf16[640,512]{1,0:T(8,128)(2,1)S(1)}, u32[]{:S(2)}, u32[]{:S(2)}) collective-permute-start(bf16[640,512]{1,0:T(8,128)(2,1)S(1)} %get-tuple-element.8), channel_id=1, source_target_pairs={{0,16},{16,0},{1,17},{17,1},{2,18},{18,2},{3,19},{19,3},{4,20},{20... | collective-permute-start | bytes 1966088 | tf_op jit(solution)/shard_map/ppermute | solution.py:98
  99.8 1.9 %collective-permute-start.25 = (bf16[32,512]{1,0:T(8,128)(2,1)}, bf16[32,512]{1,0:T(8,128)(2,1)S(1)}, u32[]{:S(2)}, u32[]{:S(2)}) collective-permute-start(bf16[32,512]{1,0:T(8,128)(2,1)} %get-tuple-element.41), channel_id=1, source_target_pairs={{0,8},{1,9},{2,10},{3,11},{4,12},{5,13},{6,14},{7,15},{8,0},{9,1},... | collective-permute-start | bytes 98312 | tf_op jit(solution)/shard_map/ppermute | solution.py:98
  103.5 2.0 %collective-permute-start.17 = (bf16[64,512]{1,0:T(8,128)(2,1)S(1)}, bf16[64,512]{1,0:T(8,128)(2,1)S(1)}, u32[]{:S(2)}, u32[]{:S(2)}) collective-permute-start(bf16[64,512]{1,0:T(8,128)(2,1)S(1)} %pad_maximum_fusion.27), channel_id=1, source_target_pairs={{0,4},{1,5},{2,6},{3,7},{4,0},{5,1},{6,2},{7,3},{8,12},{9,13},{10,... | collective-permute-start | bytes 196616 | tf_op jit(solution)/shard_map/ppermute | solution.py:98
  106.3 1.6 %collective-permute-start.26 = (bf16[64,512]{1,0:T(8,128)(2,1)S(1)}, bf16[64,512]{1,0:T(8,128)(2,1)S(1)}, u32[]{:S(2)}, u32[]{:S(2)}) collective-permute-start(bf16[64,512]{1,0:T(8,128)(2,1)S(1)} %pad_maximum_fusion.28), channel_id=1, source_target_pairs={{0,4},{1,5},{2,6},{3,7},{4,0},{5,1},{6,2},{7,3},{8,12},{9,13},{10,... | collective-permute-start | bytes 196616 | tf_op jit(solution)/shard_map/ppermute | solution.py:98
  114.4 1.6 %collective-permute-done.27 = bf16[128,512]{1,0:T(8,128)(2,1)S(1)} collective-permute-done((bf16[128,512]{1,0:T(8,128)(2,1)S(1)}, bf16[128,512]{1,0:T(8,128)(2,1)S(1)}, u32[]{:S(2)}, u32[]{:S(2)}) %collective-permute-start.27) | collective-permute-done | bytes 131104 | tf_op jit(solution)/shard_map/ppermute | solution.py:98
  120.8 1.6 %collective-permute-done.31 = bf16[640,512]{1,0:T(8,128)(2,1)} collective-permute-done((bf16[640,512]{1,0:T(8,128)(2,1)S(1)}, bf16[640,512]{1,0:T(8,128)(2,1)}, u32[]{:S(2)}, u32[]{:S(2)}) %collective-permute-start.31) | collective-permute-done | bytes 655392 | tf_op jit(solution)/shard_map/ppermute | solution.py:98
  122.3 2.3 %fusion.20 = f32[1664,512]{0,1:T(8,128)S(1)} fusion(bf16[512,512]{1,0:T(8,128)(2,1)S(1)} %copy.7, bf16[512,512]{1,0:T(8,128)(2,1)S(1)} %copy.8, bf16[640,512]{1,0:T(8,128)(2,1)} %collective-permute-done.31, bf16[256,512]{1,0:T(8,128)(2,1)S(1)} %get-tuple-element.15, bf16[256,512]{1,0:T(8,128)(2,1)S(1)} %get-tuple-element.14), kind=kOutput, calls=%fused_computation.26 | convolution fusion | flops 878575616 | bytes 5636096 | tf_op jit(solution)/shard_map/dot_general | solution.py:89
  126.1 2.7 %add_convert_fusion = bf16[1664,512]{0,1:T(8,128)(2,1)S(1)} fusion(f32[1664,512]{0,1:T(8,128)S(1)} %fusion.20, bf16[1024,512]{1,0:T(8,128)(2,1)} %collective-permute-done.8, bf16[640,512]{1,0:T(8,128)(2,1)S(1)} %collective-permute-done.30, bf16[256,512]{1,0:T(8,128)(2,1)S(1)} %get-tuple-element.13, bf16[256,512]{1,0:T(8,128)(2,1)S(1)} %get-tuple-element.12), kind=kOutput, calls=%fused_computation.5 | convolution fusion | flops 878575616 | bytes 7340032 | tf_op jit(solution)/shard_map/dot_general | solution.py:89
  131.0 2.6 %fusion.5 = bf16[1,2048,512]{1,2,0:T(8,128)(2,1)S(1)} fusion(f32[512,2048]{1,0:T(8,128)S(1)} %fusion.10, pred[]{:T(512)S(6)} %eq.119, pred[]{:T(512)S(6)} %eq.46, bf16[1664,512]{0,1:T(8,128)(2,1)S(1)} %add_convert_fusion, bf16[384,512]{0,1:T(8,128)(2,1)S(1)} %collective-permute-done.29, bf16[512,512]{1,0:T(8,128)(2,1)S(1)} %copy.8, ...), kind=kOutput, calls=%fused_computation.9 | convolution fusion | flops 1089470464 | bytes 11010050 | tf_op jit(solution)/shard_map/dot_general | solution.py:93
  133.7 2.6 %fusion.3 = bf16[1,2048,512]{1,2,0:T(8,128)(2,1)S(1)} fusion(f32[512,2048]{1,0:T(8,128)S(1)} %fusion.6, pred[]{:T(512)S(6)} %eq.118, pred[]{:T(512)S(6)} %eq.46, bf16[1664,512]{0,1:T(8,128)(2,1)S(1)} %add_convert_fusion, bf16[384,512]{0,1:T(8,128)(2,1)S(1)} %collective-permute-done.29, bf16[512,512]{1,0:T(8,128)(2,1)S(1)} %copy.8, ...), kind=kOutput, calls=%fused_computation.7 | convolution fusion | flops 1089470464 | bytes 11010050 | tf_op jit(solution)/shard_map/dot_general | solution.py:93
  136.3 2.3 %pad_maximum_fusion = bf16[2,2048,512]{1,2,0:T(8,128)(2,1)} fusion(bf16[1,2048,512]{1,2,0:T(8,128)(2,1)S(1)} %fusion.5, bf16[1,2048,512]{1,2,0:T(8,128)(2,1)S(1)} %fusion.3), kind=kLoop, calls=%fused_computation | loop fusion | flops 2097152 | bytes 8388608 | tf_op jit(solution)/shard_map/stack | solution.py:202
  138.6 6.2 %copy.15 = bf16[2,2048,512]{2,1,0:T(8,128)(2,1)} copy(bf16[2,2048,512]{1,2,0:T(8,128)(2,1)} %pad_maximum_fusion) | data formatting | bytes 8388608 | tf_op jit(solution)/shard_map/stack | solution.py:202
  (114 shorter events, 36.3 us)
Async XLA Ops:
  4.4 13.4 %collective-permute-start = (f32[256,512]{1,0:T(8,128)}, f32[256,512]{1,0:T(8,128)S(1)}, u32[]{:S(2)}, u32[]{:S(2)}) collective-permute-start(f32[256,512]{1,0:T(8,128)} %slice_select_fusion.2), channel_id=1, source_target_pairs={{0,1},{1,0},{2,3},{3,2},{4,5},{5,4},{6,7},{7,6},{8,9},{9,8},{10,11... | collective-permute-start | bytes 1572872 | tf_op jit(solution)/shard_map/ppermute | solution.py:98
  10.2 53.9 %collective-permute-start.9 = (bf16[512,512]{0,1:T(8,128)(2,1)}, bf16[512,512]{0,1:T(8,128)(2,1)S(1)}, u32[]{:S(2)}, u32[]{:S(2)}) collective-permute-start(bf16[512,512]{0,1:T(8,128)(2,1)} %bitcast.9), channel_id=1, source_target_pairs={{0,16},{16,0},{1,17},{17,1},{2,18},{18,2},{3,19},{19,3},{4,20},{20... | collective-permute-start | bytes 1572872 | tf_op jit(solution)/shard_map/ppermute | solution.py:98
  12.9 85.6 %collective-permute-start.10 = (bf16[512,512]{0,1:T(8,128)(2,1)S(1)}, bf16[512,512]{0,1:T(8,128)(2,1)}, u32[]{:S(2)}, u32[]{:S(2)}) collective-permute-start(bf16[512,512]{0,1:T(8,128)(2,1)S(1)} %bitcast.73), channel_id=1, source_target_pairs={{0,16},{16,0},{1,17},{17,1},{2,18},{18,2},{3,19},{19,3},{4,20},{20... | collective-permute-start | bytes 1572872 | tf_op jit(solution)/shard_map/ppermute | solution.py:98
  15.3 44.0 %collective-permute-start.8 = (bf16[1024,512]{1,0:T(8,128)(2,1)}, bf16[1024,512]{1,0:T(8,128)(2,1)}, u32[]{:S(2)}, u32[]{:S(2)}) collective-permute-start(bf16[1024,512]{1,0:T(8,128)(2,1)} %dynamic-slice_bitcast_fusion), channel_id=1, source_target_pairs={{0,16},{16,0},{1,17},{17,1},{2,18},{18,2},{3,19},{19,3},{4,20},{20... | collective-permute-start | bytes 3145736 | tf_op jit(solution)/shard_map/ppermute | solution.py:98
  18.0 5.1 %collective-permute-start.1 = (bf16[128,512]{1,0:T(8,128)(2,1)S(1)}, bf16[128,512]{1,0:T(8,128)(2,1)S(1)}, u32[]{:S(2)}, u32[]{:S(2)}) collective-permute-start(bf16[128,512]{1,0:T(8,128)(2,1)S(1)} %select_convert_fusion.2), channel_id=1, source_target_pairs={{0,2},{1,3},{2,0},{3,1},{4,6},{5,7},{6,4},{7,5},{8,10},{9,11},{10,... | collective-permute-start | bytes 393224 | tf_op jit(solution)/shard_map/ppermute | solution.py:98
  23.2 4.3 %collective-permute-start.2 = (bf16[64,512]{1,0:T(8,128)(2,1)S(1)}, bf16[64,512]{1,0:T(8,128)(2,1)S(1)}, u32[]{:S(2)}, u32[]{:S(2)}) collective-permute-start(bf16[64,512]{1,0:T(8,128)(2,1)S(1)} %select_convert_fusion.5), channel_id=1, source_target_pairs={{0,4},{1,5},{2,6},{3,7},{4,0},{5,1},{6,2},{7,3},{8,12},{9,13},{10,... | collective-permute-start | bytes 196616 | tf_op jit(solution)/shard_map/ppermute | solution.py:98
  62.0 6.1 %collective-permute-start.11 = (f32[256,512]{1,0:T(8,128)S(1)}, f32[256,512]{1,0:T(8,128)S(1)}, u32[]{:S(2)}, u32[]{:S(2)}) collective-permute-start(f32[256,512]{1,0:T(8,128)S(1)} %slice_select_fusion.1), channel_id=1, source_target_pairs={{0,1},{1,0},{2,3},{3,2},{4,5},{5,4},{6,7},{7,6},{8,9},{9,8},{10,11... | collective-permute-start | bytes 1572872 | tf_op jit(solution)/shard_map/ppermute | solution.py:98
  64.7 5.2 %collective-permute-start.20 = (f32[256,512]{1,0:T(8,128)S(1)}, f32[256,512]{1,0:T(8,128)S(1)}, u32[]{:S(2)}, u32[]{:S(2)}) collective-permute-start(f32[256,512]{1,0:T(8,128)S(1)} %slice_select_fusion), channel_id=1, source_target_pairs={{0,1},{1,0},{2,3},{3,2},{4,5},{5,4},{6,7},{7,6},{8,9},{9,8},{10,11... | collective-permute-start | bytes 1572872 | tf_op jit(solution)/shard_map/ppermute | solution.py:98
  65.3 23.3 %collective-permute-start.3 = (bf16[32,512]{1,0:T(8,128)(2,1)S(1)}, bf16[32,512]{1,0:T(8,128)(2,1)S(1)}, u32[]{:S(2)}, u32[]{:S(2)}) collective-permute-start(bf16[32,512]{1,0:T(8,128)(2,1)S(1)} %select_convert_fusion.8), channel_id=1, source_target_pairs={{0,8},{1,9},{2,10},{3,11},{4,12},{5,13},{6,14},{7,15},{8,0},{9,1},... | collective-permute-start | bytes 98312 | tf_op jit(solution)/shard_map/ppermute | solution.py:98
  68.4 6.5 %collective-permute-start.12 = (bf16[128,512]{1,0:T(8,128)(2,1)S(1)}, bf16[128,512]{1,0:T(8,128)(2,1)S(1)}, u32[]{:S(2)}, u32[]{:S(2)}) collective-permute-start(bf16[128,512]{1,0:T(8,128)(2,1)S(1)} %select_convert_fusion.1), channel_id=1, source_target_pairs={{0,2},{1,3},{2,0},{3,1},{4,6},{5,7},{6,4},{7,5},{8,10},{9,11},{10,... | collective-permute-start | bytes 393224 | tf_op jit(solution)/shard_map/ppermute | solution.py:98
  70.1 6.4 %collective-permute-start.21 = (bf16[128,512]{1,0:T(8,128)(2,1)S(1)}, bf16[128,512]{1,0:T(8,128)(2,1)S(1)}, u32[]{:S(2)}, u32[]{:S(2)}) collective-permute-start(bf16[128,512]{1,0:T(8,128)(2,1)S(1)} %select_convert_fusion), channel_id=1, source_target_pairs={{0,2},{1,3},{2,0},{3,1},{4,6},{5,7},{6,4},{7,5},{8,10},{9,11},{10,... | collective-permute-start | bytes 393224 | tf_op jit(solution)/shard_map/ppermute | solution.py:98
  74.9 4.5 %collective-permute-start.13 = (bf16[64,512]{1,0:T(8,128)(2,1)S(1)}, bf16[64,512]{1,0:T(8,128)(2,1)S(1)}, u32[]{:S(2)}, u32[]{:S(2)}) collective-permute-start(bf16[64,512]{1,0:T(8,128)(2,1)S(1)} %select_convert_fusion.4), channel_id=1, source_target_pairs={{0,4},{1,5},{2,6},{3,7},{4,0},{5,1},{6,2},{7,3},{8,12},{9,13},{10,... | collective-permute-start | bytes 196616 | tf_op jit(solution)/shard_map/ppermute | solution.py:98
  76.6 4.7 %collective-permute-start.22 = (bf16[64,512]{1,0:T(8,128)(2,1)S(1)}, bf16[64,512]{1,0:T(8,128)(2,1)S(1)}, u32[]{:S(2)}, u32[]{:S(2)}) collective-permute-start(bf16[64,512]{1,0:T(8,128)(2,1)S(1)} %select_convert_fusion.3), channel_id=1, source_target_pairs={{0,4},{1,5},{2,6},{3,7},{4,0},{5,1},{6,2},{7,3},{8,12},{9,13},{10,... | collective-permute-start | bytes 196616 | tf_op jit(solution)/shard_map/ppermute | solution.py:98
  79.4 4.9 %collective-permute-start.14 = (bf16[32,512]{1,0:T(8,128)(2,1)S(1)}, bf16[32,512]{1,0:T(8,128)(2,1)S(1)}, u32[]{:S(2)}, u32[]{:S(2)}) collective-permute-start(bf16[32,512]{1,0:T(8,128)(2,1)S(1)} %select_convert_fusion.7), channel_id=1, source_target_pairs={{0,8},{1,9},{2,10},{3,11},{4,12},{5,13},{6,14},{7,15},{8,0},{9,1},... | collective-permute-start | bytes 98312 | tf_op jit(solution)/shard_map/ppermute | solution.py:98
  81.4 4.9 %collective-permute-start.23 = (bf16[32,512]{1,0:T(8,128)(2,1)S(1)}, bf16[32,512]{1,0:T(8,128)(2,1)S(1)}, u32[]{:S(2)}, u32[]{:S(2)}) collective-permute-start(bf16[32,512]{1,0:T(8,128)(2,1)S(1)} %select_convert_fusion.6), channel_id=1, source_target_pairs={{0,8},{1,9},{2,10},{3,11},{4,12},{5,13},{6,14},{7,15},{8,0},{9,1},... | collective-permute-start | bytes 98312 | tf_op jit(solution)/shard_map/ppermute | solution.py:98
  84.4 4.3 %collective-permute-start.15 = (f32[32,512]{1,0:T(8,128)S(1)}, f32[32,512]{1,0:T(8,128)S(1)}, u32[]{:S(2)}, u32[]{:S(2)}) collective-permute-start(f32[32,512]{1,0:T(8,128)S(1)} %convert_add_fusion.7), channel_id=1, source_target_pairs={{0,16},{16,0},{1,17},{17,1},{2,18},{18,2},{3,19},{19,3},{4,20},{20... | collective-permute-start | bytes 196616 | tf_op jit(solution)/shard_map/ppermute | solution.py:98
  86.3 4.3 %collective-permute-start.24 = (f32[32,512]{1,0:T(8,128)S(1)}, f32[32,512]{1,0:T(8,128)S(1)}, u32[]{:S(2)}, u32[]{:S(2)}) collective-permute-start(f32[32,512]{1,0:T(8,128)S(1)} %convert_add_fusion.6), channel_id=1, source_target_pairs={{0,16},{16,0},{1,17},{17,1},{2,18},{18,2},{3,19},{19,3},{4,20},{20... | collective-permute-start | bytes 196616 | tf_op jit(solution)/shard_map/ppermute | solution.py:98
  95.0 7.8 %collective-permute-start.16 = (bf16[32,512]{1,0:T(8,128)(2,1)}, bf16[32,512]{1,0:T(8,128)(2,1)}, u32[]{:S(2)}, u32[]{:S(2)}) collective-permute-start(bf16[32,512]{1,0:T(8,128)(2,1)} %get-tuple-element.40), channel_id=1, source_target_pairs={{0,8},{1,9},{2,10},{3,11},{4,12},{5,13},{6,14},{7,15},{8,0},{9,1},... | collective-permute-start | bytes 98312 | tf_op jit(solution)/shard_map/ppermute | solution.py:98
  96.2 29.9 %collective-permute-start.30 = (bf16[640,512]{1,0:T(8,128)(2,1)S(1)}, bf16[640,512]{1,0:T(8,128)(2,1)S(1)}, u32[]{:S(2)}, u32[]{:S(2)}) collective-permute-start(bf16[640,512]{1,0:T(8,128)(2,1)S(1)} %get-tuple-element.8), channel_id=1, source_target_pairs={{0,16},{16,0},{1,17},{17,1},{2,18},{18,2},{3,19},{19,3},{4,20},{20... | collective-permute-start | bytes 1966088 | tf_op jit(solution)/shard_map/ppermute | solution.py:98
  97.8 24.6 %collective-permute-start.31 = (bf16[640,512]{1,0:T(8,128)(2,1)S(1)}, bf16[640,512]{1,0:T(8,128)(2,1)}, u32[]{:S(2)}, u32[]{:S(2)}) collective-permute-start(bf16[640,512]{1,0:T(8,128)(2,1)S(1)} %get-tuple-element.9), channel_id=1, source_target_pairs={{0,16},{16,0},{1,17},{17,1},{2,18},{18,2},{3,19},{19,3},{4,20},{20... | collective-permute-start | bytes 1966088 | tf_op jit(solution)/shard_map/ppermute | solution.py:98
  99.8 5.8 %collective-permute-start.25 = (bf16[32,512]{1,0:T(8,128)(2,1)}, bf16[32,512]{1,0:T(8,128)(2,1)S(1)}, u32[]{:S(2)}, u32[]{:S(2)}) collective-permute-start(bf16[32,512]{1,0:T(8,128)(2,1)} %get-tuple-element.41), channel_id=1, source_target_pairs={{0,8},{1,9},{2,10},{3,11},{4,12},{5,13},{6,14},{7,15},{8,0},{9,1},... | collective-permute-start | bytes 98312 | tf_op jit(solution)/shard_map/ppermute | solution.py:98
  101.6 6.3 %collective-permute-start.4 = (bf16[32,512]{1,0:T(8,128)(2,1)}, bf16[32,512]{1,0:T(8,128)(2,1)S(1)}, u32[]{:S(2)}, u32[]{:S(2)}) collective-permute-start(bf16[32,512]{1,0:T(8,128)(2,1)} %get-tuple-element.48), channel_id=1, source_target_pairs={{0,8},{1,9},{2,10},{3,11},{4,12},{5,13},{6,14},{7,15},{8,0},{9,1},... | collective-permute-start | bytes 98312 | tf_op jit(solution)/shard_map/ppermute | solution.py:98
  103.5 5.7 %collective-permute-start.17 = (bf16[64,512]{1,0:T(8,128)(2,1)S(1)}, bf16[64,512]{1,0:T(8,128)(2,1)S(1)}, u32[]{:S(2)}, u32[]{:S(2)}) collective-permute-start(bf16[64,512]{1,0:T(8,128)(2,1)S(1)} %pad_maximum_fusion.27), channel_id=1, source_target_pairs={{0,4},{1,5},{2,6},{3,7},{4,0},{5,1},{6,2},{7,3},{8,12},{9,13},{10,... | collective-permute-start | bytes 196616 | tf_op jit(solution)/shard_map/ppermute | solution.py:98
  106.3 4.6 %collective-permute-start.26 = (bf16[64,512]{1,0:T(8,128)(2,1)S(1)}, bf16[64,512]{1,0:T(8,128)(2,1)S(1)}, u32[]{:S(2)}, u32[]{:S(2)}) collective-permute-start(bf16[64,512]{1,0:T(8,128)(2,1)S(1)} %pad_maximum_fusion.28), channel_id=1, source_target_pairs={{0,4},{1,5},{2,6},{3,7},{4,0},{5,1},{6,2},{7,3},{8,12},{9,13},{10,... | collective-permute-start | bytes 196616 | tf_op jit(solution)/shard_map/ppermute | solution.py:98
  108.7 4.3 %collective-permute-start.5 = (bf16[64,512]{1,0:T(8,128)(2,1)S(1)}, bf16[64,512]{1,0:T(8,128)(2,1)S(1)}, u32[]{:S(2)}, u32[]{:S(2)}) collective-permute-start(bf16[64,512]{1,0:T(8,128)(2,1)S(1)} %pad_maximum_fusion.26), channel_id=1, source_target_pairs={{0,4},{1,5},{2,6},{3,7},{4,0},{5,1},{6,2},{7,3},{8,12},{9,13},{10,... | collective-permute-start | bytes 196616 | tf_op jit(solution)/shard_map/ppermute | solution.py:98
  109.3 5.0 %collective-permute-start.18 = (bf16[128,512]{1,0:T(8,128)(2,1)S(1)}, bf16[128,512]{1,0:T(8,128)(2,1)S(1)}, u32[]{:S(2)}, u32[]{:S(2)}) collective-permute-start(bf16[128,512]{1,0:T(8,128)(2,1)S(1)} %pad_maximum_fusion.24), channel_id=1, source_target_pairs={{0,2},{1,3},{2,0},{3,1},{4,6},{5,7},{6,4},{7,5},{8,10},{9,11},{10,... | collective-permute-start | bytes 393224 | tf_op jit(solution)/shard_map/ppermute | solution.py:98
  110.9 5.0 %collective-permute-start.27 = (bf16[128,512]{1,0:T(8,128)(2,1)S(1)}, bf16[128,512]{1,0:T(8,128)(2,1)S(1)}, u32[]{:S(2)}, u32[]{:S(2)}) collective-permute-start(bf16[128,512]{1,0:T(8,128)(2,1)S(1)} %pad_maximum_fusion.25), channel_id=1, source_target_pairs={{0,2},{1,3},{2,0},{3,1},{4,6},{5,7},{6,4},{7,5},{8,10},{9,11},{10,... | collective-permute-start | bytes 393224 | tf_op jit(solution)/shard_map/ppermute | solution.py:98
  113.0 5.0 %collective-permute-start.6 = (bf16[128,512]{1,0:T(8,128)(2,1)S(1)}, bf16[128,512]{1,0:T(8,128)(2,1)S(1)}, u32[]{:S(2)}, u32[]{:S(2)}) collective-permute-start(bf16[128,512]{1,0:T(8,128)(2,1)S(1)} %pad_maximum_fusion.23), channel_id=1, source_target_pairs={{0,2},{1,3},{2,0},{3,1},{4,6},{5,7},{6,4},{7,5},{8,10},{9,11},{10,... | collective-permute-start | bytes 393224 | tf_op jit(solution)/shard_map/ppermute | solution.py:98
  116.1 2.2 %collective-permute-start.19 = (bf16[256,512]{1,0:T(8,128)(2,1)S(1)}, bf16[256,512]{1,0:T(8,128)(2,1)S(1)}, u32[]{:S(2)}, u32[]{:S(2)}) collective-permute-start(bf16[256,512]{1,0:T(8,128)(2,1)S(1)} %pad_maximum_fusion.15), channel_id=1, source_target_pairs={{0,1},{1,0},{2,3},{3,2},{4,5},{5,4},{6,7},{7,6},{8,9},{9,8},{10,11... | collective-permute-start | bytes 786440 | tf_op jit(solution)/shard_map/ppermute | solution.py:98
  116.2 2.2 %collective-permute-start.28 = (bf16[256,512]{1,0:T(8,128)(2,1)S(1)}, bf16[256,512]{1,0:T(8,128)(2,1)S(1)}, u32[]{:S(2)}, u32[]{:S(2)}) collective-permute-start(bf16[256,512]{1,0:T(8,128)(2,1)S(1)} %pad_maximum_fusion.16), channel_id=1, source_target_pairs={{0,1},{1,0},{2,3},{3,2},{4,5},{5,4},{6,7},{7,6},{8,9},{9,8},{10,11... | collective-permute-start | bytes 786440 | tf_op jit(solution)/shard_map/ppermute | solution.py:98
  118.2 6.5 %collective-permute-start.7 = (bf16[256,512]{1,0:T(8,128)(2,1)S(1)}, bf16[256,512]{1,0:T(8,128)(2,1)S(1)}, u32[]{:S(2)}, u32[]{:S(2)}) collective-permute-start(bf16[256,512]{1,0:T(8,128)(2,1)S(1)} %pad_maximum_fusion.14), channel_id=1, source_target_pairs={{0,1},{1,0},{2,3},{3,2},{4,5},{5,4},{6,7},{7,6},{8,9},{9,8},{10,11... | collective-permute-start | bytes 786440 | tf_op jit(solution)/shard_map/ppermute | solution.py:98
  119.4 11.6 %collective-permute-start.29 = (bf16[384,512]{0,1:T(8,128)(2,1)S(1)}, bf16[384,512]{0,1:T(8,128)(2,1)S(1)}, u32[]{:S(2)}, u32[]{:S(2)}) collective-permute-start(bf16[384,512]{0,1:T(8,128)(2,1)S(1)} %fusion.28), channel_id=1, source_target_pairs={{0,16},{16,0},{1,17},{17,1},{2,18},{18,2},{3,19},{19,3},{4,20},{20... | collective-permute-start | bytes 1179656 | tf_op jit(solution)/shard_map/ppermute | solution.py:98
  (5 other events, 80.9 us)

commit v2 on v1

v2 whole, which is shorter than its diff:
```python
import functools

import jax
import jax.numpy as jnp
from jax import lax
from jax.experimental import pallas as pl
from jax.experimental.pallas import tpu as pltpu
from jax.sharding import PartitionSpec as P

CAP = 4
WIRE = jnp.bfloat16
HELPS, FOREIGN, PLACE, COUNTS = 0, 1, 2, 3
PARAMS = pltpu.CompilerParams(vmem_limit_bytes=40 * 1024 * 1024)
SMEM_SPEC = pl.BlockSpec(memory_space=pltpu.SMEM)
ANY_SPEC = pl.BlockSpec(memory_space=pl.ANY)


def general(factors, occ_energy, virt_energy, tile_table):
    owned = factors.shape[0]
    width = factors.shape[2]
    tiles = tile_table.shape[0]
    groups = lax.axis_size("orb")
    mine = lax.axis_index("orb")
    first = tile_table[:, 0]
    second = tile_table[:, 1]
    helper = tile_table[:, 2]
    block_ids = jnp.arange(owned * groups, dtype=jnp.int32)
    group_ids = jnp.arange(groups, dtype=jnp.int32)
    local_ids = jnp.arange(owned, dtype=jnp.int32)
    touched = (
        (first[:, None] == block_ids[None, :]) | (second[:, None] == block_ids[None, :])
    ).astype(jnp.int32)
    helped = (helper[:, None] == group_ids[None, :]).astype(jnp.int32)
    usage = jnp.sum(helped[:, :, None] * touched[:, None, :], axis=0) > 0
    usage = usage.reshape(groups, groups, owned).astype(jnp.int32)
    own_usage = jnp.take(usage, mine, axis=1)
    send_pick = jnp.sum(own_usage * local_ids[None, :], axis=1)
    outgoing = jnp.stack(
        [
            lax.dynamic_index_in_dim(factors, send_pick[group], 0, keepdims=False)
            for group in range(groups)
        ]
    )
    incoming = lax.all_to_all(outgoing, "orb", split_axis=0, concat_axis=0, tiled=True)
    store = jnp.concatenate([factors, incoming], axis=0)

    def position(block):
        owner = block // owned
        return jnp.where(owner == mine, block % owned, owned + owner)

    is_mine = (helper == mine).astype(jnp.int32)
    tile_ids = jnp.arange(tiles, dtype=jnp.int32)
    earlier = (tile_ids[None, :] < tile_ids[:, None]).astype(jnp.int32)
    rank = jnp.sum(earlier * is_mine[None, :], axis=1)
    slot_ids = jnp.arange(CAP, dtype=jnp.int32)
    picked = is_mine[None, :] * (rank[None, :] == slot_ids[:, None]).astype(jnp.int32)
    valid = jnp.sum(picked, axis=1)
    tile_p = jnp.sum(picked * first[None, :], axis=1)
    tile_q = jnp.sum(picked * second[None, :], axis=1)
    place_p = position(tile_p)
    place_q = position(tile_q)
    energy_p = jnp.take(virt_energy, tile_p, axis=0)
    energy_q = jnp.take(virt_energy, tile_q, axis=0)
    occ_sum = jnp.take(occ_energy, tile_p) + jnp.take(occ_energy, tile_q)
    denominators = energy_p[:, :, None] + energy_q[:, None, :] - occ_sum[:, None, None]

    def partners(slot):
        block_p = lax.dynamic_index_in_dim(store, place_p[slot], 0, keepdims=False)
        block_q = lax.dynamic_index_in_dim(store, place_q[slot], 0, keepdims=False)
        return (block_p, block_q)

    def fill(slot, buffer):
        block_p, block_q = partners(slot)
        return lax.dynamic_update_index_in_dim(buffer, outer(block_p, block_q), slot, 0)

    buffer = lax.fori_loop(0, CAP, fill, jnp.zeros((CAP, width, width), jnp.float32))
    summed = lax.psum(buffer, "aux")
    all_amps = (summed / denominators).astype(jnp.bfloat16)

    def apply_all(slot, gathered):
        block_p, block_q = partners(slot)
        amplitudes = lax.dynamic_index_in_dim(all_amps, slot, 0, keepdims=False)
        amplitudes = jnp.where(valid[slot] > 0, amplitudes, jnp.zeros_like(amplitudes))
        gathered = gathered.at[place_p[slot]].add(right_t(block_q, amplitudes))
        return gathered.at[place_q[slot]].add(right(block_p, amplitudes))

    gathered = lax.fori_loop(0, CAP, apply_all, jnp.zeros(store.shape, jnp.float32))
    helper_part = gathered[owned:].astype(jnp.bfloat16)
    returned = lax.all_to_all(helper_part, "orb", split_axis=0, concat_axis=0, tiled=True)
    landing = (send_pick[:, None] == local_ids[None, :]).astype(jnp.float32)
    gamma = gathered[:owned] + jnp.einsum(
        "dj,dav->jav", landing, returned.astype(jnp.float32), precision=lax.Precision.HIGHEST
    )
    return gamma.astype(jnp.bfloat16)


def outer(a, b):
    return lax.dot_general(a, b, (((0,), (0,)), ((), ())), preferred_element_type=jnp.float32)


def right(a, m):
    return jnp.dot(a, m, preferred_element_type=jnp.float32)


def right_t(a, m):
    return lax.dot_general(a, m, (((1,), (1,)), ((), ())), preferred_element_type=jnp.float32)


def swap(value, axis, bit):
    size = lax.axis_size(axis)
    return lax.ppermute(value, axis, [(i, i ^ (1 << bit)) for i in range(size)])


def halve(kept, sent, axis, wires):
    me = lax.axis_index(axis)
    part = kept + swap(sent, axis, 0).astype(jnp.float32)
    for bit, wire in list(enumerate(wires))[1:]:
        high = ((me >> bit) & 1) == 1
        half = part.shape[0] // 2
        low_rows, high_rows = part[:half], part[half:]
        sent = jnp.where(high, low_rows, high_rows).astype(wire)
        kept = jnp.where(high, high_rows, low_rows)
        part = kept + swap(sent, axis, bit).astype(jnp.float32)
    return part


def double(part, axis, bits):
    for bit in reversed(range(1, bits)):
        part = jnp.concatenate([part, swap(part, axis, bit)], axis=0)
    return part, swap(part, axis, 0)


def after(value, *others):
    return lax.optimization_barrier((value, *others))[0]


def plan_kernel(tiles, bits, half, table, factors, plan, pay, sem):
    helper = table[0, 2]
    helps = (lax.axis_index("orb") == helper).astype(jnp.int32)
    low, foreign_low = helper * 2, (1 - helper) * 2
    foreign = jnp.int32(0)
    for t in range(tiles):
        named = (table[t, 0] == foreign_low + 1) | (table[t, 1] == foreign_low + 1)
        foreign = foreign | named.astype(jnp.int32)
    block = jnp.where(helps == 1, 0, foreign)
    copy = pltpu.make_async_copy(
        factors.at[block, pl.ds(pl.multiple_of(helps * half, half), half)], pay, sem
    )
    copy.start()
    me = lax.axis_index("aux")
    place = jnp.int32(0)
    for bit in range(bits):
        place = place * 2 + ((me >> bit) & 1)
    plan[HELPS], plan[FOREIGN], plan[PLACE] = helps, foreign, place
    pairs = ((low, low + 1), (low, foreign_low + foreign), (low + 1, foreign_low + foreign))
    for n, (a, b) in enumerate(pairs):
        count = jnp.int32(0)
        for t in range(tiles):
            p, q = table[t, 0], table[t, 1]
            same = ((p == a) & (q == b)) | ((p == b) & (q == a))
            count = count + same.astype(jnp.int32)
        plan[COUNTS + n] = count
    copy.wait()


def pack_kernel(quarter, plan, factors, pay2, pay3, sems):
    helps, foreign = plan[HELPS], plan[FOREIGN]
    b0, b1 = jnp.where(helps == 1, 0, foreign), jnp.where(helps == 1, 1, foreign)
    second = pl.multiple_of((2 + helps) * quarter, quarter)
    third = pl.multiple_of((3 - helps) * quarter, quarter)
    copies = [
        pltpu.make_async_copy(factors.at[b1, pl.ds(second, quarter)], pay2, sems.at[0]),
        pltpu.make_async_copy(
            factors.at[b1, pl.ds(third, quarter)], pay3.at[pl.ds(0, quarter)], sems.at[1]
        ),
        pltpu.make_async_copy(
            factors.at[b0, pl.ds(quarter, quarter)], pay3.at[pl.ds(quarter, quarter)], sems.at[2]
        ),
        pltpu.make_async_copy(
            factors.at[b1, pl.ds(quarter, quarter)], pay3.at[pl.ds(2 * quarter, quarter)], sems.at[3]
        ),
    ]
    for copy in copies:
        copy.start()
    for copy in copies:
        copy.wait()


def split_halves(acc, kept, sent, core):
    half = kept.shape[0]
    kept[...] = acc[pl.ds(pl.multiple_of(core * half, half), half), :]
    sent[...] = acc[pl.ds(pl.multiple_of((1 - core) * half, half), half), :].astype(sent.dtype)


def own_kernel(plan, blocks, kept, sent, acc):
    step = pl.program_id(0)
    term = outer(blocks[0], blocks[1])

    @pl.when(step == 0)
    def _():
        acc[...] = term

    @pl.when(step > 0)
    def _():
        acc[...] += term

    @pl.when(step == pl.num_programs(0) - 1)
    def _():
        split_halves(acc, kept, sent, lax.axis_index("aux") & 1)


def first_kernel(plan, own, got, kept, sent, acc):
    step = pl.program_id(0)

    @pl.when(step == 0)
    def _():
        acc[...] = jnp.zeros_like(acc)

    @pl.when(plan[HELPS] == 1)
    def _():
        acc[...] += outer(own[0], got[...])

    @pl.when(plan[HELPS] == 0)
    def _():
        acc[...] += outer(got[...], own[0])

    @pl.when(step == pl.num_programs(0) - 1)
    def _():
        split_halves(acc, kept, sent, lax.axis_index("aux") & 1)


def second_kernel(plan, own, got1, got2, kept, sent, acc):
    step = pl.program_id(0)
    last = pl.num_programs(0) - 1

    @pl.when(step == 0)
    def _():
        acc[...] = jnp.zeros_like(acc)

    @pl.when((plan[HELPS] == 1) & (step < last))
    def _():
        acc[...] += outer(own[0], got1[...])

    @pl.when((plan[HELPS] == 1) & (step == last))
    def _():
        acc[...] += outer(own[0], got2[...])

    @pl.when((plan[HELPS] == 0) & (step == last))
    def _():
        acc[...] += outer(got2[...], own[0])

    @pl.when(step == last)
    def _():
        split_halves(acc, kept, sent, lax.axis_index("aux") & 1)


def back_kernel(shard, plan, near0, far0, near1, far1, blocks, back, amp0, amp1):
    arrange(shard, plan, near0, far0, 2, 1, amp0)
    arrange(shard, plan, near1, far1, 1, 0, amp1)
    total = right(blocks[0], amp0[...]) + right(blocks[1], amp1[...])
    back[...] = total.astype(back.dtype)


def arrange(shard, plan, near, far, pairs, which, out):
    count = out.shape[0] // shard
    for source, base in ((near, 0), (far, count // 2)):
        for n in range(count // 2):
            row = pl.multiple_of((plan[PLACE] ^ (base + n)) * shard, shard)
            begin = (n * pairs + which) * shard
            out[pl.ds(row, shard), :] = source[begin : begin + shard, :]


def last_kernel(shard, plan, near0, far0, near1, far1, got1, got2, early_a, early_b, blocks, out, own, amp0, amp1):
    seg = pl.program_id(0)
    helps = plan[HELPS] == 1

    @pl.when(seg == 0)
    def _():
        arrange(shard, plan, near0, far0, 2, 0, own)
        arrange(shard, plan, near0, far0, 2, 1, amp0)
        arrange(shard, plan, near1, far1, 1, 0, amp1)

    @pl.when(helps)
    def _():
        foreign = jnp.where(seg < 2, got1[...], jnp.where(seg == 2, got2[...], early_a[...]))
        out[0] = (right_t(blocks[1], own[...]) + right_t(foreign, amp0[...])).astype(out.dtype)
        out[1] = (right(blocks[0], own[...]) + right_t(foreign, amp1[...])).astype(out.dtype)

    @pl.when(jnp.logical_not(helps))
    def _():
        rows0 = jnp.where(seg == 1, early_a[...], got1[...])
        rows1 = jnp.where(seg == 3, got2[...], early_b[...])
        out[...] = jnp.zeros_like(out)
        total = right(rows0, amp0[...]) + right(rows1, amp1[...])
        out[plan[FOREIGN]] = total.astype(out.dtype)


def put_kernel(quarter, plan, back, gamma_in, gamma, sem):
    @pl.when(plan[HELPS] == 0)
    def _():
        copy = pltpu.make_async_copy(back, gamma.at[plan[FOREIGN], pl.ds(0, quarter)], sem)
        copy.start()
        copy.wait()


def two_groups(factors, occ_energy, virt_energy, tile_table):
    owned, rows, width = factors.shape
    aux = lax.axis_size("aux")
    bits = aux.bit_length() - 1
    tiles = tile_table.shape[0]
    half, quarter = rows // 2, rows // 4
    shard = width // aux
    wires = [jnp.float32] + [WIRE] * (bits - 1)
    dtype = factors.dtype

    plan, pay1 = pl.pallas_call(
        functools.partial(plan_kernel, tiles, bits, half),
        out_shape=(
            jax.ShapeDtypeStruct((8,), jnp.int32),
            jax.ShapeDtypeStruct((half, width), dtype),
        ),
        in_specs=[SMEM_SPEC, ANY_SPEC],
        out_specs=(SMEM_SPEC, ANY_SPEC),
        scratch_shapes=[pltpu.SemaphoreType.DMA],
        compiler_params=PARAMS,
    )(tile_table, factors)
    got1 = swap(pay1, "orb", 0)

    pay2, pay3 = pl.pallas_call(
        functools.partial(pack_kernel, quarter),
        out_shape=(
            jax.ShapeDtypeStruct((quarter, width), dtype),
            jax.ShapeDtypeStruct((3 * quarter, width), dtype),
        ),
        in_specs=[SMEM_SPEC, ANY_SPEC],
        out_specs=(ANY_SPEC, ANY_SPEC),
        scratch_shapes=[pltpu.SemaphoreType.DMA((4,))],
        compiler_params=PARAMS,
    )(plan, factors)

    def halves():
        return (
            jax.ShapeDtypeStruct((width // 2, width), jnp.float32),
            jax.ShapeDtypeStruct((width // 2, width), wires[0]),
        )

    def whole(shape):
        return pl.BlockSpec(shape, lambda i, plan: (0,) * len(shape))

    def run(kernel, steps, specs, out_shape, out_specs, scratch, cost):
        return pl.pallas_call(
            kernel,
            out_shape=out_shape,
            grid_spec=pltpu.PrefetchScalarGridSpec(
                num_scalar_prefetch=1,
                grid=(steps,),
                in_specs=specs,
                out_specs=out_specs,
                scratch_shapes=scratch,
            ),
            compiler_params=PARAMS,
            cost_estimate=pl.CostEstimate(
                flops=cost * 2 * quarter * width * width,
                bytes_accessed=cost * 2 * quarter * width * 2,
                transcendentals=0,
            ),
        )

    half_spec = whole((width // 2, width))
    square = pltpu.VMEM((width, width), jnp.float32)
    block = (1, quarter, width)

    kept, sent = run(
        own_kernel, 4, [pl.BlockSpec((2, quarter, width), lambda i, plan: (0, i, 0))],
        halves(), (half_spec, half_spec), [square], 4,
    )(plan, factors)
    sum01 = halve(kept, sent, "aux", wires)

    helper = tile_table[0, 2]
    low, foreign = helper * owned, (1 - helper) * owned + plan[FOREIGN]
    offset = plan[PLACE] * shard

    def weight(n, a, b):
        virt_a = lax.dynamic_slice(virt_energy, (a, offset), (1, shard))[0]
        virt_b = lax.dynamic_slice(virt_energy, (b, 0), (1, width))[0]
        occ_a = lax.dynamic_index_in_dim(occ_energy, a, 0, keepdims=False)
        occ_b = lax.dynamic_index_in_dim(occ_energy, b, 0, keepdims=False)
        denominators = virt_a[:, None] + virt_b[None, :] - occ_a - occ_b
        return plan[COUNTS + n].astype(jnp.float32) / denominators

    weights = (weight(0, low, low + 1), weight(1, low, foreign), weight(2, low + 1, foreign))
    got1, sum01, *weights = lax.optimization_barrier((got1, sum01, *weights))
    got2 = swap(after(pay2, got1), "orb", 0)

    def both(value):
        return value + swap(value, "orb", 0)

    kept, sent = run(
        first_kernel, 2,
        [
            pl.BlockSpec(
                block,
                lambda i, plan: (
                    jnp.where(plan[HELPS] == 1, 0, plan[FOREIGN]),
                    jnp.where(plan[HELPS] == 1, i, 2 + i),
                    0,
                ),
            ),
            pl.BlockSpec((quarter, width), lambda i, plan: (i, 0)),
        ],
        halves(), (half_spec, half_spec), [square], 2,
    )(plan, factors, got1)
    sum0f = both(halve(kept, sent, "aux", wires))
    shards0 = jnp.concatenate(
        [(sum01 * weights[0]).astype(dtype), (sum0f * weights[1]).astype(dtype)], axis=0
    )
    near0, far0 = double(shards0, "aux", bits)

    got3 = swap(after(pay3, got2), "orb", 0)
    kept, sent = run(
        second_kernel, 3,
        [
            pl.BlockSpec(
                block,
                lambda i, plan: (
                    jnp.where(plan[HELPS] == 1, 1, plan[FOREIGN]),
                    jnp.where(plan[HELPS] == 1, i, 3),
                    0,
                ),
            ),
            pl.BlockSpec((quarter, width), lambda i, plan: (jnp.minimum(i, 1), 0)),
            whole((quarter, width)),
        ],
        halves(), (half_spec, half_spec), [square], 3,
    )(plan, factors, got1, got2)
    sum1f = both(halve(kept, sent, "aux", wires))
    near1, far1 = double((sum1f * weights[2]).astype(dtype), "aux", bits)

    amp_specs = [whole(near0.shape), whole(near0.shape), whole(near1.shape), whole(near1.shape)]
    amp = pltpu.VMEM((width, width), dtype)
    back = run(
        functools.partial(back_kernel, shard), 1,
        amp_specs + [pl.BlockSpec((2, quarter, width), lambda i, plan: (0, 0, 0))],
        jax.ShapeDtypeStruct((quarter, width), dtype), whole((quarter, width)), [amp, amp], 2,
    )(plan, near0, far0, near1, far1, factors)
    got4 = swap(back, "orb", 0)

    def at(helper_blocks, owner_blocks):
        def pick(i, table):
            index = jnp.int32(table[-1])
            for n in range(len(table) - 1):
                index = jnp.where(i == n, table[n], index)
            return index

        return pl.BlockSpec(
            (quarter, width),
            lambda i, plan: (
                jnp.where(plan[HELPS] == 1, pick(i, helper_blocks), pick(i, owner_blocks)),
                0,
            ),
        )

    pieces = pl.BlockSpec((2, quarter, width), lambda i, plan: (0, i, 0))
    gamma = run(
        functools.partial(last_kernel, shard), 4,
        amp_specs
        + [
            at((0, 1, 1, 1), (0, 0, 0, 1)),
            whole((quarter, width)),
            at((0, 0, 0, 0), (1, 1, 1, 1)),
            at((0, 0, 0, 0), (2, 2, 0, 0)),
            pieces,
        ],
        jax.ShapeDtypeStruct(factors.shape, dtype), pieces, [amp, amp, amp], 12,
    )(plan, near0, far0, near1, far1, got1, got2, got3, got3, factors)

    return pl.pallas_call(
        functools.partial(put_kernel, quarter),
        out_shape=jax.ShapeDtypeStruct(factors.shape, dtype),
        in_specs=[SMEM_SPEC, ANY_SPEC, ANY_SPEC],
        out_specs=ANY_SPEC,
        scratch_shapes=[pltpu.SemaphoreType.DMA],
        input_output_aliases={2: 0},
        compiler_params=PARAMS,
    )(plan, got4, gamma)


def shards(factors, occ_energy, virt_energy, tile_table):
    groups = lax.axis_size("orb")
    aux = lax.axis_size("aux")
    simple = groups == 2 and factors.shape[0] == 2 and tile_table.shape[0] <= CAP
    width = factors.shape[2]
    whole_shards = aux & (aux - 1) == 0 and width % (32 * aux) == 0
    if simple and whole_shards and factors.shape[1] % 64 == 0:
        return two_groups(factors, occ_energy, virt_energy, tile_table)
    return general(factors, occ_energy, virt_energy, tile_table)


def solution(mesh):
    return jax.shard_map(
        shards,
        mesh=mesh,
        in_specs=(P("orb", "aux", None), P(), P(), P()),
        out_specs=P("orb", "aux", None),
        check_vma=False,
    )
```

time: 146 us -> 150 us (1.027)
  waiting for transfers between devices: 54.3 us -> 85.2 us
  matrix products: 22.4 us -> 0 us
  Pallas kernels: 0 us -> 18.2 us
  starting transfers between devices: 38.5 us -> 28.2 us
  other arithmetic: 13 us -> 3.82 us
  local copies, waits for them, and re-layouts: 13.9 us -> 8.64 us
  between operations: 2.8 us -> 4.73 us
    ppermute x32 -> x26, waiting for transfers between devices: 54.3 us -> 85.2 us  [swap(): return lax.ppermute(value, axis, [(i, i ^ 1 << bit) for i in range(size)])]
    dot_general x12 -> x0, matrix products: 22.4 us -> none  [the longest x4 8.6 us: outer(): lax.dot_general(a, b, (((0,), (0,)), ((), ())), preferred_element_type=jn...]
    pallas_call x0 -> x8, Pallas kernels: none -> 18.2 us  [the longest x1 7.28 us: two_groups(): run(functools.partial(last_kernel, shard), 4, amp_specs + [at((0, 1, 1, 1...]
    ppermute x32 -> x26, starting transfers between devices: 38.5 us -> 28.2 us  [swap(): return lax.ppermute(value, axis, [(i, i ^ 1 << bit) for i in range(size)])]
    another operation x1 -> x0, local copies, waits for them, and re-layouts: 6.2 us -> none  [two_groups(): return jnp.stack([block(0, gamma0), block(1, gamma1)], axis=0)]
    unnamed x10 -> x14, local copies, waits for them, and re-layouts: 0.03 us -> 5.95 us
    convert_element_type x1, other arithmetic: 4.37 us -> 0.02 us  [two_groups(): near1, far1 = double((sum1f * weights[2]).astype(dtype), 'aux', bits)]
    select_n x14 -> x0, other arithmetic: 3.86 us -> none  [the longest x11 2.82 us: double(): jnp.where(high, other, part)]
  transfers between devices with their start and end apart: 32 -> 26, of which waited for: 15 -> 16; matrix products, arithmetic and copies ran while one was open for 21% -> 4% of each run, Pallas kernels for 0% -> 8%
where the time goes in v2:
time: 150 us; the launch traced here: 149 us
  waiting for transfers between devices  85.2 us (57%)
  starting transfers between devices  28.2 us (19%)
  Pallas kernels  18.2 us (12%)
  local copies, waits for them, and re-layouts  8.64 us (6%)
  between operations  4.73 us (3%)
  other arithmetic  3.82 us (3%)
    ppermute x26, waiting for transfers between devices, swap(): return lax.ppermute(value, axis, [(i, i ^ 1 << bit) for i in range(size)])  85.2 us
    ppermute x26, starting transfers between devices, swap(): return lax.ppermute(value, axis, [(i, i ^ 1 << bit) for i in range(size)])  28.2 us
    pallas_call x1, Pallas kernels, two_groups(): run(functools.partial(last_kernel, shard), 4, amp_specs + [at((0, 1, 1, 1...  7.28 us
    unnamed x14, local copies, waits for them, and re-layouts  5.95 us
    pallas_call x1, Pallas kernels, two_groups(): run(own_kernel, 4, [pl.BlockSpec((2, quarter, width), lambda i, plan: (0,...  3.17 us
  transfers between devices with their start and end apart: 26, of which 16 were waited for; matrix products, arithmetic and copies ran while one was open for 4% of the time, Pallas kernels for 8%

profile of v2, /device:TPU:0, one launch (start us, length us, event | category | flops | bytes accessed | tf_op | source)
XLA Modules:
  0.0 148.9 jit_solution(6885286090333459989)
XLA Ops:
  0.0 2.2 %copy-done = bf16[2,2048,512]{2,1,0:T(8,128)(2,1)S(1)} copy-done((bf16[2,2048,512]{2,1,0:T(8,128)(2,1)S(1)}, bf16[2,2048,512]{2,1,0:T(8,128)(2,1)}, u32[]{:S(2)}) %copy-start) | copy-done | bytes 4194328
  5.1 3.2 %shard_map.47 = (f32[256,512]{1,0:T(8,128)S(1)}, f32[256,512]{1,0:T(8,128)S(1)}) custom-call(s32[8]{0:T(128)S(1)} %get-tuple-element.22.plan, bf16[2,2048,512]{2,1,0:T(8,128)(2,1)S(1)} %copy-done.1), custom_call_target="tpu_custom_call" | custom-call | flops 1073741824 | bytes 4194304 | tf_op jit(solution)/shard_map/pallas_call | solution.py:373
  8.8 2.6 %collective-permute-start = (bf16[1024,512]{1,0:T(8,128)(2,1)S(1)}, bf16[1024,512]{1,0:T(8,128)(2,1)S(1)}, u32[]{:S(2)}, u32[]{:S(2)}) collective-permute-start(bf16[1024,512]{1,0:T(8,128)(2,1)S(1)} %get-tuple-element.23), channel_id=1, source_target_pairs={{0,16},{16,0},{1,17},{17,1},{2,18},{18,2},{3,19},{19,3},{4,20},{20... | collective-permute-start | bytes 3145736 | tf_op jit(solution)/shard_map/ppermute | solution.py:111
  12.5 2.0 %collective-permute-start.2 = (bf16[128,512]{1,0:T(8,128)(2,1)S(1)}, bf16[128,512]{1,0:T(8,128)(2,1)S(1)}, u32[]{:S(2)}, u32[]{:S(2)}) collective-permute-start(bf16[128,512]{1,0:T(8,128)(2,1)S(1)} %select_convert_fusion.2), channel_id=1, source_target_pairs={{0,2},{1,3},{2,0},{3,1},{4,6},{5,7},{6,4},{7,5},{8,10},{9,11},{10,... | collective-permute-start | bytes 393224 | tf_op jit(solution)/shard_map/ppermute | solution.py:111
  21.6 1.6 %collective-permute-start.3 = (bf16[64,512]{1,0:T(8,128)(2,1)S(1)}, bf16[64,512]{1,0:T(8,128)(2,1)S(1)}, u32[]{:S(2)}, u32[]{:S(2)}) collective-permute-start(bf16[64,512]{1,0:T(8,128)(2,1)S(1)} %select_convert_fusion.5), channel_id=1, source_target_pairs={{0,4},{1,5},{2,6},{3,7},{4,0},{5,1},{6,2},{7,3},{8,12},{9,13},{10,... | collective-permute-start | bytes 196616 | tf_op jit(solution)/shard_map/ppermute | solution.py:111
  23.3 2.6 %collective-permute-done.3 = bf16[64,512]{1,0:T(8,128)(2,1)S(1)} collective-permute-done((bf16[64,512]{1,0:T(8,128)(2,1)S(1)}, bf16[64,512]{1,0:T(8,128)(2,1)S(1)}, u32[]{:S(2)}, u32[]{:S(2)}) %collective-permute-start.3) | collective-permute-done | bytes 65568 | tf_op jit(solution)/shard_map/ppermute | solution.py:111
  26.0 2.7 %collective-permute-start.4 = (bf16[32,512]{1,0:T(8,128)(2,1)S(1)}, bf16[32,512]{1,0:T(8,128)(2,1)S(1)}, u32[]{:S(2)}, u32[]{:S(2)}) collective-permute-start(bf16[32,512]{1,0:T(8,128)(2,1)S(1)} %select_convert_fusion.8), channel_id=1, source_target_pairs={{0,8},{1,9},{2,10},{3,11},{4,12},{5,13},{6,14},{7,15},{8,0},{9,1},... | collective-permute-start | bytes 98312 | tf_op jit(solution)/shard_map/ppermute | solution.py:111
  28.7 2.0 %subtract_divide_fusion = (f32[32,512]{1,0:T(8,128)S(1)}, f32[32,512]{1,0:T(8,128)S(1)}, f32[32,512]{1,0:T(8,128)S(1)}) fusion(f32[32]{0:T(128)S(1)} %get-tuple-element.43, f32[]{:T(128)} %bitcast.12, f32[]{:T(128)} %bitcast.11, f32[512]{0:T(512)S(1)} %bitcast.16, f32[]{:T(128)} %bitcast.6, f32[]{:T(128)} %bitcast.5, f32[32]{0:T(128)S(1)} %get-tuple-element.44, ...), kind=kLoop, calls=%fused_computation.25 | loop fusion | flops 196608 | bytes 200984 | tf_op jit(solution)/shard_map/div | solution.py:389
  30.9 4.2 %collective-permute-done.got.got1 = bf16[1024,512]{1,0:T(8,128)(2,1)S(1)} collective-permute-done((bf16[1024,512]{1,0:T(8,128)(2,1)S(1)}, bf16[1024,512]{1,0:T(8,128)(2,1)S(1)}, u32[]{:S(2)}, u32[]{:S(2)}) %collective-permute-start) | collective-permute-done | bytes 1048608 | tf_op jit(solution)/shard_map/ppermute | solution.py:111
  35.1 2.2 %copy-done.2 = bf16[2,2048,512]{2,1,0:T(8,128)(2,1)S(1)} copy-done((bf16[2,2048,512]{2,1,0:T(8,128)(2,1)S(1)}, bf16[2,2048,512]{2,1,0:T(8,128)(2,1)}, u32[]{:S(2)}) %copy-start.2) | copy-done | bytes 4194328
  37.3 1.7 %shard_map.48 = (f32[256,512]{1,0:T(8,128)S(1)}, f32[256,512]{1,0:T(8,128)S(1)}) custom-call(s32[8]{0:T(128)S(1)} %get-tuple-element.22.plan, bf16[2,2048,512]{2,1,0:T(8,128)(2,1)S(1)} %copy-done.2, bf16[1024,512]{1,0:T(8,128)(2,1)S(1)} %collective-permute-done.got.got1), custom_call_target="tpu_custom_call" | custom-call | flops 536870912 | bytes 2097152 | tf_op jit(solution)/shard_map/pallas_call | solution.py:398
  39.1 1.9 %collective-permute-done.5 = f32[256,512]{1,0:T(8,128)S(1)} collective-permute-done((f32[256,512]{1,0:T(8,128)S(1)}, f32[256,512]{1,0:T(8,128)S(1)}, u32[]{:S(2)}, u32[]{:S(2)}) %collective-permute-start.5) | collective-permute-done | bytes 524320 | tf_op jit(solution)/shard_map/ppermute | solution.py:111
  41.1 1.8 %collective-permute-start.6 = (bf16[128,512]{1,0:T(8,128)(2,1)S(1)}, bf16[128,512]{1,0:T(8,128)(2,1)S(1)}, u32[]{:S(2)}, u32[]{:S(2)}) collective-permute-start(bf16[128,512]{1,0:T(8,128)(2,1)S(1)} %select_convert_fusion.1), channel_id=1, source_target_pairs={{0,2},{1,3},{2,0},{3,1},{4,6},{5,7},{6,4},{7,5},{8,10},{9,11},{10,... | collective-permute-start | bytes 393224 | tf_op jit(solution)/shard_map/ppermute | solution.py:111
  43.6 1.6 %collective-permute-start.14 = (bf16[512,512]{1,0:T(8,128)(2,1)S(1)}, bf16[512,512]{1,0:T(8,128)(2,1)S(1)}, u32[]{:S(2)}, u32[]{:S(2)}) collective-permute-start(bf16[512,512]{1,0:T(8,128)(2,1)S(1)} %get-tuple-element.33), channel_id=1, source_target_pairs={{0,16},{16,0},{1,17},{17,1},{2,18},{18,2},{3,19},{19,3},{4,20},{20... | collective-permute-start | bytes 1572872 | tf_op jit(solution)/shard_map/ppermute | solution.py:111
  45.2 1.5 collective-permute-done.6
  46.8 1.9 %collective-permute-start.7 = (bf16[64,512]{1,0:T(8,128)(2,1)S(1)}, bf16[64,512]{1,0:T(8,128)(2,1)S(1)}, u32[]{:S(2)}, u32[]{:S(2)}) collective-permute-start(bf16[64,512]{1,0:T(8,128)(2,1)S(1)} %select_convert_fusion.4), channel_id=1, source_target_pairs={{0,4},{1,5},{2,6},{3,7},{4,0},{5,1},{6,2},{7,3},{8,12},{9,13},{10,... | collective-permute-start | bytes 196616 | tf_op jit(solution)/shard_map/ppermute | solution.py:111
  48.6 8.7 %collective-permute-done.14.got2 = bf16[512,512]{1,0:T(8,128)(2,1)S(1)} collective-permute-done((bf16[512,512]{1,0:T(8,128)(2,1)S(1)}, bf16[512,512]{1,0:T(8,128)(2,1)S(1)}, u32[]{:S(2)}, u32[]{:S(2)}) %collective-permute-start.14) | collective-permute-done | bytes 524320 | tf_op jit(solution)/shard_map/ppermute | solution.py:111
  57.4 2.2 %shard_map.50 = (f32[256,512]{1,0:T(8,128)S(1)}, f32[256,512]{1,0:T(8,128)S(1)}) custom-call(s32[8]{0:T(128)S(1)} %get-tuple-element.22.plan, bf16[2,2048,512]{2,1,0:T(8,128)(2,1)S(1)} %copy-done.2, bf16[1024,512]{1,0:T(8,128)(2,1)S(1)} %collective-permute-done.got.got1, bf16[512,512]{1,0:T(8,128)(2,1)S(1)} %collective-permute-done.14.got2), custom_call_target="tpu_custom_call" | custom-call | flops 805306368 | bytes 3145728 | tf_op jit(solution)/shard_map/pallas_call | solution.py:420
  59.7 2.7 %collective-permute-start.8 = (bf16[32,512]{1,0:T(8,128)(2,1)S(1)}, bf16[32,512]{1,0:T(8,128)(2,1)S(1)}, u32[]{:S(2)}, u32[]{:S(2)}) collective-permute-start(bf16[32,512]{1,0:T(8,128)(2,1)S(1)} %select_convert_fusion.7), channel_id=1, source_target_pairs={{0,8},{1,9},{2,10},{3,11},{4,12},{5,13},{6,14},{7,15},{8,0},{9,1},... | collective-permute-start | bytes 98312 | tf_op jit(solution)/shard_map/ppermute | solution.py:111
  63.1 1.5 %collective-permute-done.8 = bf16[32,512]{1,0:T(8,128)(2,1)S(1)} collective-permute-done((bf16[32,512]{1,0:T(8,128)(2,1)S(1)}, bf16[32,512]{1,0:T(8,128)(2,1)S(1)}, u32[]{:S(2)}, u32[]{:S(2)}) %collective-permute-start.8) | collective-permute-done | bytes 32800 | tf_op jit(solution)/shard_map/ppermute | solution.py:111
  66.0 34.4 %collective-permute-done.9 = f32[32,512]{1,0:T(8,128)S(1)} collective-permute-done((f32[32,512]{1,0:T(8,128)S(1)}, f32[32,512]{1,0:T(8,128)S(1)}, u32[]{:S(2)}, u32[]{:S(2)}) %collective-permute-start.9) | collective-permute-done | bytes 65568 | tf_op jit(solution)/shard_map/ppermute | solution.py:111
  100.9 1.6 %collective-permute-start.17 = (bf16[64,512]{1,0:T(8,128)(2,1)S(1)}, bf16[64,512]{1,0:T(8,128)(2,1)S(1)}, u32[]{:S(2)}, u32[]{:S(2)}) collective-permute-start(bf16[64,512]{1,0:T(8,128)(2,1)S(1)} %select_convert_fusion.3), channel_id=1, source_target_pairs={{0,4},{1,5},{2,6},{3,7},{4,0},{5,1},{6,2},{7,3},{8,12},{9,13},{10,... | collective-permute-start | bytes 196616 | tf_op jit(solution)/shard_map/ppermute | solution.py:111
  102.6 3.3 %collective-permute-done.10 = bf16[64,512]{1,0:T(8,128)(2,1)S(1)} collective-permute-done((bf16[64,512]{1,0:T(8,128)(2,1)S(1)}, bf16[64,512]{1,0:T(8,128)(2,1)S(1)}, u32[]{:S(2)}, u32[]{:S(2)}) %collective-permute-start.10) | collective-permute-done | bytes 65568 | tf_op jit(solution)/shard_map/ppermute | solution.py:111
  105.9 1.4 collective-permute-start.11
  108.7 3.9 %collective-permute-done.18 = bf16[32,512]{1,0:T(8,128)(2,1)S(1)} collective-permute-done((bf16[32,512]{1,0:T(8,128)(2,1)S(1)}, bf16[32,512]{1,0:T(8,128)(2,1)S(1)}, u32[]{:S(2)}, u32[]{:S(2)}) %collective-permute-start.18) | collective-permute-done | bytes 32800 | tf_op jit(solution)/shard_map/ppermute | solution.py:111
  113.9 3.0 %collective-permute-done.19 = f32[32,512]{1,0:T(8,128)S(1)} collective-permute-done((f32[32,512]{1,0:T(8,128)S(1)}, f32[32,512]{1,0:T(8,128)S(1)}, u32[]{:S(2)}, u32[]{:S(2)}) %collective-permute-start.19) | collective-permute-done | bytes 65568 | tf_op jit(solution)/shard_map/ppermute | solution.py:111
  118.1 4.0 %collective-permute-done.20 = bf16[32,512]{1,0:T(8,128)(2,1)S(1)} collective-permute-done((bf16[32,512]{1,0:T(8,128)(2,1)S(1)}, bf16[32,512]{1,0:T(8,128)(2,1)S(1)}, u32[]{:S(2)}, u32[]{:S(2)}) %collective-permute-start.20) | collective-permute-done | bytes 32800 | tf_op jit(solution)/shard_map/ppermute | solution.py:111
  122.4 3.9 %collective-permute-done.21 = bf16[64,512]{1,0:T(8,128)(2,1)S(1)} collective-permute-done((bf16[64,512]{1,0:T(8,128)(2,1)S(1)}, bf16[64,512]{1,0:T(8,128)(2,1)S(1)}, u32[]{:S(2)}, u32[]{:S(2)}) %collective-permute-start.21) | collective-permute-done | bytes 65568 | tf_op jit(solution)/shard_map/ppermute | solution.py:111
  126.9 4.4 %collective-permute-done.22 = bf16[128,512]{1,0:T(8,128)(2,1)S(1)} collective-permute-done((bf16[128,512]{1,0:T(8,128)(2,1)S(1)}, bf16[128,512]{1,0:T(8,128)(2,1)S(1)}, u32[]{:S(2)}, u32[]{:S(2)}) %collective-permute-start.22) | collective-permute-done | bytes 131104 | tf_op jit(solution)/shard_map/ppermute | solution.py:111
  131.5 1.5 %collective-permute-done.23.far1 = bf16[256,512]{1,0:T(8,128)(2,1)S(1)} collective-permute-done((bf16[256,512]{1,0:T(8,128)(2,1)S(1)}, bf16[256,512]{1,0:T(8,128)(2,1)S(1)}, u32[]{:S(2)}, u32[]{:S(2)}) %collective-permute-start.23) | collective-permute-done | bytes 262176 | tf_op jit(solution)/shard_map/ppermute | solution.py:111
  135.0 7.3 %shard_map.52.gamma_in = bf16[2,2048,512]{2,1,0:T(8,128)(2,1)} custom-call(s32[8]{0:T(128)S(1)} %get-tuple-element.22.plan, bf16[512,512]{1,0:T(8,128)(2,1)S(1)} %constant_dynamic-update-slice_fusion.near0, bf16[512,512]{1,0:T(8,128)(2,1)S(1)} %collective-permute-done.13.far0, bf16[256,512]{1,0:T(8,128)(2,1)S(1)} %pad_maximum_fusion.1.near1, ...), custom_call_target="tpu_custom_call" | custom-call | flops 3221225472 | bytes 12582912 | tf_op jit(solution)/shard_map/pallas_call | solution.py:464
  142.2 6.1 %collective-permute-done.24.back = bf16[512,512]{1,0:T(8,128)(2,1)S(1)} collective-permute-done((bf16[512,512]{1,0:T(8,128)(2,1)S(1)}, bf16[512,512]{1,0:T(8,128)(2,1)S(1)}, u32[]{:S(2)}, u32[]{:S(2)}) %collective-permute-start.24) | collective-permute-done | bytes 524320 | tf_op jit(solution)/shard_map/ppermute | solution.py:111
  (79 shorter events, 18.5 us)
Async XLA Ops:
  0.0 2.2 %copy-start = (bf16[2,2048,512]{2,1,0:T(8,128)(2,1)S(1)}, bf16[2,2048,512]{2,1,0:T(8,128)(2,1)}, u32[]{:S(2)}) copy-start(bf16[2,2048,512]{2,1,0:T(8,128)(2,1)} %blocks.5) | copy-start | bytes 12582916
  2.2 0.7 copy-start.3
  2.9 2.2 %copy-start.1 = (bf16[2,2048,512]{2,1,0:T(8,128)(2,1)S(1)}, bf16[2,2048,512]{2,1,0:T(8,128)(2,1)}, u32[]{:S(2)}) copy-start(bf16[2,2048,512]{2,1,0:T(8,128)(2,1)} %blocks.5) | copy-start | bytes 12582916
  2.9 18.0 %copy-start.4 = (f32[4]{0:T(128)S(1)}, f32[4]{0:T(128)}, u32[]{:S(2)}) copy-start(f32[4]{0:T(128)} %param.5) | copy-start | bytes 52
  2.9 18.6 %copy-start.5 = (f32[4,512]{1,0:T(4,128)S(1)}, f32[4,512]{1,0:T(4,128)}, u32[]{:S(2)}) copy-start(f32[4,512]{1,0:T(4,128)} %param.6) | copy-start | bytes 24580
  8.2 3.1 %collective-permute-start.1 = (f32[256,512]{1,0:T(8,128)S(1)}, f32[256,512]{1,0:T(8,128)}, u32[]{:S(2)}, u32[]{:S(2)}) collective-permute-start(f32[256,512]{1,0:T(8,128)S(1)} %get-tuple-element.25), channel_id=1, source_target_pairs={{0,1},{1,0},{2,3},{3,2},{4,5},{5,4},{6,7},{7,6},{8,9},{9,8},{10,11... | collective-permute-start | bytes 1572872 | tf_op jit(solution)/shard_map/ppermute | solution.py:111
  8.8 26.3 %collective-permute-start = (bf16[1024,512]{1,0:T(8,128)(2,1)S(1)}, bf16[1024,512]{1,0:T(8,128)(2,1)S(1)}, u32[]{:S(2)}, u32[]{:S(2)}) collective-permute-start(bf16[1024,512]{1,0:T(8,128)(2,1)S(1)} %get-tuple-element.23), channel_id=1, source_target_pairs={{0,16},{16,0},{1,17},{17,1},{2,18},{18,2},{3,19},{19,3},{4,20},{20... | collective-permute-start | bytes 3145736 | tf_op jit(solution)/shard_map/ppermute | solution.py:111
  12.5 9.0 %collective-permute-start.2 = (bf16[128,512]{1,0:T(8,128)(2,1)S(1)}, bf16[128,512]{1,0:T(8,128)(2,1)S(1)}, u32[]{:S(2)}, u32[]{:S(2)}) collective-permute-start(bf16[128,512]{1,0:T(8,128)(2,1)S(1)} %select_convert_fusion.2), channel_id=1, source_target_pairs={{0,2},{1,3},{2,0},{3,1},{4,6},{5,7},{6,4},{7,5},{8,10},{9,11},{10,... | collective-permute-start | bytes 393224 | tf_op jit(solution)/shard_map/ppermute | solution.py:111
  21.6 4.3 %collective-permute-start.3 = (bf16[64,512]{1,0:T(8,128)(2,1)S(1)}, bf16[64,512]{1,0:T(8,128)(2,1)S(1)}, u32[]{:S(2)}, u32[]{:S(2)}) collective-permute-start(bf16[64,512]{1,0:T(8,128)(2,1)S(1)} %select_convert_fusion.5), channel_id=1, source_target_pairs={{0,4},{1,5},{2,6},{3,7},{4,0},{5,1},{6,2},{7,3},{8,12},{9,13},{10,... | collective-permute-start | bytes 196616 | tf_op jit(solution)/shard_map/ppermute | solution.py:111
  26.0 4.9 %collective-permute-start.4 = (bf16[32,512]{1,0:T(8,128)(2,1)S(1)}, bf16[32,512]{1,0:T(8,128)(2,1)S(1)}, u32[]{:S(2)}, u32[]{:S(2)}) collective-permute-start(bf16[32,512]{1,0:T(8,128)(2,1)S(1)} %select_convert_fusion.8), channel_id=1, source_target_pairs={{0,8},{1,9},{2,10},{3,11},{4,12},{5,13},{6,14},{7,15},{8,0},{9,1},... | collective-permute-start | bytes 98312 | tf_op jit(solution)/shard_map/ppermute | solution.py:111
  35.1 2.2 %copy-start.2 = (bf16[2,2048,512]{2,1,0:T(8,128)(2,1)S(1)}, bf16[2,2048,512]{2,1,0:T(8,128)(2,1)}, u32[]{:S(2)}) copy-start(bf16[2,2048,512]{2,1,0:T(8,128)(2,1)} %blocks.5) | copy-start | bytes 12582916
  39.0 2.0 %collective-permute-start.5 = (f32[256,512]{1,0:T(8,128)S(1)}, f32[256,512]{1,0:T(8,128)S(1)}, u32[]{:S(2)}, u32[]{:S(2)}) collective-permute-start(f32[256,512]{1,0:T(8,128)S(1)} %get-tuple-element.30), channel_id=1, source_target_pairs={{0,1},{1,0},{2,3},{3,2},{4,5},{5,4},{6,7},{7,6},{8,9},{9,8},{10,11... | collective-permute-start | bytes 1572872 | tf_op jit(solution)/shard_map/ppermute | solution.py:111
  41.1 5.6 %collective-permute-start.6 = (bf16[128,512]{1,0:T(8,128)(2,1)S(1)}, bf16[128,512]{1,0:T(8,128)(2,1)S(1)}, u32[]{:S(2)}, u32[]{:S(2)}) collective-permute-start(bf16[128,512]{1,0:T(8,128)(2,1)S(1)} %select_convert_fusion.1), channel_id=1, source_target_pairs={{0,2},{1,3},{2,0},{3,1},{4,6},{5,7},{6,4},{7,5},{8,10},{9,11},{10,... | collective-permute-start | bytes 393224 | tf_op jit(solution)/shard_map/ppermute | solution.py:111
  43.6 13.8 %collective-permute-start.14 = (bf16[512,512]{1,0:T(8,128)(2,1)S(1)}, bf16[512,512]{1,0:T(8,128)(2,1)S(1)}, u32[]{:S(2)}, u32[]{:S(2)}) collective-permute-start(bf16[512,512]{1,0:T(8,128)(2,1)S(1)} %get-tuple-element.33), channel_id=1, source_target_pairs={{0,16},{16,0},{1,17},{17,1},{2,18},{18,2},{3,19},{19,3},{4,20},{20... | collective-permute-start | bytes 1572872 | tf_op jit(solution)/shard_map/ppermute | solution.py:111
  46.8 12.9 %collective-permute-start.7 = (bf16[64,512]{1,0:T(8,128)(2,1)S(1)}, bf16[64,512]{1,0:T(8,128)(2,1)S(1)}, u32[]{:S(2)}, u32[]{:S(2)}) collective-permute-start(bf16[64,512]{1,0:T(8,128)(2,1)S(1)} %select_convert_fusion.4), channel_id=1, source_target_pairs={{0,4},{1,5},{2,6},{3,7},{4,0},{5,1},{6,2},{7,3},{8,12},{9,13},{10,... | collective-permute-start | bytes 196616 | tf_op jit(solution)/shard_map/ppermute | solution.py:111
  59.6 5.7 %collective-permute-start.15 = (f32[256,512]{1,0:T(8,128)S(1)}, f32[256,512]{1,0:T(8,128)S(1)}, u32[]{:S(2)}, u32[]{:S(2)}) collective-permute-start(f32[256,512]{1,0:T(8,128)S(1)} %get-tuple-element.35), channel_id=1, source_target_pairs={{0,1},{1,0},{2,3},{3,2},{4,5},{5,4},{6,7},{7,6},{8,9},{9,8},{10,11... | collective-permute-start | bytes 1572872 | tf_op jit(solution)/shard_map/ppermute | solution.py:111
  59.7 4.9 %collective-permute-start.8 = (bf16[32,512]{1,0:T(8,128)(2,1)S(1)}, bf16[32,512]{1,0:T(8,128)(2,1)S(1)}, u32[]{:S(2)}, u32[]{:S(2)}) collective-permute-start(bf16[32,512]{1,0:T(8,128)(2,1)S(1)} %select_convert_fusion.7), channel_id=1, source_target_pairs={{0,8},{1,9},{2,10},{3,11},{4,12},{5,13},{6,14},{7,15},{8,0},{9,1},... | collective-permute-start | bytes 98312 | tf_op jit(solution)/shard_map/ppermute | solution.py:111
  62.4 72.5 %collective-permute-start.25 = (bf16[1536,512]{1,0:T(8,128)(2,1)S(1)}, bf16[1536,512]{1,0:T(8,128)(2,1)S(1)}, u32[]{:S(2)}, u32[]{:S(2)}) collective-permute-start(bf16[1536,512]{1,0:T(8,128)(2,1)S(1)} %get-tuple-element.38), channel_id=1, source_target_pairs={{0,16},{16,0},{1,17},{17,1},{2,18},{18,2},{3,19},{19,3},{4,20},{20... | collective-permute-start | bytes 4718600 | tf_op jit(solution)/shard_map/ppermute | solution.py:111
  64.6 35.7 %collective-permute-start.9 = (f32[32,512]{1,0:T(8,128)S(1)}, f32[32,512]{1,0:T(8,128)S(1)}, u32[]{:S(2)}, u32[]{:S(2)}) collective-permute-start(f32[32,512]{1,0:T(8,128)S(1)} %convert_add_fusion.7), channel_id=1, source_target_pairs={{0,16},{16,0},{1,17},{17,1},{2,18},{18,2},{3,19},{19,3},{4,20},{20... | collective-permute-start | bytes 196616 | tf_op jit(solution)/shard_map/ppermute | solution.py:111
  65.4 35.4 %collective-permute-start.16 = (bf16[128,512]{1,0:T(8,128)(2,1)S(1)}, bf16[128,512]{1,0:T(8,128)(2,1)S(1)}, u32[]{:S(2)}, u32[]{:S(2)}) collective-permute-start(bf16[128,512]{1,0:T(8,128)(2,1)S(1)} %select_convert_fusion), channel_id=1, source_target_pairs={{0,2},{1,3},{2,0},{3,1},{4,6},{5,7},{6,4},{7,5},{8,10},{9,11},{10,... | collective-permute-start | bytes 393224 | tf_op jit(solution)/shard_map/ppermute | solution.py:111
  100.4 5.5 %collective-permute-start.10 = (bf16[64,512]{1,0:T(8,128)(2,1)S(1)}, bf16[64,512]{1,0:T(8,128)(2,1)S(1)}, u32[]{:S(2)}, u32[]{:S(2)}) collective-permute-start(bf16[64,512]{1,0:T(8,128)(2,1)S(1)} %pad_maximum_fusion.4), channel_id=1, source_target_pairs={{0,8},{1,9},{2,10},{3,11},{4,12},{5,13},{6,14},{7,15},{8,0},{9,1},... | collective-permute-start | bytes 196616 | tf_op jit(solution)/shard_map/ppermute | solution.py:111
  100.9 6.4 %collective-permute-start.17 = (bf16[64,512]{1,0:T(8,128)(2,1)S(1)}, bf16[64,512]{1,0:T(8,128)(2,1)S(1)}, u32[]{:S(2)}, u32[]{:S(2)}) collective-permute-start(bf16[64,512]{1,0:T(8,128)(2,1)S(1)} %select_convert_fusion.3), channel_id=1, source_target_pairs={{0,4},{1,5},{2,6},{3,7},{4,0},{5,1},{6,2},{7,3},{8,12},{9,13},{10,... | collective-permute-start | bytes 196616 | tf_op jit(solution)/shard_map/ppermute | solution.py:111
  105.9 7.4 %collective-permute-start.11 = (bf16[128,512]{1,0:T(8,128)(2,1)S(1)}, bf16[128,512]{1,0:T(8,128)(2,1)S(1)}, u32[]{:S(2)}, u32[]{:S(2)}) collective-permute-start(bf16[128,512]{1,0:T(8,128)(2,1)S(1)} %pad_maximum_fusion.2), channel_id=1, source_target_pairs={{0,4},{1,5},{2,6},{3,7},{4,0},{5,1},{6,2},{7,3},{8,12},{9,13},{10,... | collective-permute-start | bytes 393224 | tf_op jit(solution)/shard_map/ppermute | solution.py:111
  107.4 5.2 %collective-permute-start.18 = (bf16[32,512]{1,0:T(8,128)(2,1)S(1)}, bf16[32,512]{1,0:T(8,128)(2,1)S(1)}, u32[]{:S(2)}, u32[]{:S(2)}) collective-permute-start(bf16[32,512]{1,0:T(8,128)(2,1)S(1)} %select_convert_fusion.6), channel_id=1, source_target_pairs={{0,8},{1,9},{2,10},{3,11},{4,12},{5,13},{6,14},{7,15},{8,0},{9,1},... | collective-permute-start | bytes 98312 | tf_op jit(solution)/shard_map/ppermute | solution.py:111
  112.6 4.3 %collective-permute-start.19 = (f32[32,512]{1,0:T(8,128)S(1)}, f32[32,512]{1,0:T(8,128)S(1)}, u32[]{:S(2)}, u32[]{:S(2)}) collective-permute-start(f32[32,512]{1,0:T(8,128)S(1)} %convert_add_fusion.6), channel_id=1, source_target_pairs={{0,16},{16,0},{1,17},{17,1},{2,18},{18,2},{3,19},{19,3},{4,20},{20... | collective-permute-start | bytes 196616 | tf_op jit(solution)/shard_map/ppermute | solution.py:111
  113.3 9.0 %collective-permute-start.12 = (bf16[256,512]{1,0:T(8,128)(2,1)S(1)}, bf16[256,512]{1,0:T(8,128)(2,1)S(1)}, u32[]{:S(2)}, u32[]{:S(2)}) collective-permute-start(bf16[256,512]{1,0:T(8,128)(2,1)S(1)} %pad_maximum_fusion), channel_id=1, source_target_pairs={{0,2},{1,3},{2,0},{3,1},{4,6},{5,7},{6,4},{7,5},{8,10},{9,11},{10,... | collective-permute-start | bytes 786440 | tf_op jit(solution)/shard_map/ppermute | solution.py:111
  117.0 5.1 %collective-permute-start.20 = (bf16[32,512]{1,0:T(8,128)(2,1)S(1)}, bf16[32,512]{1,0:T(8,128)(2,1)S(1)}, u32[]{:S(2)}, u32[]{:S(2)}) collective-permute-start(bf16[32,512]{1,0:T(8,128)(2,1)S(1)} %multiply_convert_fusion), channel_id=1, source_target_pairs={{0,8},{1,9},{2,10},{3,11},{4,12},{5,13},{6,14},{7,15},{8,0},{9,1},... | collective-permute-start | bytes 98312 | tf_op jit(solution)/shard_map/ppermute | solution.py:111
  122.1 4.3 %collective-permute-start.21 = (bf16[64,512]{1,0:T(8,128)(2,1)S(1)}, bf16[64,512]{1,0:T(8,128)(2,1)S(1)}, u32[]{:S(2)}, u32[]{:S(2)}) collective-permute-start(bf16[64,512]{1,0:T(8,128)(2,1)S(1)} %pad_maximum_fusion.5), channel_id=1, source_target_pairs={{0,4},{1,5},{2,6},{3,7},{4,0},{5,1},{6,2},{7,3},{8,12},{9,13},{10,... | collective-permute-start | bytes 196616 | tf_op jit(solution)/shard_map/ppermute | solution.py:111
  122.3 9.2 %collective-permute-start.13 = (bf16[512,512]{1,0:T(8,128)(2,1)S(1)}, bf16[512,512]{1,0:T(8,128)(2,1)S(1)}, u32[]{:S(2)}, u32[]{:S(2)}) collective-permute-start(bf16[512,512]{1,0:T(8,128)(2,1)S(1)} %constant_dynamic-update-slice_fusion.near0), channel_id=1, source_target_pairs={{0,1},{1,0},{2,3},{3,2},{4,5},{5,4},{6,7},{7,6},{8,9},{9,8},{10,11... | collective-permute-start | bytes 1572872 | tf_op jit(solution)/shard_map/ppermute | solution.py:111
  126.3 5.0 %collective-permute-start.22 = (bf16[128,512]{1,0:T(8,128)(2,1)S(1)}, bf16[128,512]{1,0:T(8,128)(2,1)S(1)}, u32[]{:S(2)}, u32[]{:S(2)}) collective-permute-start(bf16[128,512]{1,0:T(8,128)(2,1)S(1)} %pad_maximum_fusion.3), channel_id=1, source_target_pairs={{0,2},{1,3},{2,0},{3,1},{4,6},{5,7},{6,4},{7,5},{8,10},{9,11},{10,... | collective-permute-start | bytes 393224 | tf_op jit(solution)/shard_map/ppermute | solution.py:111
  131.4 1.6 %collective-permute-start.23 = (bf16[256,512]{1,0:T(8,128)(2,1)S(1)}, bf16[256,512]{1,0:T(8,128)(2,1)S(1)}, u32[]{:S(2)}, u32[]{:S(2)}) collective-permute-start(bf16[256,512]{1,0:T(8,128)(2,1)S(1)} %pad_maximum_fusion.1.near1), channel_id=1, source_target_pairs={{0,1},{1,0},{2,3},{3,2},{4,5},{5,4},{6,7},{7,6},{8,9},{9,8},{10,11... | collective-permute-start | bytes 786440 | tf_op jit(solution)/shard_map/ppermute | solution.py:111
  134.3 14.0 %collective-permute-start.24 = (bf16[512,512]{1,0:T(8,128)(2,1)S(1)}, bf16[512,512]{1,0:T(8,128)(2,1)S(1)}, u32[]{:S(2)}, u32[]{:S(2)}) collective-permute-start(bf16[512,512]{1,0:T(8,128)(2,1)S(1)} %shard_map.51), channel_id=1, source_target_pairs={{0,16},{16,0},{1,17},{17,1},{2,18},{18,2},{3,19},{19,3},{4,20},{20... | collective-permute-start | bytes 1572872 | tf_op jit(solution)/shard_map/ppermute | solution.py:111

commit v3 on v0

v3 whole, which is shorter than its diff:
```python
import functools

import jax
import jax.numpy as jnp
from jax import lax
from jax.experimental import pallas as pl
from jax.experimental.pallas import tpu as pltpu
from jax.sharding import PartitionSpec as P

CAP = 4
WIRE = jnp.bfloat16
HELPS, FOREIGN, PLACE, COUNTS, LOW, PARTNER = 0, 1, 2, 3, 6, 7
MEBI = 1024 * 1024
SMEM_SPEC = pl.BlockSpec(memory_space=pltpu.SMEM)
HBM_SPEC = pl.BlockSpec(memory_space=pltpu.HBM)
VMEM_SPEC = pl.BlockSpec(memory_space=pltpu.VMEM)


def general(factors, occ_energy, virt_energy, tile_table):
    owned = factors.shape[0]
    width = factors.shape[2]
    tiles = tile_table.shape[0]
    groups = lax.axis_size("orb")
    mine = lax.axis_index("orb")
    first = tile_table[:, 0]
    second = tile_table[:, 1]
    helper = tile_table[:, 2]
    block_ids = jnp.arange(owned * groups, dtype=jnp.int32)
    group_ids = jnp.arange(groups, dtype=jnp.int32)
    local_ids = jnp.arange(owned, dtype=jnp.int32)
    touched = (
        (first[:, None] == block_ids[None, :]) | (second[:, None] == block_ids[None, :])
    ).astype(jnp.int32)
    helped = (helper[:, None] == group_ids[None, :]).astype(jnp.int32)
    usage = jnp.sum(helped[:, :, None] * touched[:, None, :], axis=0) > 0
    usage = usage.reshape(groups, groups, owned).astype(jnp.int32)
    own_usage = jnp.take(usage, mine, axis=1)
    send_pick = jnp.sum(own_usage * local_ids[None, :], axis=1)
    outgoing = jnp.stack(
        [
            lax.dynamic_index_in_dim(factors, send_pick[group], 0, keepdims=False)
            for group in range(groups)
        ]
    )
    incoming = lax.all_to_all(outgoing, "orb", split_axis=0, concat_axis=0, tiled=True)
    store = jnp.concatenate([factors, incoming], axis=0)

    def position(block):
        owner = block // owned
        return jnp.where(owner == mine, block % owned, owned + owner)

    is_mine = (helper == mine).astype(jnp.int32)
    tile_ids = jnp.arange(tiles, dtype=jnp.int32)
    earlier = (tile_ids[None, :] < tile_ids[:, None]).astype(jnp.int32)
    rank = jnp.sum(earlier * is_mine[None, :], axis=1)
    slot_ids = jnp.arange(CAP, dtype=jnp.int32)
    picked = is_mine[None, :] * (rank[None, :] == slot_ids[:, None]).astype(jnp.int32)
    valid = jnp.sum(picked, axis=1)
    tile_p = jnp.sum(picked * first[None, :], axis=1)
    tile_q = jnp.sum(picked * second[None, :], axis=1)
    place_p = position(tile_p)
    place_q = position(tile_q)
    energy_p = jnp.take(virt_energy, tile_p, axis=0)
    energy_q = jnp.take(virt_energy, tile_q, axis=0)
    occ_sum = jnp.take(occ_energy, tile_p) + jnp.take(occ_energy, tile_q)
    denominators = energy_p[:, :, None] + energy_q[:, None, :] - occ_sum[:, None, None]

    def partners(slot):
        block_p = lax.dynamic_index_in_dim(store, place_p[slot], 0, keepdims=False)
        block_q = lax.dynamic_index_in_dim(store, place_q[slot], 0, keepdims=False)
        return (block_p, block_q)

    def fill(slot, buffer):
        block_p, block_q = partners(slot)
        return lax.dynamic_update_index_in_dim(buffer, outer(block_p, block_q), slot, 0)

    buffer = lax.fori_loop(0, CAP, fill, jnp.zeros((CAP, width, width), jnp.float32))
    summed = lax.psum(buffer, "aux")
    all_amps = (summed / denominators).astype(jnp.bfloat16)

    def apply_all(slot, gathered):
        block_p, block_q = partners(slot)
        amplitudes = lax.dynamic_index_in_dim(all_amps, slot, 0, keepdims=False)
        amplitudes = jnp.where(valid[slot] > 0, amplitudes, jnp.zeros_like(amplitudes))
        gathered = gathered.at[place_p[slot]].add(right_t(block_q, amplitudes))
        return gathered.at[place_q[slot]].add(right(block_p, amplitudes))

    gathered = lax.fori_loop(0, CAP, apply_all, jnp.zeros(store.shape, jnp.float32))
    helper_part = gathered[owned:].astype(jnp.bfloat16)
    returned = lax.all_to_all(helper_part, "orb", split_axis=0, concat_axis=0, tiled=True)
    landing = (send_pick[:, None] == local_ids[None, :]).astype(jnp.float32)
    gamma = gathered[:owned] + jnp.einsum(
        "dj,dav->jav", landing, returned.astype(jnp.float32), precision=lax.Precision.HIGHEST
    )
    return gamma.astype(jnp.bfloat16)


def outer(a, b):
    return lax.dot_general(a, b, (((0,), (0,)), ((), ())), preferred_element_type=jnp.float32)


def right(a, m):
    return jnp.dot(a, m, preferred_element_type=jnp.float32)


def right_t(a, m):
    return lax.dot_general(a, m, (((1,), (1,)), ((), ())), preferred_element_type=jnp.float32)


def swap(value, axis, bit):
    size = lax.axis_size(axis)
    return lax.ppermute(value, axis, [(i, i ^ (1 << bit)) for i in range(size)])


def halve(kept, sent, axis, wires):
    me = lax.axis_index(axis)
    part = kept + swap(sent, axis, 0).astype(jnp.float32)
    for bit, wire in list(enumerate(wires))[1:]:
        high = ((me >> bit) & 1) == 1
        half = part.shape[1] // 2
        low_rows, high_rows = part[:, :half], part[:, half:]
        sent = jnp.where(high, low_rows, high_rows).astype(wire)
        kept = jnp.where(high, high_rows, low_rows)
        part = kept + swap(sent, axis, bit).astype(jnp.float32)
    return part


def double(part, axis, bits):
    part = part[None]
    for bit in reversed(range(1, bits)):
        part = jnp.concatenate([part, swap(part, axis, bit)], axis=0)
    return part, swap(part, axis, 0)


def after(value, *others):
    return lax.optimization_barrier((value, *others))[0]


def start_all(copies):
    for copy in copies:
        copy.start()


def wait_all(copies):
    for copy in copies:
        copy.wait()


def rows_at(unit, start, size):
    return pl.ds(pl.multiple_of(start * unit, unit), size * unit)


def plan_kernel(tiles, bits, step, table, factors, plan, pay, sems):
    helper = table[0, 2]
    helps = (lax.axis_index("orb") == helper).astype(jnp.int32)
    low, foreign_low = helper * 2, (1 - helper) * 2
    foreign = jnp.int32(0)
    for t in range(tiles):
        named = (table[t, 0] == foreign_low + 1) | (table[t, 1] == foreign_low + 1)
        foreign = foreign | named.astype(jnp.int32)
    b0, b1 = jnp.where(helps == 1, 0, foreign), jnp.where(helps == 1, 1, foreign)
    copies = [
        pltpu.make_async_copy(
            factors.at[b0, rows_at(step, 2 * helps, 2)], pay.at[pl.ds(0, 2 * step)], sems.at[0]
        ),
        pltpu.make_async_copy(
            factors.at[b1, rows_at(step, 2 + helps, 1)], pay.at[pl.ds(2 * step, step)], sems.at[1]
        ),
    ]
    start_all(copies)
    me = lax.axis_index("aux")
    place = jnp.int32(0)
    for bit in range(bits):
        place = place * 2 + ((me >> bit) & 1)
    plan[HELPS], plan[FOREIGN], plan[PLACE] = helps, foreign, place
    plan[LOW], plan[PARTNER] = low, foreign_low + foreign
    pairs = ((low, low + 1), (low, foreign_low + foreign), (low + 1, foreign_low + foreign))
    for n, (a, b) in enumerate(pairs):
        count = jnp.int32(0)
        for t in range(tiles):
            p, q = table[t, 0], table[t, 1]
            same = ((p == a) & (q == b)) | ((p == b) & (q == a))
            count = count + same.astype(jnp.int32)
        plan[COUNTS + n] = count
    wait_all(copies)


def weigh_kernel(step, plan, occ, virt, factors, own_weight, weights, pay_a, sem):
    helps = plan[HELPS]
    block = jnp.where(helps == 1, 1, plan[FOREIGN])
    copy = pltpu.make_async_copy(factors.at[block, rows_at(step, 3 - helps, 1)], pay_a, sem)
    copy.start()
    low, partner = plan[LOW], plan[PARTNER]
    _, shard, width = own_weight.shape
    row = lax.broadcasted_iota(jnp.int32, (shard, width), 0)
    column = lax.broadcasted_iota(jnp.int32, (shard, width), 1)
    mine = column == row + plan[PLACE] * shard
    pairs = ((low, low + 1, own_weight, 0), (low, partner, weights, 0), (low + 1, partner, weights, 1))
    for n, (a, b, out, slot) in enumerate(pairs):
        virt_a = jnp.sum(jnp.where(mine, virt[pl.ds(a, 1), :], 0.0), axis=1, keepdims=True)
        denominators = virt_a + virt[pl.ds(b, 1), :] - occ[a] - occ[b]
        out[slot] = plan[COUNTS + n].astype(jnp.float32) / denominators
    copy.wait()


def pack_kernel(step, plan, factors, pay_b, sems):
    helps, foreign = plan[HELPS], plan[FOREIGN]
    blocks = (jnp.where(helps == 1, 0, foreign), jnp.where(helps == 1, 1, foreign))
    copies = [
        pltpu.make_async_copy(
            factors.at[block, pl.ds(step, step)], pay_b.at[pl.ds(n * step, step)], sems.at[n]
        )
        for n, block in enumerate(blocks)
    ]
    start_all(copies)
    wait_all(copies)


def split_halves(acc, pair, kept, sent, core):
    half = kept.shape[1]
    kept[pair] = acc[pl.ds(pl.multiple_of(core * half, half), half), :]
    other = acc[pl.ds(pl.multiple_of((1 - core) * half, half), half), :]
    sent[pair] = other.astype(sent.dtype)


def own_kernel(step, plan, factors, kept, sent, rows, acc, sems):
    del plan
    copies = [
        pltpu.make_async_copy(
            factors.at[:, pl.ds(n * step, step)], rows.at[:, pl.ds(n * step, step)], sems.at[n]
        )
        for n in range(4)
    ]
    start_all(copies)
    for n in range(4):
        copies[n].wait()
        term = outer(rows[0, n * step : (n + 1) * step], rows[1, n * step : (n + 1) * step])
        acc[...] = term if n == 0 else acc[...] + term
    split_halves(acc, 0, kept, sent, lax.axis_index("aux") & 1)


def pair_kernel(step, plan, factors, got, kept, sent, rows0, rows1, acc0, acc1, sems):
    helps, foreign = plan[HELPS], plan[FOREIGN]
    b0, b1 = jnp.where(helps == 1, 0, foreign), jnp.where(helps == 1, 1, foreign)
    copies0 = [
        pltpu.make_async_copy(
            factors.at[b0, rows_at(step, jnp.where(helps == 1, n, 2 + n), 1)],
            rows0.at[pl.ds(n * step, step)],
            sems.at[n],
        )
        for n in range(2)
    ]
    copies1 = [
        pltpu.make_async_copy(
            factors.at[b1, rows_at(step, jnp.where(helps == 1, n, 3), 1)],
            rows1.at[pl.ds(n * step, step)],
            sems.at[2 + n],
        )
        for n in range(3)
    ]
    start_all(copies0 + copies1)

    def cut(ref, n):
        return ref[n * step : (n + 1) * step]

    copies0[0].wait()

    @pl.when(helps == 1)
    def _():
        acc0[...] = outer(cut(rows0, 0), cut(got, 0))

    @pl.when(helps == 0)
    def _():
        acc0[...] = outer(cut(got, 0), cut(rows0, 0))

    copies0[1].wait()

    @pl.when(helps == 1)
    def _():
        acc0[...] += outer(cut(rows0, 1), cut(got, 1))

    @pl.when(helps == 0)
    def _():
        acc0[...] += outer(cut(got, 1), cut(rows0, 1))

    wait_all(copies1)

    @pl.when(helps == 1)
    def _():
        acc1[...] = outer(cut(rows1, 0), cut(got, 0)) + outer(cut(rows1, 1), cut(got, 1))
        acc1[...] += outer(cut(rows1, 2), cut(got, 2))

    @pl.when(helps == 0)
    def _():
        acc1[...] = outer(cut(got, 2), cut(rows1, 2))

    core = lax.axis_index("aux") & 1
    split_halves(acc0, 0, kept, sent, core)
    split_halves(acc1, 1, kept, sent, core)


def arrange(plan, near, far, pair, out):
    count, _, shard, _ = near.shape
    for source, base in ((near, 0), (far, count)):
        for n in range(count):
            row = pl.multiple_of((plan[PLACE] ^ (base + n)) * shard, shard)
            out[pl.ds(row, shard), :] = source[n, pair]


def back_kernel(plan, near, far, blocks, back, amp0, amp1):
    arrange(plan, near, far, 0, amp0)
    arrange(plan, near, far, 1, amp1)
    total = right(blocks[0], amp0[...]) + right(blocks[1], amp1[...])
    back[...] = total.astype(back.dtype)


def last_kernel(plan, near01, far01, near, far, x, a, y, blocks, out, own, amp0, amp1):
    seg = pl.program_id(0)
    helps = plan[HELPS] == 1

    @pl.when(seg == 0)
    def _():
        arrange(plan, near01, far01, 0, own)
        arrange(plan, near, far, 0, amp0)
        arrange(plan, near, far, 1, amp1)

    @pl.when(helps)
    def _():
        foreign = jnp.where(seg < 3, x[...], a[...])
        out[0] = (right_t(blocks[1], own[...]) + right_t(foreign, amp0[...])).astype(out.dtype)
        out[1] = (right(blocks[0], own[...]) + right_t(foreign, amp1[...])).astype(out.dtype)

    @pl.when(jnp.logical_not(helps))
    def _():
        out[...] = jnp.zeros_like(out)

    @pl.when(jnp.logical_not(helps) & (seg >= 2))
    def _():
        rows1 = jnp.where(seg < 3, a[...], y[...])
        total = right(x[...], amp0[...]) + right(rows1, amp1[...])
        out[plan[FOREIGN]] = total.astype(out.dtype)


def late_kernel(step, plan, near, far, got, gamma_in, gamma, amp0, amp1, rows, sem):
    @pl.when(plan[HELPS] == 0)
    def _():
        arrange(plan, near, far, 0, amp0)
        arrange(plan, near, far, 1, amp1)
        total = right(got[:step], amp0[...]) + right(got[step:], amp1[...])
        rows[...] = total.astype(rows.dtype)
        copy = pltpu.make_async_copy(rows, gamma.at[plan[FOREIGN], pl.ds(step, step)], sem)
        copy.start()
        copy.wait()


def put_kernel(step, plan, back, gamma_in, gamma, sem):
    @pl.when(plan[HELPS] == 0)
    def _():
        copy = pltpu.make_async_copy(back, gamma.at[plan[FOREIGN], pl.ds(0, step)], sem)
        copy.start()
        copy.wait()


def two_groups(factors, occ_energy, virt_energy, tile_table):
    owned, rows, width = factors.shape
    aux = lax.axis_size("aux")
    bits = aux.bit_length() - 1
    step = rows // 4
    shard = width // aux
    wires = [jnp.float32] + [WIRE] * (bits - 1)
    dtype = factors.dtype
    dma = pltpu.SemaphoreType.DMA

    def array(*shape, dtype=dtype):
        return jax.ShapeDtypeStruct(shape, dtype)

    def call(kernel, out_shape, in_specs, out_specs, scratch, cost=0, mebi=16, **options):
        return pl.pallas_call(
            kernel,
            out_shape=out_shape,
            in_specs=in_specs,
            out_specs=out_specs,
            scratch_shapes=scratch,
            compiler_params=pltpu.CompilerParams(vmem_limit_bytes=mebi * MEBI),
            cost_estimate=pl.CostEstimate(
                flops=cost * 2 * step * width * width,
                bytes_accessed=2 * step * width * 2,
                transcendentals=0,
            ),
            **options,
        )

    plan, pay1 = call(
        functools.partial(plan_kernel, tile_table.shape[0], bits, step),
        (array(8, dtype=jnp.int32), array(3 * step, width)),
        [SMEM_SPEC, HBM_SPEC],
        (SMEM_SPEC, VMEM_SPEC),
        [dma((2,))],
        mebi=61,
    )(tile_table, factors)
    got1 = swap(pay1, "orb", 0)

    def halves(pairs):
        kept = array(pairs, width // 2, width, dtype=jnp.float32)
        return kept, array(pairs, width // 2, width, dtype=wires[0])

    square = pltpu.VMEM((width, width), jnp.float32)

    own_weight, weights, pay_a = call(
        functools.partial(weigh_kernel, step),
        (
            array(1, shard, width, dtype=jnp.float32),
            array(2, shard, width, dtype=jnp.float32),
            array(step, width),
        ),
        [SMEM_SPEC, SMEM_SPEC, VMEM_SPEC, HBM_SPEC],
        (VMEM_SPEC, VMEM_SPEC, VMEM_SPEC),
        [dma],
    )(plan, occ_energy, virt_energy, factors)

    def own_chain():
        kept, sent = call(
            functools.partial(own_kernel, step),
            halves(1),
            [SMEM_SPEC, HBM_SPEC],
            (VMEM_SPEC, VMEM_SPEC),
            [pltpu.VMEM(factors.shape, dtype), square, dma((4,))],
            4,
        )(plan, factors)
        sum01 = halve(kept, sent, "aux", wires)
        return double((sum01 * own_weight).astype(dtype), "aux", bits)

    def no_chain():
        half = jnp.zeros((aux // 2, 1, shard, width), dtype)
        return half, half

    near01, far01 = lax.cond(plan[COUNTS] > 0, own_chain, no_chain)

    got1, near01, far01, weights, pay_a = lax.optimization_barrier(
        (got1, near01, far01, weights, pay_a)
    )
    got_a = swap(pay_a, "orb", 0)

    kept, sent = call(
        functools.partial(pair_kernel, step),
        halves(2),
        [SMEM_SPEC, HBM_SPEC, VMEM_SPEC],
        (VMEM_SPEC, VMEM_SPEC),
        [
            pltpu.VMEM((2 * step, width), dtype),
            pltpu.VMEM((3 * step, width), dtype),
            square,
            square,
            dma((5,)),
        ],
        5,
    )(plan, factors, got1)
    used = plan[COUNTS + 1] + plan[COUNTS + 2] > 0
    sums = lax.cond(
        used,
        lambda: halve(kept, sent, "aux", wires),
        lambda: jnp.zeros((2, shard, width), jnp.float32),
    )
    pay_b = call(
        functools.partial(pack_kernel, step),
        array(2 * step, width),
        [SMEM_SPEC, HBM_SPEC],
        VMEM_SPEC,
        [dma((2,))],
    )(after(plan, kept), factors)
    sums, got_a, pay_b = lax.optimization_barrier((sums, got_a, pay_b))
    sums = sums + swap(sums, "orb", 0)
    shards0, pay_b = lax.optimization_barrier(((sums * weights).astype(dtype), pay_b))
    got_b = swap(pay_b, "orb", 0)

    def gather():
        return double(shards0, "aux", bits)

    def nothing():
        half = jnp.zeros((aux // 2, 2, shard, width), dtype)
        return half, half

    near, far = lax.cond(used, gather, nothing)

    def whole(shape):
        return pl.BlockSpec(shape, lambda i, plan: (0,) * len(shape))

    def run(kernel, steps, specs, out_shape, out_specs, scratch, cost, mebi=16):
        return pl.pallas_call(
            kernel,
            out_shape=out_shape,
            grid_spec=pltpu.PrefetchScalarGridSpec(
                num_scalar_prefetch=1,
                grid=(steps,),
                in_specs=specs,
                out_specs=out_specs,
                scratch_shapes=scratch,
            ),
            compiler_params=pltpu.CompilerParams(vmem_limit_bytes=mebi * MEBI),
            cost_estimate=pl.CostEstimate(
                flops=cost * 2 * step * width * width,
                bytes_accessed=cost * step * width * 2,
                transcendentals=0,
            ),
        )

    amp = pltpu.VMEM((width, width), dtype)
    back = run(
        back_kernel,
        1,
        [
            whole(near.shape),
            whole(far.shape),
            pl.BlockSpec((2, step, width), lambda i, plan: (0, 0, 0)),
        ],
        array(step, width),
        whole((step, width)),
        [amp, amp],
        1,
    )(plan, near, far, factors)
    got_back = swap(back, "orb", 0)

    def at(helper_block, owner_block):
        return pl.BlockSpec(
            (step, width),
            lambda i, plan: (
                jnp.where(plan[HELPS] == 1, helper_block(i), owner_block(i)),
                0,
            ),
        )

    def clip(low, high, shift):
        return lambda i: jnp.clip(i + shift, low, high)

    none = clip(0, 0, 0)
    pieces = pl.BlockSpec((2, step, width), lambda i, plan: (0, i, 0))
    gamma = run(
        last_kernel,
        4,
        [whole(near01.shape), whole(far01.shape), whole(near.shape), whole(far.shape)]
        + [at(clip(0, 2, 0), clip(0, 1, -2)), at(none, none), at(none, clip(2, 2, 0)), pieces],
        array(*factors.shape),
        pieces,
        [amp, amp, amp],
        12,
    )(plan, near01, far01, near, far, got1, got_a, got1, factors)

    gamma = call(
        functools.partial(late_kernel, step),
        array(*factors.shape),
        [SMEM_SPEC, VMEM_SPEC, VMEM_SPEC, VMEM_SPEC, HBM_SPEC],
        HBM_SPEC,
        [amp, amp, pltpu.VMEM((step, width), dtype), dma],
        1,
        input_output_aliases={4: 0},
    )(plan, near, far, got_b, gamma)
    return call(
        functools.partial(put_kernel, step),
        array(*factors.shape),
        [SMEM_SPEC, VMEM_SPEC, HBM_SPEC],
        HBM_SPEC,
        [dma],
        input_output_aliases={2: 0},
    )(plan, got_back, gamma)


def shards(factors, occ_energy, virt_energy, tile_table):
    groups = lax.axis_size("orb")
    aux = lax.axis_size("aux")
    simple = groups == 2 and factors.shape[0] == 2 and tile_table.shape[0] <= CAP
    width = factors.shape[2]
    whole_shards = aux & (aux - 1) == 0 and width % (32 * aux) == 0
    if simple and whole_shards and factors.shape[1] % 128 == 0:
        return two_groups(factors, occ_energy, virt_energy, tile_table)
    return general(factors, occ_energy, virt_energy, tile_table)


def solution(mesh):
    return jax.shard_map(
        shards,
        mesh=mesh,
        in_specs=(P("orb", "aux", None), P(), P(), P()),
        out_specs=P("orb", "aux", None),
        check_vma=False,
    )
```

time: 410 us -> 129 us (0.31)
  waiting for transfers between devices: 179 us -> 58.2 us
  matrix products: 89.5 us -> 0 us
  local copies, waits for them, and re-layouts: 72.4 us -> 2.41 us
  loops' own time: 32.9 us -> 0.19 us
  Pallas kernels: 0 us -> 26.7 us
  starting transfers between devices: 11.6 us -> 32.4 us
  between operations: 13.5 us -> 2.21 us
    psum x1 -> x0, waiting for transfers between devices: 109 us -> none  [shards(): summed = lax.psum(buffer, 'aux')]
    dot_general x13 -> x0, matrix products: 89.5 us -> none  [the longest x4 26.6 us: spread(): lax.dot_general(block_q, amplitudes, (((1,), (1,)), ((), ())), preferred_...]
    all_to_all x2 -> x0, waiting for transfers between devices: 69.5 us -> none  [the longest x1 44 us: shards(): lax.all_to_all(outgoing, 'orb', split_axis=0, concat_axis=0, tiled=True)]
    ppermute x0 -> x21, waiting for transfers between devices: none -> 58.2 us  [swap(): return lax.ppermute(value, axis, [(i, i ^ 1 << bit) for i in range(size)])]
    another operation x2 -> x3, loops' own time: 32.9 us -> 0.19 us  [the longest x1 0.09 us: two_groups(): near01, far01 = lax.cond(plan[COUNTS] > 0, own_chain, no_chain)]
    ppermute x0 -> x21, starting transfers between devices: none -> 32.4 us  [swap(): return lax.ppermute(value, axis, [(i, i ^ 1 << bit) for i in range(size)])]
    pallas_call x0 -> x9, Pallas kernels: none -> 26.7 us  [the longest x1 5.82 us: two_groups(): run(last_kernel, 4, [whole(near01.shape), whole(far01.shape), whole(near....]
    while x1 -> x0, local copies, waits for them, and re-layouts: 20.9 us -> none  [shards(): gathered = lax.fori_loop(0, CAP, apply_all, gathered)]
  transfers between devices with their start and end apart: 3 -> 21, of which waited for: 3 -> 18; matrix products, arithmetic and copies ran while one was open for 7% -> 6% of each run, Pallas kernels for 0% -> 17%
where the time goes in v3:
time: 129 us
  waiting for transfers between devices  58.2 us (45%)
  starting transfers between devices  32.4 us (25%)
  Pallas kernels  26.7 us (21%)
  other arithmetic  6.85 us (5%)
  local copies, waits for them, and re-layouts  2.41 us (2%)
  between operations  2.21 us (2%)
    ppermute x21, waiting for transfers between devices, swap(): return lax.ppermute(value, axis, [(i, i ^ 1 << bit) for i in range(size)])  58.2 us
    ppermute x21, starting transfers between devices, swap(): return lax.ppermute(value, axis, [(i, i ^ 1 << bit) for i in range(size)])  32.4 us
    pallas_call x1, Pallas kernels, two_groups(): run(last_kernel, 4, [whole(near01.shape), whole(far01.shape), whole(near....  5.82 us
    pallas_call x1, Pallas kernels, two_groups(): call(functools.partial(pair_kernel, step), halves(2), [SMEM_SPEC, HBM_SPE...  4.49 us
    pallas_call x1, Pallas kernels, two_groups(): call(functools.partial(plan_kernel, tile_table.shape[0], bits, step), (ar...  3.37 us
    pallas_call x1, Pallas kernels, two_groups(): call(functools.partial(late_kernel, step), array(*factors.shape), [SMEM_S...  3.11 us
    pallas_call x1, Pallas kernels, two_groups(): run(back_kernel, 1, [whole(near.shape), whole(far.shape), pl.BlockSpec((2...  3.08 us
  transfers between devices with their start and end apart: 21, of which 18 were waited for; matrix products, arithmetic and copies ran while one was open for 6% of the time, Pallas kernels for 17%

profile of v3, /device:TPU:0, one launch (start us, length us, event | category | flops | bytes accessed | tf_op | source)
XLA Modules:
  0.0 129.0 jit_solution(17502376963474222602)
XLA Ops:
  0.0 3.4 %shard_map.46 = (s32[8]{0:T(128)S(1)}, bf16[1536,512]{1,0:T(8,128)(2,1)}) custom-call(s32[4,3]{1,0:T(4,128)} %table.1, bf16[2,2048,512]{2,1,0:T(8,128)(2,1)} %blocks.3), custom_call_target="tpu_custom_call" | custom-call | bytes 1048576 | tf_op jit(solution)/shard_map/pallas_call | solution.py:393
  3.4 3.0 %collective-permute-start.16 = (bf16[1536,512]{1,0:T(8,128)(2,1)}, bf16[1536,512]{1,0:T(8,128)(2,1)S(1)}, u32[]{:S(2)}, u32[]{:S(2)}) collective-permute-start(bf16[1536,512]{1,0:T(8,128)(2,1)} %get-tuple-element.49), channel_id=1, source_target_pairs={{0,16},{16,0},{1,17},{17,1},{2,18},{18,2},{3,19},{19,3},{4,20},{20... | collective-permute-start | bytes 4718600 | tf_op jit(solution)/shard_map/ppermute | solution.py:112
  6.4 2.4 %shard_map.47 = (f32[1,32,512]{2,1,0:T(8,128)S(1)}, f32[2,32,512]{2,1,0:T(8,128)S(1)}, bf16[512,512]{1,0:T(8,128)(2,1)}) custom-call(s32[8]{0:T(128)S(1)} %get-tuple-element.59.plan, f32[4]{0:T(128)S(1)} %copy-done.1, f32[4,512]{1,0:T(4,128)S(1)} %copy-done, bf16[2,2048,512]{2,1,0:T(8,128)(2,1)} %blocks.3), custom_call_target="tpu_custom_call" | custom-call | bytes 1048576 | tf_op jit(solution)/shard_map/pallas_call | solution.py:409
  10.1 36.4 %conditional.3 = (bf16[8,1,32,512]{3,2,1,0:T(8,128)(2,1)}, bf16[8,1,32,512]{3,2,1,0:T(8,128)(2,1)}) conditional(s32[]{:T(128)} %bitcast.3, () %tuple.33, (s32[8]{0:T(128)S(1)}, bf16[2,2048,512]{2,1,0:T(8,128)(2,1)S(1)}, f32[1,32,512]{2,1,0:T(8,128)S(1)}) %tuple.48), branch_computations={%region_0.0_spmd, %region_1.2_spmd} | conditional | flops 1074921472 | bytes 10846669 | solution.py:437
  10.1 2.5 %branch_1_fun.1 = (f32[1,256,512]{2,1,0:T(8,128)S(1)}, f32[1,256,512]{2,1,0:T(8,128)S(1)}) custom-call(s32[8]{0:T(128)S(1)} %get-tuple-element.19.plan, bf16[2,2048,512]{2,1,0:T(8,128)(2,1)S(1)} %get-tuple-element.20.factors), custom_call_target="tpu_custom_call" | custom-call | flops 1073741824 | bytes 1048576 | tf_op jit(solution)/shard_map/cond/branch_1_fun/pallas_call | solution.py:422
  16.3 4.0 %collective-permute-done.1 = bf16[1,128,512]{2,1,0:T(8,128)(2,1)S(1)} collective-permute-done((bf16[1,128,512]{2,1,0:T(8,128)(2,1)S(1)}, bf16[1,128,512]{2,1,0:T(8,128)(2,1)S(1)}, u32[]{:S(2)}, u32[]{:S(2)}) %collective-permute-start.1) | collective-permute-done | bytes 131104 | tf_op jit(solution)/shard_map/cond/branch_1_fun/ppermute | solution.py:112
  22.0 2.7 %collective-permute-done.2 = bf16[1,64,512]{2,1,0:T(8,128)(2,1)S(1)} collective-permute-done((bf16[1,64,512]{2,1,0:T(8,128)(2,1)S(1)}, bf16[1,64,512]{2,1,0:T(8,128)(2,1)S(1)}, u32[]{:S(2)}, u32[]{:S(2)}) %collective-permute-start.2) | collective-permute-done | bytes 65568 | tf_op jit(solution)/shard_map/cond/branch_1_fun/ppermute | solution.py:112
  24.8 2.7 %collective-permute-start.3 = (bf16[1,32,512]{2,1,0:T(8,128)(2,1)S(1)}, bf16[1,32,512]{2,1,0:T(8,128)(2,1)S(1)}, u32[]{:S(2)}, u32[]{:S(2)}) collective-permute-start(bf16[1,32,512]{2,1,0:T(8,128)(2,1)S(1)} %select_convert_fusion.2), channel_id=1, source_target_pairs={{0,8},{1,9},{2,10},{3,11},{4,12},{5,13},{6,14},{7,15},{8,0},{9,1},... | collective-permute-start | bytes 98312 | tf_op jit(solution)/shard_map/cond/branch_1_fun/ppermute | solution.py:112
  27.4 2.2 %collective-permute-done.3 = bf16[1,32,512]{2,1,0:T(8,128)(2,1)S(1)} collective-permute-done((bf16[1,32,512]{2,1,0:T(8,128)(2,1)S(1)}, bf16[1,32,512]{2,1,0:T(8,128)(2,1)S(1)}, u32[]{:S(2)}, u32[]{:S(2)}) %collective-permute-start.3) | collective-permute-done | bytes 32800 | tf_op jit(solution)/shard_map/cond/branch_1_fun/ppermute | solution.py:112
  29.7 2.7 %collective-permute-start.4 = (bf16[1,1,32,512]{3,2,1,0:T(8,128)(2,1)S(1)}, bf16[1,1,32,512]{3,2,1,0:T(8,128)(2,1)S(1)}, u32[]{:S(2)}, u32[]{:S(2)}) collective-permute-start(bf16[1,1,32,512]{3,2,1,0:T(8,128)(2,1)S(1)} %fusion), channel_id=1, source_target_pairs={{0,8},{1,9},{2,10},{3,11},{4,12},{5,13},{6,14},{7,15},{8,0},{9,1},... | collective-permute-start | bytes 98312 | tf_op jit(solution)/shard_map/cond/branch_1_fun/ppermute | solution.py:112
  32.4 2.2 %collective-permute-done.4 = bf16[1,1,32,512]{3,2,1,0:T(8,128)(2,1)S(1)} collective-permute-done((bf16[1,1,32,512]{3,2,1,0:T(8,128)(2,1)S(1)}, bf16[1,1,32,512]{3,2,1,0:T(8,128)(2,1)S(1)}, u32[]{:S(2)}, u32[]{:S(2)}) %collective-permute-start.4) | collective-permute-done | bytes 32800 | tf_op jit(solution)/shard_map/cond/branch_1_fun/ppermute | solution.py:112
  36.3 2.6 %collective-permute-done.5 = bf16[2,1,32,512]{3,2,1,0:T(8,128)(2,1)S(1)} collective-permute-done((bf16[2,1,32,512]{3,2,1,0:T(8,128)(2,1)S(1)}, bf16[2,1,32,512]{3,2,1,0:T(8,128)(2,1)S(1)}, u32[]{:S(2)}, u32[]{:S(2)}) %collective-permute-start.5) | collective-permute-done | bytes 65568 | tf_op jit(solution)/shard_map/cond/branch_1_fun/ppermute | solution.py:112
  40.5 3.5 %collective-permute-done.6 = bf16[4,1,32,512]{3,2,1,0:T(8,128)(2,1)S(1)} collective-permute-done((bf16[4,1,32,512]{3,2,1,0:T(8,128)(2,1)S(1)}, bf16[4,1,32,512]{3,2,1,0:T(8,128)(2,1)S(1)}, u32[]{:S(2)}, u32[]{:S(2)}) %collective-permute-start.6) | collective-permute-done | bytes 131104 | tf_op jit(solution)/shard_map/cond/branch_1_fun/ppermute | solution.py:112
  48.5 4.5 %shard_map.48 = (f32[2,256,512]{2,1,0:T(8,128)}, f32[2,256,512]{2,1,0:T(8,128)}) custom-call(s32[8]{0:T(128)S(1)} %get-tuple-element.59.plan, bf16[2,2048,512]{2,1,0:T(8,128)(2,1)} %blocks.3, bf16[1536,512]{1,0:T(8,128)(2,1)S(1)} %collective-permute-done.16.got.x.y), custom_call_target="tpu_custom_call" | custom-call | flops 1342177280 | bytes 1048576 | tf_op jit(solution)/shard_map/pallas_call | solution.py:444
  53.7 28.7 %conditional.4 = (f32[2,32,512]{2,1,0:T(8,128)S(1)}) conditional(s32[]{:T(128)} %bitcast.2, () %tuple.32, (f32[2,256,512]{2,1,0:T(8,128)}, f32[2,256,512]{2,1,0:T(8,128)}) %tuple.36), branch_computations={%region_2.3_spmd, %region_3.4_spmd} | conditional | flops 1179659 | bytes 20054360 | solution.py:459
  53.8 3.0 %collective-permute-done.8 = f32[2,256,512]{2,1,0:T(8,128)} collective-permute-done((f32[2,256,512]{2,1,0:T(8,128)}, f32[2,256,512]{2,1,0:T(8,128)}, u32[]{:S(2)}, u32[]{:S(2)}) %collective-permute-start.8) | collective-permute-done | bytes 1048608 | tf_op jit(solution)/shard_map/cond/branch_1_fun/ppermute | solution.py:112
  62.0 6.8 %collective-permute-done.9 = bf16[2,128,512]{2,1,0:T(8,128)(2,1)S(1)} collective-permute-done((bf16[2,128,512]{2,1,0:T(8,128)(2,1)}, bf16[2,128,512]{2,1,0:T(8,128)(2,1)S(1)}, u32[]{:S(2)}, u32[]{:S(2)}) %collective-permute-start.9) | collective-permute-done | bytes 262176 | tf_op jit(solution)/shard_map/cond/branch_1_fun/ppermute | solution.py:112
  72.9 3.1 %collective-permute-done.10 = bf16[2,64,512]{2,1,0:T(8,128)(2,1)S(1)} collective-permute-done((bf16[2,64,512]{2,1,0:T(8,128)(2,1)S(1)}, bf16[2,64,512]{2,1,0:T(8,128)(2,1)S(1)}, u32[]{:S(2)}, u32[]{:S(2)}) %collective-permute-start.10) | collective-permute-done | bytes 131104 | tf_op jit(solution)/shard_map/cond/branch_1_fun/ppermute | solution.py:112
  77.1 2.9 %collective-permute-start.11 = (bf16[2,32,512]{2,1,0:T(8,128)(2,1)S(1)}, bf16[2,32,512]{2,1,0:T(8,128)(2,1)S(1)}, u32[]{:S(2)}, u32[]{:S(2)}) collective-permute-start(bf16[2,32,512]{2,1,0:T(8,128)(2,1)S(1)} %select_convert_fusion.5), channel_id=1, source_target_pairs={{0,8},{1,9},{2,10},{3,11},{4,12},{5,13},{6,14},{7,15},{8,0},{9,1},... | collective-permute-start | bytes 196616 | tf_op jit(solution)/shard_map/cond/branch_1_fun/ppermute | solution.py:112
  80.0 2.3 %collective-permute-done.11 = bf16[2,32,512]{2,1,0:T(8,128)(2,1)S(1)} collective-permute-done((bf16[2,32,512]{2,1,0:T(8,128)(2,1)S(1)}, bf16[2,32,512]{2,1,0:T(8,128)(2,1)S(1)}, u32[]{:S(2)}, u32[]{:S(2)}) %collective-permute-start.11) | collective-permute-done | bytes 65568 | tf_op jit(solution)/shard_map/cond/branch_1_fun/ppermute | solution.py:112
  84.3 4.3 %collective-permute-done.18 = f32[2,32,512]{2,1,0:T(8,128)S(1)} collective-permute-done((f32[2,32,512]{2,1,0:T(8,128)S(1)}, f32[2,32,512]{2,1,0:T(8,128)S(1)}, u32[]{:S(2)}, u32[]{:S(2)}) %collective-permute-start.18) | collective-permute-done | bytes 131104 | tf_op jit(solution)/shard_map/ppermute | solution.py:112
  88.6 2.2 %collective-permute-start.20 = (bf16[1024,512]{1,0:T(8,128)(2,1)S(1)}, bf16[1024,512]{1,0:T(8,128)(2,1)}, u32[]{:S(2)}, u32[]{:S(2)}) collective-permute-start(bf16[1024,512]{1,0:T(8,128)(2,1)S(1)} %shard_map.49), channel_id=1, source_target_pairs={{0,16},{16,0},{1,17},{17,1},{2,18},{18,2},{3,19},{19,3},{4,20},{20... | collective-permute-start | bytes 3145736 | tf_op jit(solution)/shard_map/ppermute | solution.py:112
  90.8 19.8 %conditional.5 = (bf16[8,2,32,512]{3,2,1,0:T(8,128)(2,1)}, bf16[8,2,32,512]{3,2,1,0:T(8,128)(2,1)}) conditional(s32[]{:T(128)} %bitcast.2, () %tuple.31, bf16[2,32,512]{2,1,0:T(8,128)(2,1)S(1)} %multiply_convert_fusion.1), branch_computations={%region_4.5_spmd, %region_5.6_spmd} | conditional | flops 1114112 | bytes 5767344 | solution.py:483
  90.8 2.6 %collective-permute-start.12 = (bf16[1,2,32,512]{3,2,1,0:T(8,128)(2,1)S(1)}, bf16[1,2,32,512]{3,2,1,0:T(8,128)(2,1)S(1)}, u32[]{:S(2)}, u32[]{:S(2)}) collective-permute-start(bf16[1,2,32,512]{3,2,1,0:T(8,128)(2,1)S(1)} %bitcast.5), channel_id=1, source_target_pairs={{0,8},{1,9},{2,10},{3,11},{4,12},{5,13},{6,14},{7,15},{8,0},{9,1},... | collective-permute-start | bytes 196616 | tf_op jit(solution)/shard_map/cond/branch_1_fun/ppermute | solution.py:112
  93.3 2.6 %collective-permute-done.12 = bf16[1,2,32,512]{3,2,1,0:T(8,128)(2,1)S(1)} collective-permute-done((bf16[1,2,32,512]{3,2,1,0:T(8,128)(2,1)S(1)}, bf16[1,2,32,512]{3,2,1,0:T(8,128)(2,1)S(1)}, u32[]{:S(2)}, u32[]{:S(2)}) %collective-permute-start.12) | collective-permute-done | bytes 65568 | tf_op jit(solution)/shard_map/cond/branch_1_fun/ppermute | solution.py:112
  97.8 3.2 %collective-permute-done.13 = bf16[2,2,32,512]{3,2,1,0:T(8,128)(2,1)S(1)} collective-permute-done((bf16[2,2,32,512]{3,2,1,0:T(8,128)(2,1)S(1)}, bf16[2,2,32,512]{3,2,1,0:T(8,128)(2,1)S(1)}, u32[]{:S(2)}, u32[]{:S(2)}) %collective-permute-start.13) | collective-permute-done | bytes 131104 | tf_op jit(solution)/shard_map/cond/branch_1_fun/ppermute | solution.py:112
  102.6 4.9 %collective-permute-done.14 = bf16[4,2,32,512]{3,2,1,0:T(8,128)(2,1)S(1)} collective-permute-done((bf16[4,2,32,512]{3,2,1,0:T(8,128)(2,1)S(1)}, bf16[4,2,32,512]{3,2,1,0:T(8,128)(2,1)S(1)}, u32[]{:S(2)}, u32[]{:S(2)}) %collective-permute-start.14) | collective-permute-done | bytes 262176 | tf_op jit(solution)/shard_map/cond/branch_1_fun/ppermute | solution.py:112
  108.3 2.2 %collective-permute-done.15 = bf16[8,2,32,512]{3,2,1,0:T(8,128)(2,1)} collective-permute-done((bf16[8,2,32,512]{3,2,1,0:T(8,128)(2,1)}, bf16[8,2,32,512]{3,2,1,0:T(8,128)(2,1)}, u32[]{:S(2)}, u32[]{:S(2)}) %collective-permute-start.15) | collective-permute-done | bytes 524320 | tf_op jit(solution)/shard_map/cond/branch_1_fun/ppermute | solution.py:112
  110.5 3.1 %shard_map.50 = bf16[512,512]{1,0:T(8,128)(2,1)S(1)} custom-call(s32[8]{0:T(128)S(1)} %get-tuple-element.59.plan, bf16[8,2,32,512]{3,2,1,0:T(8,128)(2,1)} %get-tuple-element.64.near, bf16[8,2,32,512]{3,2,1,0:T(8,128)(2,1)} %get-tuple-element.65.far, bf16[2,2048,512]{2,1,0:T(8,128)(2,1)} %blocks.3), custom_call_target="tpu_custom_call" | custom-call | flops 268435456 | bytes 524288 | tf_op jit(solution)/shard_map/pallas_call | solution.py:508
  113.9 5.8 %shard_map.51.gamma_in = bf16[2,2048,512]{2,1,0:T(8,128)(2,1)} custom-call(s32[8]{0:T(128)S(1)} %get-tuple-element.59.plan, bf16[8,1,32,512]{3,2,1,0:T(8,128)(2,1)} %get-tuple-element.67.near01, bf16[8,1,32,512]{3,2,1,0:T(8,128)(2,1)} %get-tuple-element.68.far01, bf16[8,2,32,512]{3,2,1,0:T(8,128)(2,1)} %get-tuple-element.64.near, ...), custom_call_target="tpu_custom_call" | custom-call | flops 3221225472 | bytes 6291456 | tf_op jit(solution)/shard_map/pallas_call | solution.py:537
  119.7 3.1 %shard_map.52.gamma_in = bf16[2,2048,512]{2,1,0:T(8,128)(2,1)} custom-call(s32[8]{0:T(128)S(1)} %get-tuple-element.59.plan, bf16[8,2,32,512]{3,2,1,0:T(8,128)(2,1)} %get-tuple-element.64.near, bf16[8,2,32,512]{3,2,1,0:T(8,128)(2,1)} %get-tuple-element.65.far, bf16[1024,512]{1,0:T(8,128)(2,1)} %collective-permute-done.20.got, ...), custom_call_target="tpu_custom_call", output_to_operand_aliasing={{}: (4, {})} | custom-call | flops 268435456 | bytes 1048576 | tf_op jit(solution)/shard_map/pallas_call | solution.py:548
  122.8 4.8 %collective-permute-done.19.back = bf16[512,512]{1,0:T(8,128)(2,1)S(1)} collective-permute-done((bf16[512,512]{1,0:T(8,128)(2,1)S(1)}, bf16[512,512]{1,0:T(8,128)(2,1)S(1)}, u32[]{:S(2)}, u32[]{:S(2)}) %collective-permute-start.19) | collective-permute-done | bytes 524320 | tf_op jit(solution)/shard_map/ppermute | solution.py:112
  (58 shorter events, 31.4 us)
Async XLA Ops:
  0.0 6.4 %copy-start.1 = (f32[4]{0:T(128)S(1)}, f32[4]{0:T(128)}, u32[]{:S(2)}) copy-start(f32[4]{0:T(128)} %occ.1) | copy-start | bytes 52
  0.0 6.4 %copy-start = (f32[4,512]{1,0:T(4,128)S(1)}, f32[4,512]{1,0:T(4,128)}, u32[]{:S(2)}) copy-start(f32[4,512]{1,0:T(4,128)} %virt.1) | copy-start | bytes 24580
  3.4 6.7 %copy-start.2 = (bf16[2,2048,512]{2,1,0:T(8,128)(2,1)S(1)}, bf16[2,2048,512]{2,1,0:T(8,128)(2,1)}, u32[]{:S(2)}) copy-start(bf16[2,2048,512]{2,1,0:T(8,128)(2,1)} %blocks.3) | copy-start | bytes 12582916
  3.4 43.2 %collective-permute-start.16 = (bf16[1536,512]{1,0:T(8,128)(2,1)}, bf16[1536,512]{1,0:T(8,128)(2,1)S(1)}, u32[]{:S(2)}, u32[]{:S(2)}) collective-permute-start(bf16[1536,512]{1,0:T(8,128)(2,1)} %get-tuple-element.49), channel_id=1, source_target_pairs={{0,16},{16,0},{1,17},{17,1},{2,18},{18,2},{3,19},{19,3},{4,20},{20... | collective-permute-start | bytes 4718600 | tf_op jit(solution)/shard_map/ppermute | solution.py:112
  12.6 2.0 %collective-permute-start = (f32[1,256,512]{2,1,0:T(8,128)S(1)}, f32[1,256,512]{2,1,0:T(8,128)S(1)}, u32[]{:S(2)}, u32[]{:S(2)}) collective-permute-start(f32[1,256,512]{2,1,0:T(8,128)S(1)} %get-tuple-element.22), channel_id=1, source_target_pairs={{0,1},{1,0},{2,3},{3,2},{4,5},{5,4},{6,7},{7,6},{8,9},{9,8},{10,11... | collective-permute-start | bytes 1572872 | tf_op jit(solution)/shard_map/cond/branch_1_fun/ppermute | solution.py:112
  14.7 5.6 %collective-permute-start.1 = (bf16[1,128,512]{2,1,0:T(8,128)(2,1)S(1)}, bf16[1,128,512]{2,1,0:T(8,128)(2,1)S(1)}, u32[]{:S(2)}, u32[]{:S(2)}) collective-permute-start(bf16[1,128,512]{2,1,0:T(8,128)(2,1)S(1)} %select_convert_fusion), channel_id=1, source_target_pairs={{0,2},{1,3},{2,0},{3,1},{4,6},{5,7},{6,4},{7,5},{8,10},{9,11},{10,... | collective-permute-start | bytes 393224 | tf_op jit(solution)/shard_map/cond/branch_1_fun/ppermute | solution.py:112
  20.4 4.3 %collective-permute-start.2 = (bf16[1,64,512]{2,1,0:T(8,128)(2,1)S(1)}, bf16[1,64,512]{2,1,0:T(8,128)(2,1)S(1)}, u32[]{:S(2)}, u32[]{:S(2)}) collective-permute-start(bf16[1,64,512]{2,1,0:T(8,128)(2,1)S(1)} %select_convert_fusion.1), channel_id=1, source_target_pairs={{0,4},{1,5},{2,6},{3,7},{4,0},{5,1},{6,2},{7,3},{8,12},{9,13},{10,... | collective-permute-start | bytes 196616 | tf_op jit(solution)/shard_map/cond/branch_1_fun/ppermute | solution.py:112
  24.8 4.9 %collective-permute-start.3 = (bf16[1,32,512]{2,1,0:T(8,128)(2,1)S(1)}, bf16[1,32,512]{2,1,0:T(8,128)(2,1)S(1)}, u32[]{:S(2)}, u32[]{:S(2)}) collective-permute-start(bf16[1,32,512]{2,1,0:T(8,128)(2,1)S(1)} %select_convert_fusion.2), channel_id=1, source_target_pairs={{0,8},{1,9},{2,10},{3,11},{4,12},{5,13},{6,14},{7,15},{8,0},{9,1},... | collective-permute-start | bytes 98312 | tf_op jit(solution)/shard_map/cond/branch_1_fun/ppermute | solution.py:112
  29.7 4.9 %collective-permute-start.4 = (bf16[1,1,32,512]{3,2,1,0:T(8,128)(2,1)S(1)}, bf16[1,1,32,512]{3,2,1,0:T(8,128)(2,1)S(1)}, u32[]{:S(2)}, u32[]{:S(2)}) collective-permute-start(bf16[1,1,32,512]{3,2,1,0:T(8,128)(2,1)S(1)} %fusion), channel_id=1, source_target_pairs={{0,8},{1,9},{2,10},{3,11},{4,12},{5,13},{6,14},{7,15},{8,0},{9,1},... | collective-permute-start | bytes 98312 | tf_op jit(solution)/shard_map/cond/branch_1_fun/ppermute | solution.py:112
  34.6 4.3 %collective-permute-start.5 = (bf16[2,1,32,512]{3,2,1,0:T(8,128)(2,1)S(1)}, bf16[2,1,32,512]{3,2,1,0:T(8,128)(2,1)S(1)}, u32[]{:S(2)}, u32[]{:S(2)}) collective-permute-start(bf16[2,1,32,512]{3,2,1,0:T(8,128)(2,1)S(1)} %pad_maximum_fusion.2), channel_id=1, source_target_pairs={{0,4},{1,5},{2,6},{3,7},{4,0},{5,1},{6,2},{7,3},{8,12},{9,13},{10,... | collective-permute-start | bytes 196616 | tf_op jit(solution)/shard_map/cond/branch_1_fun/ppermute | solution.py:112
  38.9 5.0 %collective-permute-start.6 = (bf16[4,1,32,512]{3,2,1,0:T(8,128)(2,1)S(1)}, bf16[4,1,32,512]{3,2,1,0:T(8,128)(2,1)S(1)}, u32[]{:S(2)}, u32[]{:S(2)}) collective-permute-start(bf16[4,1,32,512]{3,2,1,0:T(8,128)(2,1)S(1)} %pad_maximum_fusion.1), channel_id=1, source_target_pairs={{0,2},{1,3},{2,0},{3,1},{4,6},{5,7},{6,4},{7,5},{8,10},{9,11},{10,... | collective-permute-start | bytes 393224 | tf_op jit(solution)/shard_map/cond/branch_1_fun/ppermute | solution.py:112
  44.7 1.9 %collective-permute-start.7 = (bf16[8,1,32,512]{3,2,1,0:T(8,128)(2,1)}, bf16[8,1,32,512]{3,2,1,0:T(8,128)(2,1)}, u32[]{:S(2)}, u32[]{:S(2)}) collective-permute-start(bf16[8,1,32,512]{3,2,1,0:T(8,128)(2,1)} %pad_maximum_fusion), channel_id=1, source_target_pairs={{0,1},{1,0},{2,3},{3,2},{4,5},{5,4},{6,7},{7,6},{8,9},{9,8},{10,11... | collective-permute-start | bytes 786440 | tf_op jit(solution)/shard_map/cond/branch_1_fun/ppermute | solution.py:112
  46.6 6.5 %copy-start.3 = (bf16[2,2048,512]{2,1,0:T(8,128)(2,1)S(1)}, bf16[2,2048,512]{2,1,0:T(8,128)(2,1)}, u32[]{:S(2)}) copy-start(bf16[2,2048,512]{2,1,0:T(8,128)(2,1)} %blocks.3) | copy-start | bytes 12582916
  46.6 35.8 %collective-permute-start.17 = (bf16[512,512]{1,0:T(8,128)(2,1)}, bf16[512,512]{1,0:T(8,128)(2,1)S(1)}, u32[]{:S(2)}, u32[]{:S(2)}) collective-permute-start(bf16[512,512]{1,0:T(8,128)(2,1)} %get-tuple-element.58), channel_id=1, source_target_pairs={{0,16},{16,0},{1,17},{17,1},{2,18},{18,2},{3,19},{19,3},{4,20},{20... | collective-permute-start | bytes 1572872 | tf_op jit(solution)/shard_map/ppermute | solution.py:112
  53.7 3.1 %collective-permute-start.8 = (f32[2,256,512]{2,1,0:T(8,128)}, f32[2,256,512]{2,1,0:T(8,128)}, u32[]{:S(2)}, u32[]{:S(2)}) collective-permute-start(f32[2,256,512]{2,1,0:T(8,128)} %get-tuple-element.25), channel_id=1, source_target_pairs={{0,1},{1,0},{2,3},{3,2},{4,5},{5,4},{6,7},{7,6},{8,9},{9,8},{10,11... | collective-permute-start | bytes 3145736 | tf_op jit(solution)/shard_map/cond/branch_1_fun/ppermute | solution.py:112
  58.5 1.0 copy-start.5
  60.2 8.6 %collective-permute-start.9 = (bf16[2,128,512]{2,1,0:T(8,128)(2,1)}, bf16[2,128,512]{2,1,0:T(8,128)(2,1)S(1)}, u32[]{:S(2)}, u32[]{:S(2)}) collective-permute-start(bf16[2,128,512]{2,1,0:T(8,128)(2,1)} %select_convert_fusion.3), channel_id=1, source_target_pairs={{0,2},{1,3},{2,0},{3,1},{4,6},{5,7},{6,4},{7,5},{8,10},{9,11},{10,... | collective-permute-start | bytes 786440 | tf_op jit(solution)/shard_map/cond/branch_1_fun/ppermute | solution.py:112
  70.1 0.8 copy-start.6
  70.9 5.0 %collective-permute-start.10 = (bf16[2,64,512]{2,1,0:T(8,128)(2,1)S(1)}, bf16[2,64,512]{2,1,0:T(8,128)(2,1)S(1)}, u32[]{:S(2)}, u32[]{:S(2)}) collective-permute-start(bf16[2,64,512]{2,1,0:T(8,128)(2,1)S(1)} %select_convert_fusion.4), channel_id=1, source_target_pairs={{0,4},{1,5},{2,6},{3,7},{4,0},{5,1},{6,2},{7,3},{8,12},{9,13},{10,... | collective-permute-start | bytes 393224 | tf_op jit(solution)/shard_map/cond/branch_1_fun/ppermute | solution.py:112
  77.1 5.2 %collective-permute-start.11 = (bf16[2,32,512]{2,1,0:T(8,128)(2,1)S(1)}, bf16[2,32,512]{2,1,0:T(8,128)(2,1)S(1)}, u32[]{:S(2)}, u32[]{:S(2)}) collective-permute-start(bf16[2,32,512]{2,1,0:T(8,128)(2,1)S(1)} %select_convert_fusion.5), channel_id=1, source_target_pairs={{0,8},{1,9},{2,10},{3,11},{4,12},{5,13},{6,14},{7,15},{8,0},{9,1},... | collective-permute-start | bytes 196616 | tf_op jit(solution)/shard_map/cond/branch_1_fun/ppermute | solution.py:112
  82.4 6.2 %collective-permute-start.18 = (f32[2,32,512]{2,1,0:T(8,128)S(1)}, f32[2,32,512]{2,1,0:T(8,128)S(1)}, u32[]{:S(2)}, u32[]{:S(2)}) collective-permute-start(f32[2,32,512]{2,1,0:T(8,128)S(1)} %get-tuple-element.81), channel_id=1, source_target_pairs={{0,16},{16,0},{1,17},{17,1},{2,18},{18,2},{3,19},{19,3},{4,20},{20... | collective-permute-start | bytes 393224 | tf_op jit(solution)/shard_map/ppermute | solution.py:112
  88.6 31.1 %collective-permute-start.20 = (bf16[1024,512]{1,0:T(8,128)(2,1)S(1)}, bf16[1024,512]{1,0:T(8,128)(2,1)}, u32[]{:S(2)}, u32[]{:S(2)}) collective-permute-start(bf16[1024,512]{1,0:T(8,128)(2,1)S(1)} %shard_map.49), channel_id=1, source_target_pairs={{0,16},{16,0},{1,17},{17,1},{2,18},{18,2},{3,19},{19,3},{4,20},{20... | collective-permute-start | bytes 3145736 | tf_op jit(solution)/shard_map/ppermute | solution.py:112
  90.8 5.2 %collective-permute-start.12 = (bf16[1,2,32,512]{3,2,1,0:T(8,128)(2,1)S(1)}, bf16[1,2,32,512]{3,2,1,0:T(8,128)(2,1)S(1)}, u32[]{:S(2)}, u32[]{:S(2)}) collective-permute-start(bf16[1,2,32,512]{3,2,1,0:T(8,128)(2,1)S(1)} %bitcast.5), channel_id=1, source_target_pairs={{0,8},{1,9},{2,10},{3,11},{4,12},{5,13},{6,14},{7,15},{8,0},{9,1},... | collective-permute-start | bytes 196616 | tf_op jit(solution)/shard_map/cond/branch_1_fun/ppermute | solution.py:112
  95.9 5.0 %collective-permute-start.13 = (bf16[2,2,32,512]{3,2,1,0:T(8,128)(2,1)S(1)}, bf16[2,2,32,512]{3,2,1,0:T(8,128)(2,1)S(1)}, u32[]{:S(2)}, u32[]{:S(2)}) collective-permute-start(bf16[2,2,32,512]{3,2,1,0:T(8,128)(2,1)S(1)} %pad_maximum_fusion.5), channel_id=1, source_target_pairs={{0,4},{1,5},{2,6},{3,7},{4,0},{5,1},{6,2},{7,3},{8,12},{9,13},{10,... | collective-permute-start | bytes 393224 | tf_op jit(solution)/shard_map/cond/branch_1_fun/ppermute | solution.py:112
  101.0 6.4 %collective-permute-start.14 = (bf16[4,2,32,512]{3,2,1,0:T(8,128)(2,1)S(1)}, bf16[4,2,32,512]{3,2,1,0:T(8,128)(2,1)S(1)}, u32[]{:S(2)}, u32[]{:S(2)}) collective-permute-start(bf16[4,2,32,512]{3,2,1,0:T(8,128)(2,1)S(1)} %pad_maximum_fusion.4), channel_id=1, source_target_pairs={{0,2},{1,3},{2,0},{3,1},{4,6},{5,7},{6,4},{7,5},{8,10},{9,11},{10,... | collective-permute-start | bytes 786440 | tf_op jit(solution)/shard_map/cond/branch_1_fun/ppermute | solution.py:112
  108.3 2.3 %collective-permute-start.15 = (bf16[8,2,32,512]{3,2,1,0:T(8,128)(2,1)}, bf16[8,2,32,512]{3,2,1,0:T(8,128)(2,1)}, u32[]{:S(2)}, u32[]{:S(2)}) collective-permute-start(bf16[8,2,32,512]{3,2,1,0:T(8,128)(2,1)} %pad_maximum_fusion.3), channel_id=1, source_target_pairs={{0,1},{1,0},{2,3},{3,2},{4,5},{5,4},{6,7},{7,6},{8,9},{9,8},{10,11... | collective-permute-start | bytes 1572872 | tf_op jit(solution)/shard_map/cond/branch_1_fun/ppermute | solution.py:112
  110.5 3.3 %copy-start.4 = (bf16[2,2048,512]{2,1,0:T(8,128)(2,1)S(1)}, bf16[2,2048,512]{2,1,0:T(8,128)(2,1)}, u32[]{:S(2)}) copy-start(bf16[2,2048,512]{2,1,0:T(8,128)(2,1)} %blocks.3) | copy-start | bytes 12582916
  113.6 14.0 %collective-permute-start.19 = (bf16[512,512]{1,0:T(8,128)(2,1)S(1)}, bf16[512,512]{1,0:T(8,128)(2,1)S(1)}, u32[]{:S(2)}, u32[]{:S(2)}) collective-permute-start(bf16[512,512]{1,0:T(8,128)(2,1)S(1)} %shard_map.50), channel_id=1, source_target_pairs={{0,16},{16,0},{1,17},{17,1},{2,18},{18,2},{3,19},{19,3},{4,20},{20... | collective-permute-start | bytes 1572872 | tf_op jit(solution)/shard_map/ppermute | solution.py:112

commit v4 on v3

--- a/solution.py
+++ b/solution.py
@@ -185,11 +185,16 @@
     wait_all(copies)
 
 
-def weigh_kernel(step, plan, occ, virt, factors, own_weight, weights, pay_a, sem):
-    helps = plan[HELPS]
-    block = jnp.where(helps == 1, 1, plan[FOREIGN])
-    copy = pltpu.make_async_copy(factors.at[block, rows_at(step, 3 - helps, 1)], pay_a, sem)
-    copy.start()
+def weigh_kernel(step, plan, occ, virt, factors, own_weight, weights, pay_a, sems):
+    helps, foreign = plan[HELPS], plan[FOREIGN]
+    b0, b1 = jnp.where(helps == 1, 0, foreign), jnp.where(helps == 1, 1, foreign)
+    copies = [
+        pltpu.make_async_copy(
+            factors.at[block, rows_at(step, start, 1)], pay_a.at[pl.ds(n * step, step)], sems.at[n]
+        )
+        for n, (block, start) in enumerate(((b1, 3 - helps), (b0, 1)))
+    ]
+    start_all(copies)
     low, partner = plan[LOW], plan[PARTNER]
     _, shard, width = own_weight.shape
     row = lax.broadcasted_iota(jnp.int32, (shard, width), 0)
@@ -200,17 +205,19 @@
         virt_a = jnp.sum(jnp.where(mine, virt[pl.ds(a, 1), :], 0.0), axis=1, keepdims=True)
         denominators = virt_a + virt[pl.ds(b, 1), :] - occ[a] - occ[b]
         out[slot] = plan[COUNTS + n].astype(jnp.float32) / denominators
-    copy.wait()
-
-
-def pack_kernel(step, plan, factors, pay_b, sems):
+    wait_all(copies)
+
+
+def pack_kernel(unit, plan, factors, pay_b, sems):
     helps, foreign = plan[HELPS], plan[FOREIGN]
-    blocks = (jnp.where(helps == 1, 0, foreign), jnp.where(helps == 1, 1, foreign))
+    b0, b1 = jnp.where(helps == 1, 0, foreign), jnp.where(helps == 1, 1, foreign)
     copies = [
         pltpu.make_async_copy(
-            factors.at[block, pl.ds(step, step)], pay_b.at[pl.ds(n * step, step)], sems.at[n]
-        )
-        for n, block in enumerate(blocks)
+            factors.at[block, pl.ds(start * unit, size * unit)],
+            pay_b.at[pl.ds(to * unit, size * unit)],
+            sems.at[n],
+        )
+        for n, (block, start, size, to) in enumerate(((b1, 2, 2, 0), (b0, 1, 1, 2), (b1, 1, 1, 3)))
     ]
     start_all(copies)
     wait_all(copies)
@@ -314,49 +321,61 @@
     back[...] = total.astype(back.dtype)
 
 
-def last_kernel(plan, near01, far01, near, far, x, a, y, blocks, out, own, amp0, amp1):
+def last_kernel(plan, near01, far01, near, far, x, a, y, block0, block1, out, amps0, amps1):
     seg = pl.program_id(0)
     helps = plan[HELPS] == 1
-
-    @pl.when(seg == 0)
-    def _():
-        arrange(plan, near01, far01, 0, own)
+    width = block0.shape[2]
+
+    @pl.when((seg == 0) & helps)
+    def _():
+        arrange(plan, near01, far01, 0, amps1.at[:width])
+        amps0[:width] = amps1[:width].T
+        arrange(plan, near, far, 0, amps1.at[width:])
+        amps0[width:] = amps1[width:].T
+        arrange(plan, near, far, 1, amps1.at[width:])
+        amps1[width:] = amps1[width:].T
+
+    @pl.when((seg == 0) & jnp.logical_not(helps))
+    def _():
+        arrange(plan, near, far, 0, amps0.at[:width])
+        arrange(plan, near, far, 1, amps0.at[width:])
+
+    @pl.when(helps)
+    def _():
+        foreign = jnp.where(seg < 3, x[...], a[...])
+        rows0 = jnp.concatenate([block1[0], foreign], axis=1)
+        rows1 = jnp.concatenate([block0[0], foreign], axis=1)
+        out[0] = right(rows0, amps0[...]).astype(out.dtype)
+        out[1] = right(rows1, amps1[...]).astype(out.dtype)
+
+    @pl.when(jnp.logical_not(helps))
+    def _():
+        out[...] = jnp.zeros_like(out)
+
+    @pl.when(jnp.logical_not(helps) & (seg >= 2))
+    def _():
+        rows = jnp.concatenate([x[...], jnp.where(seg < 3, a[...], y[...])], axis=1)
+        out[plan[FOREIGN]] = right(rows, amps0[...]).astype(out.dtype)
+
+
+def late_kernel(unit, plan, near, far, got_a, got_b, gamma_in, gamma, amp0, amp1, rows, sem):
+    @pl.when(plan[HELPS] == 0)
+    def _():
         arrange(plan, near, far, 0, amp0)
         arrange(plan, near, far, 1, amp1)
-
-    @pl.when(helps)
-    def _():
-        foreign = jnp.where(seg < 3, x[...], a[...])
-        out[0] = (right_t(blocks[1], own[...]) + right_t(foreign, amp0[...])).astype(out.dtype)
-        out[1] = (right(blocks[0], own[...]) + right_t(foreign, amp1[...])).astype(out.dtype)
-
-    @pl.when(jnp.logical_not(helps))
-    def _():
-        out[...] = jnp.zeros_like(out)
-
-    @pl.when(jnp.logical_not(helps) & (seg >= 2))
-    def _():
-        rows1 = jnp.where(seg < 3, a[...], y[...])
-        total = right(x[...], amp0[...]) + right(rows1, amp1[...])
-        out[plan[FOREIGN]] = total.astype(out.dtype)
-
-
-def late_kernel(step, plan, near, far, got, gamma_in, gamma, amp0, amp1, rows, sem):
-    @pl.when(plan[HELPS] == 0)
-    def _():
-        arrange(plan, near, far, 0, amp0)
-        arrange(plan, near, far, 1, amp1)
-        total = right(got[:step], amp0[...]) + right(got[step:], amp1[...])
-        rows[...] = total.astype(rows.dtype)
-        copy = pltpu.make_async_copy(rows, gamma.at[plan[FOREIGN], pl.ds(step, step)], sem)
+        total = right(got_b[2 * unit : 3 * unit], amp0[...]) + right(got_b[3 * unit :], amp1[...])
+        rows[:unit] = total.astype(rows.dtype)
+        total = right(got_a[2 * unit :], amp0[...]) + right(got_b[: 2 * unit], amp1[...])
+        rows[unit:] = total.astype(rows.dtype)
+        copy = pltpu.make_async_copy(rows, gamma.at[plan[FOREIGN], pl.ds(unit, 3 * unit)], sem)
         copy.start()
         copy.wait()
 
 
-def put_kernel(step, plan, back, gamma_in, gamma, sem):
+def put_kernel(unit, plan, back, gamma_in, gamma, sem):
     @pl.when(plan[HELPS] == 0)
     def _():
-        copy = pltpu.make_async_copy(back, gamma.at[plan[FOREIGN], pl.ds(0, step)], sem)
+        copy = pltpu.make_async_copy(back, gamma.at[plan[FOREIGN], pl.ds(0, unit)], sem)
         copy.start()
         copy.wait()
 
@@ -365,7 +384,7 @@
     owned, rows, width = factors.shape
     aux = lax.axis_size("aux")
     bits = aux.bit_length() - 1
-    step = rows // 4
+    step, unit = rows // 4, rows // 8
     shard = width // aux
     wires = [jnp.float32] + [WIRE] * (bits - 1)
     dtype = factors.dtype
@@ -406,17 +425,18 @@
 
     square = pltpu.VMEM((width, width), jnp.float32)
 
-    own_weight, weights, pay_a = call(
-        functools.partial(weigh_kernel, step),
-        (
-            array(1, shard, width, dtype=jnp.float32),
-            array(2, shard, width, dtype=jnp.float32),
-            array(step, width),
-        ),
-        [SMEM_SPEC, SMEM_SPEC, VMEM_SPEC, HBM_SPEC],
-        (VMEM_SPEC, VMEM_SPEC, VMEM_SPEC),
-        [dma],
-    )(plan, occ_energy, virt_energy, factors)
+    def prepare():
+        return call(
+            functools.partial(weigh_kernel, step),
+            (
+                array(1, shard, width, dtype=jnp.float32),
+                array(2, shard, width, dtype=jnp.float32),
+                array(2 * step, width),
+            ),
+            [SMEM_SPEC, SMEM_SPEC, VMEM_SPEC, HBM_SPEC],
+            (VMEM_SPEC, VMEM_SPEC, VMEM_SPEC),
+            [dma((2,))],
+        )(plan, occ_energy, virt_energy, factors)
 
     def own_chain():
         kept, sent = call(
@@ -427,47 +447,50 @@
             [pltpu.VMEM(factors.shape, dtype), square, dma((4,))],
             4,
         )(plan, factors)
+        own_weight, weights, pay_a = prepare()
         sum01 = halve(kept, sent, "aux", wires)
-        return double((sum01 * own_weight).astype(dtype), "aux", bits)
+        return *double((sum01 * own_weight).astype(dtype), "aux", bits), weights, pay_a
 
     def no_chain():
         half = jnp.zeros((aux // 2, 1, shard, width), dtype)
-        return half, half
-
-    near01, far01 = lax.cond(plan[COUNTS] > 0, own_chain, no_chain)
-
+        return half, half, *prepare()[1:]
+
+    near01, far01, weights, pay_a = lax.cond(plan[COUNTS] > 0, own_chain, no_chain)
     got1, near01, far01, weights, pay_a = lax.optimization_barrier(
         (got1, near01, far01, weights, pay_a)
     )
     got_a = swap(pay_a, "orb", 0)
 
-    kept, sent = call(
-        functools.partial(pair_kernel, step),
-        halves(2),
-        [SMEM_SPEC, HBM_SPEC, VMEM_SPEC],
-        (VMEM_SPEC, VMEM_SPEC),
-        [
-            pltpu.VMEM((2 * step, width), dtype),
-            pltpu.VMEM((3 * step, width), dtype),
-            square,
-            square,
-            dma((5,)),
-        ],
-        5,
-    )(plan, factors, got1)
+    def pair_chain():
+        kept, sent = call(
+            functools.partial(pair_kernel, step),
+            halves(2),
+            [SMEM_SPEC, HBM_SPEC, VMEM_SPEC],
+            (VMEM_SPEC, VMEM_SPEC),
+            [
+                pltpu.VMEM((2 * step, width), dtype),
+                pltpu.VMEM((3 * step, width), dtype),
+                square,
+                square,
+                dma((5,)),
+            ],
+            5,
+        )(plan, factors, got1)
+        return halve(kept, sent, "aux", wires), pack(after(plan, kept))
+
+    def pack(plan):
+        return call(
+            functools.partial(pack_kernel, unit),
+            array(4 * unit, width),
+            [SMEM_SPEC, HBM_SPEC],
+            VMEM_SPEC,
+            [dma((3,))],
+        )(plan, factors)
+
     used = plan[COUNTS + 1] + plan[COUNTS + 2] > 0
-    sums = lax.cond(
-        used,
-        lambda: halve(kept, sent, "aux", wires),
-        lambda: jnp.zeros((2, shard, width), jnp.float32),
+    sums, pay_b = lax.cond(
+        used, pair_chain, lambda: (jnp.zeros((2, shard, width), jnp.float32), pack(plan))
     )
-    pay_b = call(
-        functools.partial(pack_kernel, step),
-        array(2 * step, width),
-        [SMEM_SPEC, HBM_SPEC],
-        VMEM_SPEC,
-        [dma((2,))],
-    )(after(plan, kept), factors)
     sums, got_a, pay_b = lax.optimization_barrier((sums, got_a, pay_b))
     sums = sums + swap(sums, "orb", 0)
     shards0, pay_b = lax.optimization_barrier(((sums * weights).astype(dtype), pay_b))
@@ -511,10 +534,10 @@
         [
             whole(near.shape),
             whole(far.shape),
-            pl.BlockSpec((2, step, width), lambda i, plan: (0, 0, 0)),
+            pl.BlockSpec((2, unit, width), lambda i, plan: (0, 0, 0)),
         ],
-        array(step, width),
-        whole((step, width)),
+        array(unit, width),
+        whole((unit, width)),
         [amp, amp],
         1,
     )(plan, near, far, factors)
@@ -538,24 +561,28 @@
         last_kernel,
         4,
         [whole(near01.shape), whole(far01.shape), whole(near.shape), whole(far.shape)]
-        + [at(clip(0, 2, 0), clip(0, 1, -2)), at(none, none), at(none, clip(2, 2, 0)), pieces],
+        + [at(clip(0, 2, 0), clip(0, 1, -2)), at(none, none), at(none, clip(2, 2, 0))]
+        + [
+            pl.BlockSpec((1, step, width), lambda i, plan: (0, i, 0)),
+            pl.BlockSpec((1, step, width), lambda i, plan: (1, i, 0)),
+        ],
         array(*factors.shape),
         pieces,
-        [amp, amp, amp],
+        [pltpu.VMEM((2 * width, width), dtype)] * 2,
         12,
-    )(plan, near01, far01, near, far, got1, got_a, got1, factors)
+    )(plan, near01, far01, near, far, got1, got_a, got1, factors, factors)
 
     gamma = call(
-        functools.partial(late_kernel, step),
+        functools.partial(late_kernel, unit),
         array(*factors.shape),
-        [SMEM_SPEC, VMEM_SPEC, VMEM_SPEC, VMEM_SPEC, HBM_SPEC],
+        [SMEM_SPEC, VMEM_SPEC, VMEM_SPEC, VMEM_SPEC, VMEM_SPEC, HBM_SPEC],
         HBM_SPEC,
-        [amp, amp, pltpu.VMEM((step, width), dtype), dma],
+        [amp, amp, pltpu.VMEM((3 * unit, width), dtype), dma],
         1,
-        input_output_aliases={4: 0},
-    )(plan, near, far, got_b, gamma)
+        input_output_aliases={5: 0},
+    )(plan, near, far, got_a, got_b, gamma)
     return call(
-        functools.partial(put_kernel, step),
+        functools.partial(put_kernel, unit),
         array(*factors.shape),
         [SMEM_SPEC, VMEM_SPEC, HBM_SPEC],
         HBM_SPEC,

time: 129 us -> 115 us (0.89)
  waiting for transfers between devices: 58.2 us -> 47.7 us
  other arithmetic: 6.85 us -> 3.61 us
  Pallas kernels: 26.7 us -> 29.5 us
  local copies, waits for them, and re-layouts: 2.41 us -> 0.65 us
    ppermute x21, waiting for transfers between devices: 58.2 us -> 47.7 us  [swap(): return lax.ppermute(value, axis, [(i, i ^ 1 << bit) for i in range(size)])]
    add x5, other arithmetic: 2.51 us -> 0.27 us  [halve(): part = kept + swap(sent, axis, bit).astype(jnp.float32)]
    pallas_call x5, Pallas kernels: 12 us -> 13.9 us  [the longest x1 4.05 us: pair_chain(): call(functools.partial(pair_kernel, step), halves(2), [SMEM_SPEC, HBM_SPE...]
    cond x4 -> x0, local copies, waits for them, and re-layouts: 1.74 us -> none
  transfers between devices with their start and end apart: 21 -> 21, of which waited for: 18 -> 16; matrix products, arithmetic and copies ran while one was open for 6% -> 4% of each run, Pallas kernels for 17% -> 22%
where the time goes in v4:
time: 115 us; the launch traced here: 116 us
  waiting for transfers between devices  47.7 us (41%)
  starting transfers between devices  32 us (28%)
  Pallas kernels  29.5 us (26%)
  other arithmetic  3.61 us (3%)
  between operations  1.97 us (2%)
    ppermute x21, waiting for transfers between devices, swap(): return lax.ppermute(value, axis, [(i, i ^ 1 << bit) for i in range(size)])  47.7 us
    ppermute x21, starting transfers between devices, swap(): return lax.ppermute(value, axis, [(i, i ^ 1 << bit) for i in range(size)])  32 us
    pallas_call x1, Pallas kernels, two_groups(): run(last_kernel, 4, [whole(near01.shape), whole(far01.shape), whole(near....  6.16 us
    pallas_call x1, Pallas kernels, pair_chain(): call(functools.partial(pair_kernel, step), halves(2), [SMEM_SPEC, HBM_SPE...  4.05 us
    pallas_call x1, Pallas kernels, own_chain(): call(functools.partial(own_kernel, step), halves(1), [SMEM_SPEC, HBM_SPEC...  3.4 us
    pallas_call x1, Pallas kernels, two_groups(): call(functools.partial(plan_kernel, tile_table.shape[0], bits, step), (ar...  3.37 us
    pallas_call x1, Pallas kernels, two_groups(): call(functools.partial(late_kernel, unit), array(*factors.shape), [SMEM_S...  3.12 us
    pallas_call x1, Pallas kernels, prepare(): call(functools.partial(weigh_kernel, step), (array(1, shard, width, dtype...  2.76 us
  transfers between devices with their start and end apart: 21, of which 16 were waited for; matrix products, arithmetic and copies ran while one was open for 4% of the time, Pallas kernels for 22%

profile of v4, /device:TPU:0, one launch (start us, length us, event | category | flops | bytes accessed | tf_op | source)
XLA Modules:
  0.0 115.6 jit_solution(635855206784043160)
XLA Ops:
  0.0 3.4 %shard_map.46 = (s32[8]{0:T(128)S(1)}, bf16[1536,512]{1,0:T(8,128)(2,1)}) custom-call(s32[4,3]{1,0:T(4,128)} %table.1, bf16[2,2048,512]{2,1,0:T(8,128)(2,1)} %block1.1), custom_call_target="tpu_custom_call" | custom-call | bytes 1048576 | tf_op jit(solution)/shard_map/pallas_call | solution.py:412
  3.4 3.0 %collective-permute-start.16 = (bf16[1536,512]{1,0:T(8,128)(2,1)}, bf16[1536,512]{1,0:T(8,128)(2,1)}, u32[]{:S(2)}, u32[]{:S(2)}) collective-permute-start(bf16[1536,512]{1,0:T(8,128)(2,1)} %get-tuple-element.76), channel_id=1, source_target_pairs={{0,16},{16,0},{1,17},{17,1},{2,18},{18,2},{3,19},{19,3},{4,20},{20... | collective-permute-start | bytes 4718600 | tf_op jit(solution)/shard_map/ppermute | solution.py:112
  7.7 37.9 %conditional.3 = (bf16[8,1,32,512]{3,2,1,0:T(8,128)(2,1)}, bf16[8,1,32,512]{3,2,1,0:T(8,128)(2,1)}, f32[2,32,512]{2,1,0:T(8,128)S(1)}, bf16[1024,512]{1,0:T(8,128)(2,1)}) conditional(s32[]{:T(128)} %bitcast.3, (s32[8]{0:T(128)S(1)}, f32[4]{0:T(128)S(1)}, f32[4,512]{1,0:T(4,128)S(1)}, bf16[2,2048,512]{2,1,0:T(8,128)(2,1)}) %tuple.51, (s32[8]{0:T(128)S(1)}, ...), branch_computations={%region_0.0_spmd, %region_1.2_spmd} | conditional | flops 1074921472 | bytes 11895261 | solution.py:458
  7.7 3.4 %branch_1_fun.4 = (f32[1,256,512]{2,1,0:T(8,128)S(1)}, f32[1,256,512]{2,1,0:T(8,128)S(1)}) custom-call(s32[8]{0:T(128)S(1)} %get-tuple-element.38.plan, bf16[2,2048,512]{2,1,0:T(8,128)(2,1)} %get-tuple-element.39.factors), custom_call_target="tpu_custom_call" | custom-call | flops 1073741824 | bytes 1048576 | tf_op jit(solution)/shard_map/cond/branch_1_fun/pallas_call | solution.py:442
  14.8 4.0 %collective-permute-done.1 = bf16[1,128,512]{2,1,0:T(8,128)(2,1)S(1)} collective-permute-done((bf16[1,128,512]{2,1,0:T(8,128)(2,1)S(1)}, bf16[1,128,512]{2,1,0:T(8,128)(2,1)S(1)}, u32[]{:S(2)}, u32[]{:S(2)}) %collective-permute-start.1) | collective-permute-done | bytes 131104 | tf_op jit(solution)/shard_map/cond/branch_1_fun/ppermute | solution.py:112
  20.6 2.7 %collective-permute-done.2 = bf16[1,64,512]{2,1,0:T(8,128)(2,1)S(1)} collective-permute-done((bf16[1,64,512]{2,1,0:T(8,128)(2,1)S(1)}, bf16[1,64,512]{2,1,0:T(8,128)(2,1)S(1)}, u32[]{:S(2)}, u32[]{:S(2)}) %collective-permute-start.2) | collective-permute-done | bytes 65568 | tf_op jit(solution)/shard_map/cond/branch_1_fun/ppermute | solution.py:112
  23.3 2.7 %collective-permute-start.3 = (bf16[1,32,512]{2,1,0:T(8,128)(2,1)S(1)}, bf16[1,32,512]{2,1,0:T(8,128)(2,1)S(1)}, u32[]{:S(2)}, u32[]{:S(2)}) collective-permute-start(bf16[1,32,512]{2,1,0:T(8,128)(2,1)S(1)} %select_convert_fusion.2), channel_id=1, source_target_pairs={{0,8},{1,9},{2,10},{3,11},{4,12},{5,13},{6,14},{7,15},{8,0},{9,1},... | collective-permute-start | bytes 98312 | tf_op jit(solution)/shard_map/cond/branch_1_fun/ppermute | solution.py:112
  25.9 2.8 %branch_1_fun.5 = (f32[1,32,512]{2,1,0:T(8,128)S(1)}, f32[2,32,512]{2,1,0:T(8,128)S(1)}, bf16[1024,512]{1,0:T(8,128)(2,1)}) custom-call(s32[8]{0:T(128)S(1)} %get-tuple-element.38.plan, f32[4]{0:T(128)S(1)} %get-tuple-element.42.occ, f32[4,512]{1,0:T(4,128)S(1)} %get-tuple-element.43.virt, bf16[2,2048,512]{2,1,0:T(8,128)(2,1)} %get-tuple-element.39.factors), custom_call_target="tpu_custom_call" | custom-call | bytes 1048576 | tf_op jit(solution)/shard_map/cond/branch_1_fun/pallas_call | solution.py:429
  28.7 2.1 %collective-permute-start.4 = (bf16[1,1,32,512]{3,2,1,0:T(8,128)(2,1)S(1)}, bf16[1,1,32,512]{3,2,1,0:T(8,128)(2,1)S(1)}, u32[]{:S(2)}, u32[]{:S(2)}) collective-permute-start(bf16[1,1,32,512]{3,2,1,0:T(8,128)(2,1)S(1)} %fusion), channel_id=1, source_target_pairs={{0,8},{1,9},{2,10},{3,11},{4,12},{5,13},{6,14},{7,15},{8,0},{9,1},... | collective-permute-start | bytes 98312 | tf_op jit(solution)/shard_map/cond/branch_1_fun/ppermute | solution.py:112
  30.9 2.8 %collective-permute-done.4 = bf16[1,1,32,512]{3,2,1,0:T(8,128)(2,1)S(1)} collective-permute-done((bf16[1,1,32,512]{3,2,1,0:T(8,128)(2,1)S(1)}, bf16[1,1,32,512]{3,2,1,0:T(8,128)(2,1)S(1)}, u32[]{:S(2)}, u32[]{:S(2)}) %collective-permute-start.4) | collective-permute-done | bytes 32800 | tf_op jit(solution)/shard_map/cond/branch_1_fun/ppermute | solution.py:112
  35.6 2.3 %collective-permute-done.5 = bf16[2,1,32,512]{3,2,1,0:T(8,128)(2,1)S(1)} collective-permute-done((bf16[2,1,32,512]{3,2,1,0:T(8,128)(2,1)S(1)}, bf16[2,1,32,512]{3,2,1,0:T(8,128)(2,1)S(1)}, u32[]{:S(2)}, u32[]{:S(2)}) %collective-permute-start.5) | collective-permute-done | bytes 65568 | tf_op jit(solution)/shard_map/cond/branch_1_fun/ppermute | solution.py:112
  39.5 3.5 %collective-permute-done.6 = bf16[4,1,32,512]{3,2,1,0:T(8,128)(2,1)S(1)} collective-permute-done((bf16[4,1,32,512]{3,2,1,0:T(8,128)(2,1)S(1)}, bf16[4,1,32,512]{3,2,1,0:T(8,128)(2,1)S(1)}, u32[]{:S(2)}, u32[]{:S(2)}) %collective-permute-start.6) | collective-permute-done | bytes 131104 | tf_op jit(solution)/shard_map/cond/branch_1_fun/ppermute | solution.py:112
  47.4 27.4 %conditional.4 = (f32[2,32,512]{2,1,0:T(8,128)S(1)}, bf16[1024,512]{1,0:T(8,128)(2,1)}) conditional(s32[]{:T(128)} %bitcast.2, (s32[8]{0:T(128)S(1)}, bf16[2,2048,512]{2,1,0:T(8,128)(2,1)}) %tuple.34, (s32[8]{0:T(128)S(1)}, bf16[2,2048,512]{2,1,0:T(8,128)(2,1)}, bf16[1536,512]{1,0:T(8,128)(2,1)}) %tuple.38), branch_computations={%region_2.3_spmd, %region_3.4_spmd} | conditional | flops 1343356928 | bytes 15860013 | solution.py:491
  47.4 4.1 %branch_1_fun.6 = (f32[2,256,512]{2,1,0:T(8,128)S(1)}, f32[2,256,512]{2,1,0:T(8,128)S(1)}) custom-call(s32[8]{0:T(128)S(1)} %get-tuple-element.54.plan, bf16[2,2048,512]{2,1,0:T(8,128)(2,1)} %get-tuple-element.50.factors, bf16[1536,512]{1,0:T(8,128)(2,1)} %get-tuple-element.51.got), custom_call_target="tpu_custom_call" | custom-call | flops 1342177280 | bytes 1048576 | tf_op jit(solution)/shard_map/cond/branch_1_fun/pallas_call | solution.py:465
  51.6 2.8 %collective-permute-done.8 = f32[2,256,512]{2,1,0:T(8,128)} collective-permute-done((f32[2,256,512]{2,1,0:T(8,128)S(1)}, f32[2,256,512]{2,1,0:T(8,128)}, u32[]{:S(2)}, u32[]{:S(2)}) %collective-permute-start.8) | collective-permute-done | bytes 1048608 | tf_op jit(solution)/shard_map/cond/branch_1_fun/ppermute | solution.py:112
  57.4 6.8 %collective-permute-done.9 = bf16[2,128,512]{2,1,0:T(8,128)(2,1)S(1)} collective-permute-done((bf16[2,128,512]{2,1,0:T(8,128)(2,1)S(1)}, bf16[2,128,512]{2,1,0:T(8,128)(2,1)S(1)}, u32[]{:S(2)}, u32[]{:S(2)}) %collective-permute-start.9) | collective-permute-done | bytes 262176 | tf_op jit(solution)/shard_map/cond/branch_1_fun/ppermute | solution.py:112
  66.4 3.0 %collective-permute-done.10 = bf16[2,64,512]{2,1,0:T(8,128)(2,1)S(1)} collective-permute-done((bf16[2,64,512]{2,1,0:T(8,128)(2,1)S(1)}, bf16[2,64,512]{2,1,0:T(8,128)(2,1)S(1)}, u32[]{:S(2)}, u32[]{:S(2)}) %collective-permute-start.10) | collective-permute-done | bytes 131104 | tf_op jit(solution)/shard_map/cond/branch_1_fun/ppermute | solution.py:112
  69.5 2.1 %collective-permute-start.11 = (bf16[2,32,512]{2,1,0:T(8,128)(2,1)S(1)}, bf16[2,32,512]{2,1,0:T(8,128)(2,1)S(1)}, u32[]{:S(2)}, u32[]{:S(2)}) collective-permute-start(bf16[2,32,512]{2,1,0:T(8,128)(2,1)S(1)} %select_convert_fusion.5), channel_id=1, source_target_pairs={{0,8},{1,9},{2,10},{3,11},{4,12},{5,13},{6,14},{7,15},{8,0},{9,1},... | collective-permute-start | bytes 196616 | tf_op jit(solution)/shard_map/cond/branch_1_fun/ppermute | solution.py:112
  71.6 2.7 %branch_1_fun.7 = bf16[1024,512]{1,0:T(8,128)(2,1)} custom-call(s32[8]{0:T(128)S(1)} %get-tuple-element.54.plan, bf16[2,2048,512]{2,1,0:T(8,128)(2,1)} %get-tuple-element.50.factors), custom_call_target="tpu_custom_call" | custom-call | bytes 1048576 | tf_op jit(solution)/shard_map/cond/branch_1_fun/pallas_call | solution.py:482
  74.8 2.1 %collective-permute-start.18 = (f32[2,32,512]{2,1,0:T(8,128)S(1)}, f32[2,32,512]{2,1,0:T(8,128)S(1)}, u32[]{:S(2)}, u32[]{:S(2)}) collective-permute-start(f32[2,32,512]{2,1,0:T(8,128)S(1)} %get-tuple-element.85), channel_id=1, source_target_pairs={{0,16},{16,0},{1,17},{17,1},{2,18},{18,2},{3,19},{19,3},{4,20},{20... | collective-permute-start | bytes 393224 | tf_op jit(solution)/shard_map/ppermute | solution.py:112
  76.9 2.9 %collective-permute-done.18 = f32[2,32,512]{2,1,0:T(8,128)S(1)} collective-permute-done((f32[2,32,512]{2,1,0:T(8,128)S(1)}, f32[2,32,512]{2,1,0:T(8,128)S(1)}, u32[]{:S(2)}, u32[]{:S(2)}) %collective-permute-start.18) | collective-permute-done | bytes 131104 | tf_op jit(solution)/shard_map/ppermute | solution.py:112
  79.9 2.3 %collective-permute-start.20 = (bf16[1024,512]{1,0:T(8,128)(2,1)}, bf16[1024,512]{1,0:T(8,128)(2,1)S(1)}, u32[]{:S(2)}, u32[]{:S(2)}) collective-permute-start(bf16[1024,512]{1,0:T(8,128)(2,1)} %get-tuple-element.92), channel_id=1, source_target_pairs={{0,16},{16,0},{1,17},{17,1},{2,18},{18,2},{3,19},{19,3},{4,20},{20... | collective-permute-start | bytes 3145736 | tf_op jit(solution)/shard_map/ppermute | solution.py:112
  82.3 19.9 %conditional.5 = (bf16[8,2,32,512]{3,2,1,0:T(8,128)(2,1)}, bf16[8,2,32,512]{3,2,1,0:T(8,128)(2,1)}) conditional(s32[]{:T(128)} %bitcast.2, () %tuple.33, bf16[2,32,512]{2,1,0:T(8,128)(2,1)S(1)} %multiply_convert_fusion.1), branch_computations={%region_4.5_spmd, %region_5.6_spmd} | conditional | flops 1114112 | bytes 5767344 | solution.py:506
  82.3 2.6 %collective-permute-start.12 = (bf16[1,2,32,512]{3,2,1,0:T(8,128)(2,1)S(1)}, bf16[1,2,32,512]{3,2,1,0:T(8,128)(2,1)S(1)}, u32[]{:S(2)}, u32[]{:S(2)}) collective-permute-start(bf16[1,2,32,512]{3,2,1,0:T(8,128)(2,1)S(1)} %bitcast.5), channel_id=1, source_target_pairs={{0,8},{1,9},{2,10},{3,11},{4,12},{5,13},{6,14},{7,15},{8,0},{9,1},... | collective-permute-start | bytes 196616 | tf_op jit(solution)/shard_map/cond/branch_1_fun/ppermute | solution.py:112
  84.9 2.5 %collective-permute-done.12 = bf16[1,2,32,512]{3,2,1,0:T(8,128)(2,1)S(1)} collective-permute-done((bf16[1,2,32,512]{3,2,1,0:T(8,128)(2,1)S(1)}, bf16[1,2,32,512]{3,2,1,0:T(8,128)(2,1)S(1)}, u32[]{:S(2)}, u32[]{:S(2)}) %collective-permute-start.12) | collective-permute-done | bytes 65568 | tf_op jit(solution)/shard_map/cond/branch_1_fun/ppermute | solution.py:112
  87.4 2.2 %collective-permute-start.13 = (bf16[2,2,32,512]{3,2,1,0:T(8,128)(2,1)S(1)}, bf16[2,2,32,512]{3,2,1,0:T(8,128)(2,1)S(1)}, u32[]{:S(2)}, u32[]{:S(2)}) collective-permute-start(bf16[2,2,32,512]{3,2,1,0:T(8,128)(2,1)S(1)} %pad_maximum_fusion.5), channel_id=1, source_target_pairs={{0,4},{1,5},{2,6},{3,7},{4,0},{5,1},{6,2},{7,3},{8,12},{9,13},{10,... | collective-permute-start | bytes 393224 | tf_op jit(solution)/shard_map/cond/branch_1_fun/ppermute | solution.py:112
  89.6 2.9 %collective-permute-done.13 = bf16[2,2,32,512]{3,2,1,0:T(8,128)(2,1)S(1)} collective-permute-done((bf16[2,2,32,512]{3,2,1,0:T(8,128)(2,1)S(1)}, bf16[2,2,32,512]{3,2,1,0:T(8,128)(2,1)S(1)}, u32[]{:S(2)}, u32[]{:S(2)}) %collective-permute-start.13) | collective-permute-done | bytes 131104 | tf_op jit(solution)/shard_map/cond/branch_1_fun/ppermute | solution.py:112
  94.2 4.9 %collective-permute-done.14 = bf16[4,2,32,512]{3,2,1,0:T(8,128)(2,1)S(1)} collective-permute-done((bf16[4,2,32,512]{3,2,1,0:T(8,128)(2,1)S(1)}, bf16[4,2,32,512]{3,2,1,0:T(8,128)(2,1)S(1)}, u32[]{:S(2)}, u32[]{:S(2)}) %collective-permute-start.14) | collective-permute-done | bytes 262176 | tf_op jit(solution)/shard_map/cond/branch_1_fun/ppermute | solution.py:112
  99.9 2.2 %collective-permute-done.15 = bf16[8,2,32,512]{3,2,1,0:T(8,128)(2,1)} collective-permute-done((bf16[8,2,32,512]{3,2,1,0:T(8,128)(2,1)}, bf16[8,2,32,512]{3,2,1,0:T(8,128)(2,1)}, u32[]{:S(2)}, u32[]{:S(2)}) %collective-permute-start.15) | collective-permute-done | bytes 524320 | tf_op jit(solution)/shard_map/cond/branch_1_fun/ppermute | solution.py:112
  102.1 2.6 %shard_map.47 = bf16[256,512]{1,0:T(8,128)(2,1)S(1)} custom-call(s32[8]{0:T(128)S(1)} %get-tuple-element.75.plan, bf16[8,2,32,512]{3,2,1,0:T(8,128)(2,1)} %get-tuple-element.89.near, bf16[8,2,32,512]{3,2,1,0:T(8,128)(2,1)} %get-tuple-element.90.far, bf16[2,2048,512]{2,1,0:T(8,128)(2,1)} %block1.1), custom_call_target="tpu_custom_call" | custom-call | flops 268435456 | bytes 524288 | tf_op jit(solution)/shard_map/pallas_call | solution.py:531
  105.0 6.2 %shard_map.48.gamma_in = bf16[2,2048,512]{2,1,0:T(8,128)(2,1)} custom-call(s32[8]{0:T(128)S(1)} %get-tuple-element.75.plan, bf16[8,1,32,512]{3,2,1,0:T(8,128)(2,1)} %get-tuple-element.93.near01, bf16[8,1,32,512]{3,2,1,0:T(8,128)(2,1)} %get-tuple-element.94.far01, bf16[8,2,32,512]{3,2,1,0:T(8,128)(2,1)} %get-tuple-element.89.near, ...), custom_call_target="tpu_custom_call" | custom-call | flops 3221225472 | bytes 6291456 | tf_op jit(solution)/shard_map/pallas_call | solution.py:560
  111.2 3.1 %shard_map.49.gamma_in = bf16[2,2048,512]{2,1,0:T(8,128)(2,1)} custom-call(s32[8]{0:T(128)S(1)} %get-tuple-element.75.plan, bf16[8,2,32,512]{3,2,1,0:T(8,128)(2,1)} %get-tuple-element.89.near, bf16[8,2,32,512]{3,2,1,0:T(8,128)(2,1)} %get-tuple-element.90.far, bf16[1024,512]{1,0:T(8,128)(2,1)S(1)} %collective-permute-done.17.a.got_a, ...), custom_call_target="tpu_custom_call", output_to_operand_aliasing={{}: (5, {})} | custom-call | flops 268435456 | bytes 1048576 | tf_op jit(solution)/shard_map/pallas_call | solution.py:575
  (50 shorter events, 22.5 us)
Async XLA Ops:
  0.0 7.7 %copy-start.2 = (f32[4]{0:T(128)S(1)}, f32[4]{0:T(128)}, u32[]{:S(2)}) copy-start(f32[4]{0:T(128)} %param.11) | copy-start | bytes 52
  0.0 7.7 %copy-start.1 = (f32[4,512]{1,0:T(4,128)S(1)}, f32[4,512]{1,0:T(4,128)}, u32[]{:S(2)}) copy-start(f32[4,512]{1,0:T(4,128)} %param.12) | copy-start | bytes 24580
  3.4 42.3 %collective-permute-start.16 = (bf16[1536,512]{1,0:T(8,128)(2,1)}, bf16[1536,512]{1,0:T(8,128)(2,1)}, u32[]{:S(2)}, u32[]{:S(2)}) collective-permute-start(bf16[1536,512]{1,0:T(8,128)(2,1)} %get-tuple-element.76), channel_id=1, source_target_pairs={{0,16},{16,0},{1,17},{17,1},{2,18},{18,2},{3,19},{19,3},{4,20},{20... | collective-permute-start | bytes 4718600 | tf_op jit(solution)/shard_map/ppermute | solution.py:112
  11.1 2.0 %collective-permute-start = (f32[1,256,512]{2,1,0:T(8,128)S(1)}, f32[1,256,512]{2,1,0:T(8,128)S(1)}, u32[]{:S(2)}, u32[]{:S(2)}) collective-permute-start(f32[1,256,512]{2,1,0:T(8,128)S(1)} %get-tuple-element.41), channel_id=1, source_target_pairs={{0,1},{1,0},{2,3},{3,2},{4,5},{5,4},{6,7},{7,6},{8,9},{9,8},{10,11... | collective-permute-start | bytes 1572872 | tf_op jit(solution)/shard_map/cond/branch_1_fun/ppermute | solution.py:112
  13.2 5.6 %collective-permute-start.1 = (bf16[1,128,512]{2,1,0:T(8,128)(2,1)S(1)}, bf16[1,128,512]{2,1,0:T(8,128)(2,1)S(1)}, u32[]{:S(2)}, u32[]{:S(2)}) collective-permute-start(bf16[1,128,512]{2,1,0:T(8,128)(2,1)S(1)} %select_convert_fusion), channel_id=1, source_target_pairs={{0,2},{1,3},{2,0},{3,1},{4,6},{5,7},{6,4},{7,5},{8,10},{9,11},{10,... | collective-permute-start | bytes 393224 | tf_op jit(solution)/shard_map/cond/branch_1_fun/ppermute | solution.py:112
  18.9 4.3 %collective-permute-start.2 = (bf16[1,64,512]{2,1,0:T(8,128)(2,1)S(1)}, bf16[1,64,512]{2,1,0:T(8,128)(2,1)S(1)}, u32[]{:S(2)}, u32[]{:S(2)}) collective-permute-start(bf16[1,64,512]{2,1,0:T(8,128)(2,1)S(1)} %select_convert_fusion.1), channel_id=1, source_target_pairs={{0,4},{1,5},{2,6},{3,7},{4,0},{5,1},{6,2},{7,3},{8,12},{9,13},{10,... | collective-permute-start | bytes 196616 | tf_op jit(solution)/shard_map/cond/branch_1_fun/ppermute | solution.py:112
  23.3 5.4 %collective-permute-start.3 = (bf16[1,32,512]{2,1,0:T(8,128)(2,1)S(1)}, bf16[1,32,512]{2,1,0:T(8,128)(2,1)S(1)}, u32[]{:S(2)}, u32[]{:S(2)}) collective-permute-start(bf16[1,32,512]{2,1,0:T(8,128)(2,1)S(1)} %select_convert_fusion.2), channel_id=1, source_target_pairs={{0,8},{1,9},{2,10},{3,11},{4,12},{5,13},{6,14},{7,15},{8,0},{9,1},... | collective-permute-start | bytes 98312 | tf_op jit(solution)/shard_map/cond/branch_1_fun/ppermute | solution.py:112
  28.7 4.9 %collective-permute-start.4 = (bf16[1,1,32,512]{3,2,1,0:T(8,128)(2,1)S(1)}, bf16[1,1,32,512]{3,2,1,0:T(8,128)(2,1)S(1)}, u32[]{:S(2)}, u32[]{:S(2)}) collective-permute-start(bf16[1,1,32,512]{3,2,1,0:T(8,128)(2,1)S(1)} %fusion), channel_id=1, source_target_pairs={{0,8},{1,9},{2,10},{3,11},{4,12},{5,13},{6,14},{7,15},{8,0},{9,1},... | collective-permute-start | bytes 98312 | tf_op jit(solution)/shard_map/cond/branch_1_fun/ppermute | solution.py:112
  33.6 4.3 %collective-permute-start.5 = (bf16[2,1,32,512]{3,2,1,0:T(8,128)(2,1)S(1)}, bf16[2,1,32,512]{3,2,1,0:T(8,128)(2,1)S(1)}, u32[]{:S(2)}, u32[]{:S(2)}) collective-permute-start(bf16[2,1,32,512]{3,2,1,0:T(8,128)(2,1)S(1)} %pad_maximum_fusion.2), channel_id=1, source_target_pairs={{0,4},{1,5},{2,6},{3,7},{4,0},{5,1},{6,2},{7,3},{8,12},{9,13},{10,... | collective-permute-start | bytes 196616 | tf_op jit(solution)/shard_map/cond/branch_1_fun/ppermute | solution.py:112
  38.0 5.0 %collective-permute-start.6 = (bf16[4,1,32,512]{3,2,1,0:T(8,128)(2,1)S(1)}, bf16[4,1,32,512]{3,2,1,0:T(8,128)(2,1)S(1)}, u32[]{:S(2)}, u32[]{:S(2)}) collective-permute-start(bf16[4,1,32,512]{3,2,1,0:T(8,128)(2,1)S(1)} %pad_maximum_fusion.1), channel_id=1, source_target_pairs={{0,2},{1,3},{2,0},{3,1},{4,6},{5,7},{6,4},{7,5},{8,10},{9,11},{10,... | collective-permute-start | bytes 393224 | tf_op jit(solution)/shard_map/cond/branch_1_fun/ppermute | solution.py:112
  43.8 1.9 %collective-permute-start.7 = (bf16[8,1,32,512]{3,2,1,0:T(8,128)(2,1)}, bf16[8,1,32,512]{3,2,1,0:T(8,128)(2,1)}, u32[]{:S(2)}, u32[]{:S(2)}) collective-permute-start(bf16[8,1,32,512]{3,2,1,0:T(8,128)(2,1)} %pad_maximum_fusion), channel_id=1, source_target_pairs={{0,1},{1,0},{2,3},{3,2},{4,5},{5,4},{6,7},{7,6},{8,9},{9,8},{10,11... | collective-permute-start | bytes 786440 | tf_op jit(solution)/shard_map/cond/branch_1_fun/ppermute | solution.py:112
  45.6 29.2 %collective-permute-start.17 = (bf16[1024,512]{1,0:T(8,128)(2,1)}, bf16[1024,512]{1,0:T(8,128)(2,1)S(1)}, u32[]{:S(2)}, u32[]{:S(2)}) collective-permute-start(bf16[1024,512]{1,0:T(8,128)(2,1)} %get-tuple-element.83), channel_id=1, source_target_pairs={{0,16},{16,0},{1,17},{17,1},{2,18},{18,2},{3,19},{19,3},{4,20},{20... | collective-permute-start | bytes 3145736 | tf_op jit(solution)/shard_map/ppermute | solution.py:112
  51.5 2.9 %collective-permute-start.8 = (f32[2,256,512]{2,1,0:T(8,128)S(1)}, f32[2,256,512]{2,1,0:T(8,128)}, u32[]{:S(2)}, u32[]{:S(2)}) collective-permute-start(f32[2,256,512]{2,1,0:T(8,128)S(1)} %get-tuple-element.53), channel_id=1, source_target_pairs={{0,1},{1,0},{2,3},{3,2},{4,5},{5,4},{6,7},{7,6},{8,9},{9,8},{10,11... | collective-permute-start | bytes 3145736 | tf_op jit(solution)/shard_map/cond/branch_1_fun/ppermute | solution.py:112
  55.8 8.4 %collective-permute-start.9 = (bf16[2,128,512]{2,1,0:T(8,128)(2,1)S(1)}, bf16[2,128,512]{2,1,0:T(8,128)(2,1)S(1)}, u32[]{:S(2)}, u32[]{:S(2)}) collective-permute-start(bf16[2,128,512]{2,1,0:T(8,128)(2,1)S(1)} %select_convert_fusion.3), channel_id=1, source_target_pairs={{0,2},{1,3},{2,0},{3,1},{4,6},{5,7},{6,4},{7,5},{8,10},{9,11},{10,... | collective-permute-start | bytes 786440 | tf_op jit(solution)/shard_map/cond/branch_1_fun/ppermute | solution.py:112
  64.4 5.0 %collective-permute-start.10 = (bf16[2,64,512]{2,1,0:T(8,128)(2,1)S(1)}, bf16[2,64,512]{2,1,0:T(8,128)(2,1)S(1)}, u32[]{:S(2)}, u32[]{:S(2)}) collective-permute-start(bf16[2,64,512]{2,1,0:T(8,128)(2,1)S(1)} %select_convert_fusion.4), channel_id=1, source_target_pairs={{0,4},{1,5},{2,6},{3,7},{4,0},{5,1},{6,2},{7,3},{8,12},{9,13},{10,... | collective-permute-start | bytes 393224 | tf_op jit(solution)/shard_map/cond/branch_1_fun/ppermute | solution.py:112
  69.5 5.2 %collective-permute-start.11 = (bf16[2,32,512]{2,1,0:T(8,128)(2,1)S(1)}, bf16[2,32,512]{2,1,0:T(8,128)(2,1)S(1)}, u32[]{:S(2)}, u32[]{:S(2)}) collective-permute-start(bf16[2,32,512]{2,1,0:T(8,128)(2,1)S(1)} %select_convert_fusion.5), channel_id=1, source_target_pairs={{0,8},{1,9},{2,10},{3,11},{4,12},{5,13},{6,14},{7,15},{8,0},{9,1},... | collective-permute-start | bytes 196616 | tf_op jit(solution)/shard_map/cond/branch_1_fun/ppermute | solution.py:112
  74.8 5.1 %collective-permute-start.18 = (f32[2,32,512]{2,1,0:T(8,128)S(1)}, f32[2,32,512]{2,1,0:T(8,128)S(1)}, u32[]{:S(2)}, u32[]{:S(2)}) collective-permute-start(f32[2,32,512]{2,1,0:T(8,128)S(1)} %get-tuple-element.85), channel_id=1, source_target_pairs={{0,16},{16,0},{1,17},{17,1},{2,18},{18,2},{3,19},{19,3},{4,20},{20... | collective-permute-start | bytes 393224 | tf_op jit(solution)/shard_map/ppermute | solution.py:112
  79.9 31.3 %collective-permute-start.20 = (bf16[1024,512]{1,0:T(8,128)(2,1)}, bf16[1024,512]{1,0:T(8,128)(2,1)S(1)}, u32[]{:S(2)}, u32[]{:S(2)}) collective-permute-start(bf16[1024,512]{1,0:T(8,128)(2,1)} %get-tuple-element.92), channel_id=1, source_target_pairs={{0,16},{16,0},{1,17},{17,1},{2,18},{18,2},{3,19},{19,3},{4,20},{20... | collective-permute-start | bytes 3145736 | tf_op jit(solution)/shard_map/ppermute | solution.py:112
  82.3 5.2 %collective-permute-start.12 = (bf16[1,2,32,512]{3,2,1,0:T(8,128)(2,1)S(1)}, bf16[1,2,32,512]{3,2,1,0:T(8,128)(2,1)S(1)}, u32[]{:S(2)}, u32[]{:S(2)}) collective-permute-start(bf16[1,2,32,512]{3,2,1,0:T(8,128)(2,1)S(1)} %bitcast.5), channel_id=1, source_target_pairs={{0,8},{1,9},{2,10},{3,11},{4,12},{5,13},{6,14},{7,15},{8,0},{9,1},... | collective-permute-start | bytes 196616 | tf_op jit(solution)/shard_map/cond/branch_1_fun/ppermute | solution.py:112
  87.4 5.1 %collective-permute-start.13 = (bf16[2,2,32,512]{3,2,1,0:T(8,128)(2,1)S(1)}, bf16[2,2,32,512]{3,2,1,0:T(8,128)(2,1)S(1)}, u32[]{:S(2)}, u32[]{:S(2)}) collective-permute-start(bf16[2,2,32,512]{3,2,1,0:T(8,128)(2,1)S(1)} %pad_maximum_fusion.5), channel_id=1, source_target_pairs={{0,4},{1,5},{2,6},{3,7},{4,0},{5,1},{6,2},{7,3},{8,12},{9,13},{10,... | collective-permute-start | bytes 393224 | tf_op jit(solution)/shard_map/cond/branch_1_fun/ppermute | solution.py:112
  92.6 6.4 %collective-permute-start.14 = (bf16[4,2,32,512]{3,2,1,0:T(8,128)(2,1)S(1)}, bf16[4,2,32,512]{3,2,1,0:T(8,128)(2,1)S(1)}, u32[]{:S(2)}, u32[]{:S(2)}) collective-permute-start(bf16[4,2,32,512]{3,2,1,0:T(8,128)(2,1)S(1)} %pad_maximum_fusion.4), channel_id=1, source_target_pairs={{0,2},{1,3},{2,0},{3,1},{4,6},{5,7},{6,4},{7,5},{8,10},{9,11},{10,... | collective-permute-start | bytes 786440 | tf_op jit(solution)/shard_map/cond/branch_1_fun/ppermute | solution.py:112
  99.9 2.3 %collective-permute-start.15 = (bf16[8,2,32,512]{3,2,1,0:T(8,128)(2,1)}, bf16[8,2,32,512]{3,2,1,0:T(8,128)(2,1)}, u32[]{:S(2)}, u32[]{:S(2)}) collective-permute-start(bf16[8,2,32,512]{3,2,1,0:T(8,128)(2,1)} %pad_maximum_fusion.3), channel_id=1, source_target_pairs={{0,1},{1,0},{2,3},{3,2},{4,5},{5,4},{6,7},{7,6},{8,9},{9,8},{10,11... | collective-permute-start | bytes 1572872 | tf_op jit(solution)/shard_map/cond/branch_1_fun/ppermute | solution.py:112
  102.1 2.9 %copy-start = (bf16[2,2048,512]{2,1,0:T(8,128)(2,1)S(1)}, bf16[2,2048,512]{2,1,0:T(8,128)(2,1)}, u32[]{:S(2)}) copy-start(bf16[2,2048,512]{2,1,0:T(8,128)(2,1)} %block1.1) | copy-start | bytes 12582916
  104.8 9.6 %collective-permute-start.19 = (bf16[256,512]{1,0:T(8,128)(2,1)S(1)}, bf16[256,512]{1,0:T(8,128)(2,1)S(1)}, u32[]{:S(2)}, u32[]{:S(2)}) collective-permute-start(bf16[256,512]{1,0:T(8,128)(2,1)S(1)} %shard_map.47), channel_id=1, source_target_pairs={{0,16},{16,0},{1,17},{17,1},{2,18},{18,2},{3,19},{19,3},{4,20},{20... | collective-permute-start | bytes 786440 | tf_op jit(solution)/shard_map/ppermute | solution.py:112
